TPU v7x, 32 devices: a whole 2x2x4 slice. The times are simulated.
32 devices in a mesh: group: 2 (over x), row: 8 (over z, y), col: 2 (over core).
Axes of the slice: x: 2, y: 2, z: 4, core: 2. Of those that a mesh axis runs over, the one named last changes fastest.
Arguments:
- pair: float32 [64, 32, 128], P(('group', 'row'), 'col'), parts along dimension 0, may hold values from -6 to 6
- token_mask: int32 [64], P('group'), parts along dimension 0, may hold values from 0 to 1, as said below
- chains: int32 [64], P('group'), parts along dimension 0, may hold values from 0 to 3, never falling along the last dimension, each value on 1 to 16 neighbouring positions
- chain_bias: float32 [128], replicated, may hold values from -4 to 4
- proj_weight: bfloat16 [2, 128, 512], replicated, may hold values from -0.5 to 0.5
- gate_weight: bfloat16 [2, 128, 128], replicated, may hold values from -0.5 to 0.5
- out_weight: bfloat16 [2, 128, 128], replicated, may hold values from -0.5 to 0.5
Outputs:
- updated: float32 [64, 32, 128], P(('group', 'row'), 'col'), parts along dimension 0
There are 2 independent parts, one for each index of `group`. A program takes and returns all parts, laid end to end along the dimension named above; an argument that names none is the same for every part. Nothing has to cross between parts.
Inputs may be any that keep to these rules, and one draw needn't show every extreme that they name: token_mask is 1 on a leading run of at least 16 tokens and 0 after it; the last token is always padding. `chains`: chain numbers never fall along the crop; a chain holds at most 16 tokens.
All inputs are finite; a program needn't handle non-finite values.
Results may differ from a plain program's by a relative error of at most 0.003.
Values may be sent and summed in bfloat16 or wider, within the bound.
No kernel may reach another device: no remote copies, remote signals or barrier semaphores. Data moves between devices by JAX's collectives and lax.ppermute only.
A program may use at most 128 MiB of HBM per device.

v0:
```python
import jax
import jax.numpy as jnp
from jax import lax
from jax.sharding import PartitionSpec as P


def layer_norm(values):
    mean = jnp.mean(values, -1, keepdims=True)
    centred = values - mean
    var = jnp.mean(centred * centred, -1, keepdims=True)
    return centred * lax.rsqrt(var + 1e-05)


def flat_dot(values, weight):
    shape = values.shape
    result = jnp.dot(values.reshape(-1, shape[-1]), weight, preferred_element_type=jnp.float32)
    return result.reshape(shape[:-1] + (weight.shape[1],))


def project(state, pmask, p_weight):
    normed = layer_norm(state).astype(jnp.bfloat16)
    proj = flat_dot(normed, p_weight)
    hidden = p_weight.shape[1] // 4
    gate_a = proj[..., :hidden]
    value_a = proj[..., hidden : 2 * hidden]
    gate_b = proj[..., 2 * hidden : 3 * hidden]
    value_b = proj[..., 3 * hidden :]
    left = (jax.nn.sigmoid(gate_a) * value_a * pmask[..., None]).astype(jnp.bfloat16)
    right = (jax.nn.sigmoid(gate_b) * value_b * pmask[..., None]).astype(jnp.bfloat16)
    return (normed, left, right)


def finish(state, normed, tri, g_weight, o_weight):
    tnorm = layer_norm(tri).astype(jnp.bfloat16)
    gate = jax.nn.sigmoid(flat_dot(normed, g_weight))
    return state + gate * flat_dot(tnorm, o_weight)


def shards(pair, token_mask, chains, chain_bias, proj_weight, gate_weight, out_weight):
    rows, cols, width = pair.shape
    row_start = lax.axis_index("row") * rows
    col_start = lax.axis_index("col") * cols
    chain_rows = lax.dynamic_slice_in_dim(chains, row_start, rows)
    chain_cols = lax.dynamic_slice_in_dim(chains, col_start, cols)
    mask_rows = lax.dynamic_slice_in_dim(token_mask, row_start, rows).astype(jnp.float32)
    mask_cols = lax.dynamic_slice_in_dim(token_mask, col_start, cols).astype(jnp.float32)
    same = (chain_rows[:, None] == chain_cols[None, :]).astype(jnp.float32)
    state = pair + same[..., None] * chain_bias
    pmask = mask_rows[:, None] * mask_cols[None, :]
    normed, left, right = project(state, pmask, proj_weight[0])
    left_rows, right_rows = (
        lax.all_gather(left, "col", axis=1, tiled=True),
        lax.all_gather(right, "col", axis=1, tiled=True),
    )
    every = jnp.einsum(
        "ikh,jkh->ijh",
        left_rows,
        lax.all_gather(right_rows, "row", axis=0, tiled=True),
        preferred_element_type=jnp.float32,
    )
    tri = lax.dynamic_slice_in_dim(every, col_start, cols, 1)
    state = finish(state, normed, tri, gate_weight[0], out_weight[0])
    normed, left, right = project(state, pmask, proj_weight[1])
    left_rows = lax.all_gather(left, "col", axis=1, tiled=True)
    left_cols = lax.all_to_all(left_rows, "row", split_axis=1, concat_axis=0, tiled=True)
    tri = jnp.einsum(
        "kih,kjh->ijh",
        left_cols,
        lax.all_gather(right, "row", axis=0, tiled=True),
        preferred_element_type=jnp.float32,
    )
    return finish(state, normed, tri, gate_weight[1], out_weight[1])


def solution(mesh):
    placed = (P(("group", "row"), "col", None), P("group"), P("group"), P(), P(), P(), P())
    return jax.shard_map(
        shards,
        mesh=mesh,
        in_specs=placed,
        out_specs=P(("group", "row"), "col", None),
        check_vma=False,
    )
```

profile of v0, /device:TPU:0, one launch (start us, length us, event | category | flops | bytes accessed | tf_op | source)
XLA Modules:
  0.0 88.2 jit_solution(13237935402769814355)
XLA Ops:
  0.0 0.7 dynamic_slice.16
  0.7 0.7 dynamic_slice.15
  1.5 0.7 dynamic-slice_convert_fusion
  2.2 0.7 dynamic-slice_convert_fusion.1
  3.0 0.6 copy-done.3
  3.9 1.1 %fusion.10 = f32[4,16,512]{2,1,0:T(8,128)S(1)} fusion(bf16[2,128,512]{2,1,0:T(8,128)(2,1)} %param.11, f32[4,16,128]{2,1,0:T(8,128)S(1)} %copy-done, f32[4,16]{1,0:T(4,128)S(1)} %add_rsqrt_fusion.3, f32[4,16]{1,0:T(4,128)S(1)} %broadcast_multiply_fusion.4, f32[128]{0:T(128)S(1)} %copy-done.3, f32[4,16]{1,0:T(4,128)S(1)} %compare_convert_fusion), kind=kOutput, calls=%fused_computation.14 | convolution fusion | flops 8429568 | bytes 296192 | tf_op jit(solution)/shard_map/dot_general | solution.py:16
  5.2 1.9 %all_gather.15 = bf16[4,32,128]{2,1,0:T(8,128)(2,1)S(1)} all-gather(bf16[4,16,128]{2,1,0:T(8,128)(2,1)S(1)} %get-tuple-element.8), channel_id=1, replica_groups=mesh['group'=2,'row'=8,'col'=2] {'col'}, dimensions={1}, use_global_device_ids=true | all-gather | bytes 49152 | tf_op jit(solution)/shard_map/all_gather | solution.py:53
  7.2 32.4 %all_gather.16 = bf16[32,32,128]{2,1,0:T(8,128)(2,1)S(1)} all-gather(bf16[4,32,128]{2,1,0:T(8,128)(2,1)S(1)} %all_gather.15), channel_id=1, replica_groups=mesh['group'=2,'row'=8,'col'=2] {'row'}, dimensions={0}, use_global_device_ids=true | all-gather | bytes 294912 | tf_op jit(solution)/shard_map/all_gather | solution.py:58
  39.6 1.4 %copy.29 = bf16[32,32,128]{1,0,2:T(8,128)(2,1)S(1)} copy(bf16[32,32,128]{2,1,0:T(8,128)(2,1)S(1)} %all_gather.16) | data formatting | bytes 524288 | tf_op jit(solution)/shard_map/all_gather | solution.py:58
  41.0 1.8 %all_gather.17 = bf16[4,32,128]{2,1,0:T(8,128)(2,1)S(1)} all-gather(bf16[4,16,128]{2,1,0:T(8,128)(2,1)S(1)} %get-tuple-element.7), channel_id=1, replica_groups=mesh['group'=2,'row'=8,'col'=2] {'col'}, dimensions={1}, use_global_device_ids=true | all-gather | bytes 49152 | tf_op jit(solution)/shard_map/all_gather | solution.py:52
  43.0 0.6 fusion.48
  43.6 0.2 constant_dynamic-slice_fusion
  44.2 0.5 copy-done.4
  44.7 0.2 fusion.7
  44.9 0.3 fusion.47
  45.4 0.2 fusion.8
  45.7 1.8 %all_gather.19 = bf16[4,32,128]{2,1,0:T(8,128)(2,1)S(1)} all-gather(bf16[4,16,128]{2,1,0:T(8,128)(2,1)S(1)} %get-tuple-element.5), channel_id=1, replica_groups=mesh['group'=2,'row'=8,'col'=2] {'col'}, dimensions={1}, use_global_device_ids=true | all-gather | bytes 49152 | tf_op jit(solution)/shard_map/all_gather | solution.py:64
  47.5 0.6 copy.32
  48.2 5.5 %all-to-all-start = ((bf16[4,32,128]{2,0,1:T(4,128)(2,1)}), bf16[4,32,128]{2,0,1:T(4,128)(2,1)S(1)}, u32[]{:S(2)}, u32[]{:S(2)}) async-start(bf16[4,32,128]{2,0,1:T(4,128)(2,1)} %copy.32), calls=%async_computation | async-start | bytes 65536 | tf_op jit(solution)/shard_map/all_to_all | solution.py:65
  53.7 0.2 fusion.3
  53.9 31.2 %all_gather.18 = bf16[32,16,128]{2,1,0:T(8,128)(2,1)S(1)} all-gather(bf16[4,16,128]{2,1,0:T(8,128)(2,1)S(1)} %get-tuple-element.6), channel_id=1, replica_groups=mesh['group'=2,'row'=8,'col'=2] {'row'}, dimensions={0}, use_global_device_ids=true | all-gather | bytes 147456 | tf_op jit(solution)/shard_map/all_gather | solution.py:69
  85.0 1.4 %copy.34 = bf16[32,16,128]{1,0,2:T(8,128)(2,1)S(1)} copy(bf16[32,16,128]{2,1,0:T(8,128)(2,1)S(1)} %all_gather.18) | data formatting | bytes 262144 | tf_op jit(solution)/shard_map/all_gather | solution.py:69
  86.6 0.4 fusion.49
  87.4 0.8 fusion
  (33 shorter events, 1.9 us)
Async XLA Ops:
  0.0 3.0 %copy-start = (f32[4,16,128]{2,1,0:T(8,128)S(1)}, f32[4,16,128]{2,1,0:T(8,128)}, u32[]{:S(2)}) copy-start(f32[4,16,128]{2,1,0:T(8,128)} %param.7) | copy-start | bytes 98308
  2.9 0.7 copy-start.3
  43.8 0.8 copy-start.4
  43.9 1.0 %copy-start.2 = (bf16[2,128,128]{2,1,0:T(8,128)(2,1)S(1)}, bf16[2,128,128]{2,1,0:T(8,128)(2,1)}, u32[]{:S(2)}) copy-start(bf16[2,128,128]{2,1,0:T(8,128)(2,1)} %param.13) | copy-start | bytes 196612
  44.0 1.4 %copy-start.1 = (bf16[2,128,512]{2,1,0:T(8,128)(2,1)S(1)}, bf16[2,128,512]{2,1,0:T(8,128)(2,1)}, u32[]{:S(2)}) copy-start(bf16[2,128,512]{2,1,0:T(8,128)(2,1)} %param.11) | copy-start | bytes 786436
  48.2 38.3 %all-to-all-start = ((bf16[4,32,128]{2,0,1:T(4,128)(2,1)}), bf16[4,32,128]{2,0,1:T(4,128)(2,1)S(1)}, u32[]{:S(2)}, u32[]{:S(2)}) async-start(bf16[4,32,128]{2,0,1:T(4,128)(2,1)} %copy.32), calls=%async_computation | async-start | bytes 65536 | tf_op jit(solution)/shard_map/all_to_all | solution.py:65
where the time goes:
time: 88.6 us; the launch traced here: 88.2 us
  blocking collectives  69.2 us (78%)
  local copies, waits for them, and re-layouts  6.71 us (8%)
  starting transfers between devices  5.5 us (6%)
  matrix products  3.87 us (4%)
  other arithmetic  2.83 us (3%)
    all_gather x1, blocking collectives, shards(): lax.all_gather(right_rows, 'row', axis=0, tiled=True)  32.4 us
    all_gather x1, blocking collectives, shards(): lax.all_gather(right, 'row', axis=0, tiled=True)  31.2 us
    all_to_all x1, starting transfers between devices, shards(): lax.all_to_all(left_rows, 'row', split_axis=1, concat_axis=0, tiled=True)  5.5 us
    dot_general x6, matrix products, flat_dot(): jnp.dot(values.reshape(-1, shape[-1]), weight, preferred_element_type=jnp...  2.86 us
    all_gather x1, blocking collectives, shards(): lax.all_gather(right, 'col', axis=1, tiled=True)  1.95 us
    all_gather x1, blocking collectives, shards(): lax.all_gather(left, 'col', axis=1, tiled=True)  1.83 us
    all_gather x1, blocking collectives, shards(): left_rows = lax.all_gather(left, 'col', axis=1, tiled=True)  1.83 us
  transfers between devices with their start and end apart: 1, of which 0 were waited for; matrix products, arithmetic and copies ran while one was open for 2% of the time, Pallas kernels for 0%

commit v1 on v0

--- a/solution.py
+++ b/solution.py
@@ -17,6 +17,18 @@
     return result.reshape(shape[:-1] + (weight.shape[1],))
 
 
+def edge(normed, mask, weight):
+    proj = flat_dot(normed, weight)
+    hidden = weight.shape[1] // 2
+    return (jax.nn.sigmoid(proj[..., :hidden]) * proj[..., hidden:] * mask[..., None]).astype(jnp.bfloat16)
+
+
+def finish(state, normed, tri, g_weight, o_weight):
+    tnorm = layer_norm(tri).astype(jnp.bfloat16)
+    gate = jax.nn.sigmoid(flat_dot(normed, g_weight))
+    return state + gate * flat_dot(tnorm, o_weight)
+
+
 def project(state, pmask, p_weight):
     normed = layer_norm(state).astype(jnp.bfloat16)
     proj = flat_dot(normed, p_weight)
@@ -30,13 +42,7 @@
     return (normed, left, right)
 
 
-def finish(state, normed, tri, g_weight, o_weight):
-    tnorm = layer_norm(tri).astype(jnp.bfloat16)
-    gate = jax.nn.sigmoid(flat_dot(normed, g_weight))
-    return state + gate * flat_dot(tnorm, o_weight)
-
-
-def shards(pair, token_mask, chains, chain_bias, proj_weight, gate_weight, out_weight):
+def sharded_plan(pair, token_mask, chains, chain_bias, proj_weight, gate_weight, out_weight):
     rows, cols, width = pair.shape
     row_start = lax.axis_index("row") * rows
     col_start = lax.axis_index("col") * cols
@@ -72,6 +78,54 @@
     return finish(state, normed, tri, gate_weight[1], out_weight[1])
 
 
+def gather_rows(block):
+    n = lax.axis_size("row")
+    me = lax.axis_index("row")
+    parts = [block]
+    for s in range(1, n):
+        parts.append(lax.ppermute(block, "row", [(i, (i + s) % n) for i in range(n)]))
+    stacked = jnp.stack(parts)
+    order = lax.rem(me - jnp.arange(n) + n, n)
+    return jnp.take(stacked, order, axis=0).reshape((-1,) + block.shape[1:])
+
+
+def whole_crop_plan(pair, token_mask, chains, chain_bias, proj_weight, gate_weight, out_weight):
+    rows, cols, width = pair.shape
+    row_start = lax.axis_index("row") * rows
+    col = lax.axis_index("col")
+    col_start = col * cols
+    mine = gather_rows(pair.astype(jnp.bfloat16))
+    other = lax.ppermute(mine, "col", [(0, 1), (1, 0)])
+    first = jnp.where(col == 0, mine, other)
+    second = jnp.where(col == 0, other, mine)
+    whole = jnp.concatenate([first, second], axis=1).astype(jnp.float32)
+    whole = lax.dynamic_update_slice(whole, pair, (row_start, col_start, 0))
+    same = (chains[:, None] == chains[None, :]).astype(jnp.float32)
+    state = whole + same[..., None] * chain_bias
+    mask = token_mask.astype(jnp.float32)
+    pmask = mask[:, None] * mask[None, :]
+    hidden2 = proj_weight.shape[2] // 2
+    normed = layer_norm(state).astype(jnp.bfloat16)
+    left = edge(normed, pmask, proj_weight[0, :, :hidden2])
+    right = edge(normed, pmask, proj_weight[0, :, hidden2:])
+    tri = jnp.einsum("ikh,jkh->ijh", left, right, preferred_element_type=jnp.float32)
+    state = finish(state, normed, tri, gate_weight[0], out_weight[0])
+    mine_rows = lax.dynamic_slice_in_dim(state, row_start, rows, 1)
+    mine_cols = lax.dynamic_slice_in_dim(state, col_start, cols, 1)
+    left = edge(layer_norm(mine_rows).astype(jnp.bfloat16), lax.dynamic_slice_in_dim(pmask, row_start, rows, 1), proj_weight[1, :, :hidden2])
+    normed = layer_norm(mine_cols).astype(jnp.bfloat16)
+    right = edge(normed, lax.dynamic_slice_in_dim(pmask, col_start, cols, 1), proj_weight[1, :, hidden2:])
+    tri = jnp.einsum("kih,kjh->ijh", left, right, preferred_element_type=jnp.float32)
+    own = lax.dynamic_slice_in_dim(mine_cols, row_start, rows, 0)
+    return finish(own, lax.dynamic_slice_in_dim(normed, row_start, rows, 0), tri, gate_weight[1], out_weight[1])
+
+
+def shards(pair, token_mask, *rest):
+    tokens = token_mask.shape[0]
+    plan = whole_crop_plan if tokens * tokens <= 4096 else sharded_plan
+    return plan(pair, token_mask, *rest)
+
+
 def solution(mesh):
     placed = (P(("group", "row"), "col", None), P("group"), P("group"), P(), P(), P(), P())
     return jax.shard_map(

time: 88.6 us -> 39.7 us (0.45)
  blocking collectives: 69.2 us -> 0 us
  starting transfers between devices: 5.5 us -> 13.8 us
  other arithmetic: 2.83 us -> 7.47 us
  waiting for transfers between devices: 0.01 us -> 3.37 us
  local copies, waits for them, and re-layouts: 6.71 us -> 9.39 us
  matrix products: 3.87 us -> 4.97 us
    all_gather x5 -> x0, blocking collectives: 69.2 us -> none  [the longest x1 32.4 us: shards(): lax.all_gather(right_rows, 'row', axis=0, tiled=True)]
    ppermute x0 -> x8, starting transfers between devices: none -> 13.8 us  [the longest x7 13.8 us: gather_rows(): lax.ppermute(block, 'row', [(i, (i + s) % n) for i in range(n)])]
    convert_element_type x0 -> x5, local copies, waits for them, and re-layouts: none -> 7.93 us  [the longest x4 5.28 us: edge(): (jax.nn.sigmoid(proj[..., :hidden]) * proj[..., hidden:] * mask[..., None...]
    all_to_all x1 -> x0, starting transfers between devices: 5.5 us -> none  [shards(): lax.all_to_all(left_rows, 'row', split_axis=1, concat_axis=0, tiled=True)]
    all_gather x4 -> x0, local copies, waits for them, and re-layouts: 3.65 us -> none  [the longest x1 1.45 us: shards(): lax.all_gather(right_rows, 'row', axis=0, tiled=True)]
    ppermute x0 -> x8, waiting for transfers between devices: none -> 3.37 us  [the longest x7 2.26 us: gather_rows(): lax.ppermute(block, 'row', [(i, (i + s) % n) for i in range(n)])]
    convert_element_type x5 -> x10, other arithmetic: 1.71 us -> 4.11 us  [the longest x1 1.26 us: finish(): tnorm = layer_norm(tri).astype(jnp.bfloat16)]
    dot_general x2, matrix products: 1.02 us -> 2.57 us  [the longest x1 2.2 us: whole_crop_plan(): jnp.einsum('ikh,jkh->ijh', left, right, preferred_element_type=jnp.float32)]
  transfers between devices with their start and end apart: 1 -> 8, of which waited for: 0 -> 3; matrix products, arithmetic and copies ran while one was open for 2% -> 5% of each run, Pallas kernels for 0% -> 0%
where the time goes in v1:
time: 39.7 us; the launch traced here: 39.4 us
  starting transfers between devices  13.8 us (35%)
  local copies, waits for them, and re-layouts  9.39 us (24%)
  other arithmetic  7.47 us (19%)
  matrix products  4.97 us (13%)
  waiting for transfers between devices  3.37 us (8%)
    ppermute x7, starting transfers between devices, gather_rows(): lax.ppermute(block, 'row', [(i, (i + s) % n) for i in range(n)])  13.8 us
    convert_element_type x4, local copies, waits for them, and re-layouts, edge(): (jax.nn.sigmoid(proj[..., :hidden]) * proj[..., hidden:] * mask[..., None...  5.28 us
    convert_element_type x1, local copies, waits for them, and re-layouts, finish(): tnorm = layer_norm(tri).astype(jnp.bfloat16)  2.65 us
    dot_general x8, matrix products, flat_dot(): jnp.dot(values.reshape(-1, shape[-1]), weight, preferred_element_type=jnp...  2.4 us
    ppermute x7, waiting for transfers between devices, gather_rows(): lax.ppermute(block, 'row', [(i, (i + s) % n) for i in range(n)])  2.26 us
    dot_general x1, matrix products, whole_crop_plan(): jnp.einsum('ikh,jkh->ijh', left, right, preferred_element_type=jnp.float32)  2.2 us
    reduce_sum x5, other arithmetic, layer_norm(): var = jnp.mean(centred * centred, -1, keepdims=True)  1.4 us
    convert_element_type x1, other arithmetic, finish(): tnorm = layer_norm(tri).astype(jnp.bfloat16)  1.26 us
  transfers between devices with their start and end apart: 8, of which 3 were waited for; matrix products, arithmetic and copies ran while one was open for 5% of the time, Pallas kernels for 0%

profile of v1, /device:TPU:0, one launch (start us, length us, event | category | flops | bytes accessed | tf_op | source)
XLA Modules:
  0.0 39.4 jit_solution(762611959658629012)
XLA Ops:
  0.0 0.8 %constant_dynamic-update-slice_fusion.7 = (bf16[8,4,16,128]{3,2,1,0:T(8,128)(2,1)S(1)}, bf16[4,16,128]{2,1,0:T(8,128)(2,1)S(1)}) fusion(f32[4,16,128]{2,1,0:T(8,128)} %param.7), kind=kLoop, calls=%fused_computation.91 | loop fusion | flops 8191 | bytes 65536
  0.8 3.0 %collective-permute-start = (bf16[4,16,128]{2,1,0:T(8,128)(2,1)S(1)}, bf16[4,16,128]{2,1,0:T(8,128)(2,1)S(1)}, u32[]{:S(2)}, u32[]{:S(2)}) collective-permute-start(bf16[4,16,128]{2,1,0:T(8,128)(2,1)S(1)} %get-tuple-element.6), channel_id=1, source_target_pairs={{0,2},{2,4},{4,6},{6,8},{8,10},{10,12},{12,14},{14,0},{1,3},{3,5},... | collective-permute-start | bytes 49160 | tf_op jit(solution)/shard_map/ppermute | solution.py:86
  3.8 1.6 %collective-permute-start.1 = (bf16[4,16,128]{2,1,0:T(8,128)(2,1)S(1)}, bf16[4,16,128]{2,1,0:T(8,128)(2,1)S(1)}, u32[]{:S(2)}, u32[]{:S(2)}) collective-permute-start(bf16[4,16,128]{2,1,0:T(8,128)(2,1)S(1)} %get-tuple-element.6), channel_id=1, source_target_pairs={{0,4},{2,6},{4,8},{6,10},{8,12},{10,14},{12,0},{14,2},{1,5},{3,7},... | collective-permute-start | bytes 49160 | tf_op jit(solution)/shard_map/ppermute | solution.py:86
  5.4 2.5 %collective-permute-start.2 = (bf16[4,16,128]{2,1,0:T(8,128)(2,1)S(1)}, bf16[4,16,128]{2,1,0:T(8,128)(2,1)S(1)}, u32[]{:S(2)}, u32[]{:S(2)}) collective-permute-start(bf16[4,16,128]{2,1,0:T(8,128)(2,1)S(1)} %get-tuple-element.6), channel_id=1, source_target_pairs={{0,6},{2,8},{4,10},{6,12},{8,14},{10,0},{12,2},{14,4},{1,7},{3,9},... | collective-permute-start | bytes 49160 | tf_op jit(solution)/shard_map/ppermute | solution.py:86
  7.9 1.2 %collective-permute-start.3 = (bf16[4,16,128]{2,1,0:T(8,128)(2,1)S(1)}, bf16[4,16,128]{2,1,0:T(8,128)(2,1)S(1)}, u32[]{:S(2)}, u32[]{:S(2)}) collective-permute-start(bf16[4,16,128]{2,1,0:T(8,128)(2,1)S(1)} %get-tuple-element.6), channel_id=1, source_target_pairs={{0,8},{2,10},{4,12},{6,14},{8,0},{10,2},{12,4},{14,6},{1,9},{3,11}... | collective-permute-start | bytes 49160 | tf_op jit(solution)/shard_map/ppermute | solution.py:86
  9.2 2.6 %collective-permute-start.4 = (bf16[4,16,128]{2,1,0:T(8,128)(2,1)S(1)}, bf16[4,16,128]{2,1,0:T(8,128)(2,1)S(1)}, u32[]{:S(2)}, u32[]{:S(2)}) collective-permute-start(bf16[4,16,128]{2,1,0:T(8,128)(2,1)S(1)} %get-tuple-element.6), channel_id=1, source_target_pairs={{0,10},{2,12},{4,14},{6,0},{8,2},{10,4},{12,6},{14,8},{1,11},{3,13... | collective-permute-start | bytes 49160 | tf_op jit(solution)/shard_map/ppermute | solution.py:86
  11.8 0.8 %compare_convert_fusion = f32[32,32]{1,0:T(8,128)S(1)} fusion(s32[32]{0:T(128)} %param.9), kind=kLoop, calls=%fused_computation.99 | loop fusion | flops 2048 | bytes 4224 | tf_op jit(solution)/shard_map/convert_element_type | solution.py:103
  12.6 0.7 %convert_element_type.47 = f32[32]{0:T(128)S(1)} convert(s32[32]{0:T(128)} %param.8) | non-fusion elementwise | flops 32 | bytes 256 | tf_op jit(solution)/shard_map/convert_element_type | solution.py:105
  13.5 1.4 %collective-permute-start.5 = (bf16[4,16,128]{2,1,0:T(8,128)(2,1)S(1)}, bf16[4,16,128]{2,1,0:T(8,128)(2,1)S(1)}, u32[]{:S(2)}, u32[]{:S(2)}) collective-permute-start(bf16[4,16,128]{2,1,0:T(8,128)(2,1)S(1)} %get-tuple-element.6), channel_id=1, source_target_pairs={{0,12},{2,14},{4,0},{6,2},{8,4},{10,6},{12,8},{14,10},{1,13},{3,15... | collective-permute-start | bytes 49160 | tf_op jit(solution)/shard_map/ppermute | solution.py:86
  15.0 1.4 %collective-permute-start.6 = (bf16[4,16,128]{2,1,0:T(8,128)(2,1)S(1)}, bf16[4,16,128]{2,1,0:T(8,128)(2,1)S(1)}, u32[]{:S(2)}, u32[]{:S(2)}) collective-permute-start(bf16[4,16,128]{2,1,0:T(8,128)(2,1)S(1)} %get-tuple-element.6), channel_id=1, source_target_pairs={{0,14},{2,0},{4,2},{6,4},{8,6},{10,8},{12,10},{14,12},{1,15},{3,1}... | collective-permute-start | bytes 49160 | tf_op jit(solution)/shard_map/ppermute | solution.py:86
  16.4 0.9 %collective-permute-done.5 = bf16[4,16,128]{2,1,0:T(8,128)(2,1)S(1)} collective-permute-done((bf16[4,16,128]{2,1,0:T(8,128)(2,1)S(1)}, bf16[4,16,128]{2,1,0:T(8,128)(2,1)S(1)}, u32[]{:S(2)}, u32[]{:S(2)}) %collective-permute-start.5) | collective-permute-done | bytes 16416 | tf_op jit(solution)/shard_map/ppermute | solution.py:86
  17.3 1.4 %collective-permute-done.6 = bf16[4,16,128]{2,1,0:T(8,128)(2,1)S(1)} collective-permute-done((bf16[4,16,128]{2,1,0:T(8,128)(2,1)S(1)}, bf16[4,16,128]{2,1,0:T(8,128)(2,1)S(1)}, u32[]{:S(2)}, u32[]{:S(2)}) %collective-permute-start.6) | collective-permute-done | bytes 16416 | tf_op jit(solution)/shard_map/ppermute | solution.py:86
  18.7 0.6 %gather_fusion = bf16[8,4,16,128]{3,2,1,0:T(8,128)(2,1)S(1)} fusion(bf16[8,4,16,128]{3,2,1,0:T(8,128)(2,1)S(1)} %constant_dynamic-update-slice_fusion, s32[1024]{0:T(1024)S(1)} %pad_clamp_fusion), kind=kCustom, calls=%fused_computation | custom fusion | bytes 262176 | tf_op jit(solution)/shard_map/jit(_take)/gather | solution.py:89
  19.7 1.1 %collective-permute-done.7 = bf16[32,16,128]{2,1,0:T(8,128)(2,1)S(1)} collective-permute-done((bf16[32,16,128]{2,1,0:T(8,128)(2,1)S(1)}, bf16[32,16,128]{2,1,0:T(8,128)(2,1)S(1)}, u32[]{:S(2)}, u32[]{:S(2)}) %collective-permute-start.7) | collective-permute-done | bytes 131104 | tf_op jit(solution)/shard_map/ppermute | solution.py:98
  21.0 0.4 fusion.18
  21.4 0.5 %multiply_reduce_fusion.1 = f32[32,32]{1,0:T(8,128)S(1)} fusion(f32[32,32,128]{2,1,0:T(8,128)S(1)} %constant_dynamic-update-slice_fusion.8, f32[32,32]{1,0:T(8,128)S(1)} %broadcast_multiply_fusion.4, f32[128]{0:T(128)S(1)} %copy-done.3, f32[32,32]{1,0:T(8,128)S(1)} %compare_convert_fusion), kind=kLoop, calls=%fused_computation.32 | loop fusion | flops 654336 | bytes 537088 | tf_op jit(solution)/shard_map/reduce_sum | solution.py:10
  21.9 0.5 %multiply_convert_fusion.1 = bf16[32,32,128]{2,1,0:T(8,128)(2,1)S(1)} fusion(f32[32,32,128]{2,1,0:T(8,128)S(1)} %constant_dynamic-update-slice_fusion.8, f32[32,32]{1,0:T(8,128)S(1)} %add_rsqrt_fusion.3, f32[32,32]{1,0:T(8,128)S(1)} %broadcast_multiply_fusion.4, f32[128]{0:T(128)S(1)} %copy-done.3, f32[32,32]{1,0:T(8,128)S(1)} %compare_convert_fusion), kind=kLoop, calls=%fused_computation.31 | loop fusion | flops 655360 | bytes 799232 | tf_op jit(solution)/shard_map/convert_element_type | solution.py:108
  23.3 2.3 %copy.50 = bf16[32,32,128]{1,0,2:T(8,128)(2,1)} copy(bf16[32,32,128]{2,1,0:T(8,128)(2,1)S(1)} %get-tuple-element.10) | data formatting | bytes 524288 | tf_op jit(solution)/shard_map/convert_element_type | solution.py:23
  25.6 2.4 %copy.51 = bf16[32,32,128]{1,0,2:T(8,128)(2,1)} copy(bf16[32,32,128]{2,1,0:T(8,128)(2,1)S(1)} %get-tuple-element.9) | data formatting | bytes 524288 | tf_op jit(solution)/shard_map/convert_element_type | solution.py:23
  28.0 2.2 %bitcast_reduce_fusion = (f32[32,32]{0,1:T(8,128)S(1)}, f32[128,32,32]{2,1,0:T(8,128)S(1)}) fusion(bf16[32,32,128]{1,0,2:T(8,128)(2,1)} %copy.50, bf16[32,32,128]{1,0,2:T(8,128)(2,1)} %copy.51), kind=kOutput, calls=%fused_computation.2 | convolution fusion | flops 8518656 | bytes 1052672 | tf_op jit(solution)/shard_map/ikh,jkh->ijh/dot_general | solution.py:111
  30.8 1.3 %multiply_convert_fusion = bf16[32,32,128]{0,1,2:T(8,128)(2,1)} fusion(f32[128,32,32]{2,1,0:T(8,128)S(1)} %get-tuple-element.12, f32[32,32]{0,1:T(8,128)S(1)} %copy.55, f32[32,32]{0,1:T(8,128)S(1)} %copy.53), kind=kLoop, calls=%fused_computation.3 | loop fusion | flops 393216 | bytes 794624 | tf_op jit(solution)/shard_map/convert_element_type | solution.py:27
  32.1 2.7 %copy.56 = bf16[32,32,128]{2,1,0:T(8,128)(2,1)S(1)} copy(bf16[32,32,128]{0,1,2:T(8,128)(2,1)} %multiply_convert_fusion) | data formatting | bytes 524288 | tf_op jit(solution)/shard_map/convert_element_type | solution.py:27
  37.3 0.5 %copy.59 = bf16[32,16,128]{0,1,2:T(8,128)(2,1)S(1)} copy(bf16[32,16,128]{2,1,0:T(8,128)(2,1)S(1)} %fusion.20) | data formatting | bytes 262144 | tf_op jit(solution)/shard_map/convert_element_type | solution.py:23
  38.6 0.8 %fusion.4 = f32[4,16,128]{2,1,0:T(8,128)} fusion(f32[4,16,128]{2,1,0:T(8,128)S(1)} %fusion.7, bf16[2,128,128]{2,1,0:T(8,128)(2,1)S(1)} %copy-done.2, f32[32,32,128]{2,1,0:T(8,128)S(1)} %fusion.3, s32[]{:T(128)S(6)} %select_n.57, s32[]{:T(128)S(6)} %select_n.58, f32[128,16,4]{0,1,2:T(8,128)S(1)} %copy.61, f32[4,16]{1,0:T(4,128)S(1)} %add_rsqrt_fusion.4, ...), kind=kOutput, calls=%fused_computation.12 | convolution fusion | flops 2138112 | bytes 167944 | tf_op jit(solution)/shard_map/dot_general | solution.py:16
  (72 shorter events, 5.6 us)
Async XLA Ops:
  0.0 21.0 %copy-start.1 = (f32[4,16,128]{2,1,0:T(8,128)S(1)}, f32[4,16,128]{2,1,0:T(8,128)}, u32[]{:S(2)}) copy-start(f32[4,16,128]{2,1,0:T(8,128)} %param.7) | copy-start | bytes 98308
  0.0 21.0 %copy-start.3 = (f32[128]{0:T(128)S(1)}, f32[128]{0:T(128)}, u32[]{:S(2)}) copy-start(f32[128]{0:T(128)} %param.10) | copy-start | bytes 1540
  0.8 12.7 %collective-permute-start = (bf16[4,16,128]{2,1,0:T(8,128)(2,1)S(1)}, bf16[4,16,128]{2,1,0:T(8,128)(2,1)S(1)}, u32[]{:S(2)}, u32[]{:S(2)}) collective-permute-start(bf16[4,16,128]{2,1,0:T(8,128)(2,1)S(1)} %get-tuple-element.6), channel_id=1, source_target_pairs={{0,2},{2,4},{4,6},{6,8},{8,10},{10,12},{12,14},{14,0},{1,3},{3,5},... | collective-permute-start | bytes 49160 | tf_op jit(solution)/shard_map/ppermute | solution.py:86
  3.8 11.1 %collective-permute-start.1 = (bf16[4,16,128]{2,1,0:T(8,128)(2,1)S(1)}, bf16[4,16,128]{2,1,0:T(8,128)(2,1)S(1)}, u32[]{:S(2)}, u32[]{:S(2)}) collective-permute-start(bf16[4,16,128]{2,1,0:T(8,128)(2,1)S(1)} %get-tuple-element.6), channel_id=1, source_target_pairs={{0,4},{2,6},{4,8},{6,10},{8,12},{10,14},{12,0},{14,2},{1,5},{3,7},... | collective-permute-start | bytes 49160 | tf_op jit(solution)/shard_map/ppermute | solution.py:86
  5.4 11.0 %collective-permute-start.2 = (bf16[4,16,128]{2,1,0:T(8,128)(2,1)S(1)}, bf16[4,16,128]{2,1,0:T(8,128)(2,1)S(1)}, u32[]{:S(2)}, u32[]{:S(2)}) collective-permute-start(bf16[4,16,128]{2,1,0:T(8,128)(2,1)S(1)} %get-tuple-element.6), channel_id=1, source_target_pairs={{0,6},{2,8},{4,10},{6,12},{8,14},{10,0},{12,2},{14,4},{1,7},{3,9},... | collective-permute-start | bytes 49160 | tf_op jit(solution)/shard_map/ppermute | solution.py:86
  7.9 8.5 %collective-permute-start.3 = (bf16[4,16,128]{2,1,0:T(8,128)(2,1)S(1)}, bf16[4,16,128]{2,1,0:T(8,128)(2,1)S(1)}, u32[]{:S(2)}, u32[]{:S(2)}) collective-permute-start(bf16[4,16,128]{2,1,0:T(8,128)(2,1)S(1)} %get-tuple-element.6), channel_id=1, source_target_pairs={{0,8},{2,10},{4,12},{6,14},{8,0},{10,2},{12,4},{14,6},{1,9},{3,11}... | collective-permute-start | bytes 49160 | tf_op jit(solution)/shard_map/ppermute | solution.py:86
  9.2 7.3 %collective-permute-start.4 = (bf16[4,16,128]{2,1,0:T(8,128)(2,1)S(1)}, bf16[4,16,128]{2,1,0:T(8,128)(2,1)S(1)}, u32[]{:S(2)}, u32[]{:S(2)}) collective-permute-start(bf16[4,16,128]{2,1,0:T(8,128)(2,1)S(1)} %get-tuple-element.6), channel_id=1, source_target_pairs={{0,10},{2,12},{4,14},{6,0},{8,2},{10,4},{12,6},{14,8},{1,11},{3,13... | collective-permute-start | bytes 49160 | tf_op jit(solution)/shard_map/ppermute | solution.py:86
  13.5 3.8 %collective-permute-start.5 = (bf16[4,16,128]{2,1,0:T(8,128)(2,1)S(1)}, bf16[4,16,128]{2,1,0:T(8,128)(2,1)S(1)}, u32[]{:S(2)}, u32[]{:S(2)}) collective-permute-start(bf16[4,16,128]{2,1,0:T(8,128)(2,1)S(1)} %get-tuple-element.6), channel_id=1, source_target_pairs={{0,12},{2,14},{4,0},{6,2},{8,4},{10,6},{12,8},{14,10},{1,13},{3,15... | collective-permute-start | bytes 49160 | tf_op jit(solution)/shard_map/ppermute | solution.py:86
  15.0 3.7 %collective-permute-start.6 = (bf16[4,16,128]{2,1,0:T(8,128)(2,1)S(1)}, bf16[4,16,128]{2,1,0:T(8,128)(2,1)S(1)}, u32[]{:S(2)}, u32[]{:S(2)}) collective-permute-start(bf16[4,16,128]{2,1,0:T(8,128)(2,1)S(1)} %get-tuple-element.6), channel_id=1, source_target_pairs={{0,14},{2,0},{4,2},{6,4},{8,6},{10,8},{12,10},{14,12},{1,15},{3,1}... | collective-permute-start | bytes 49160 | tf_op jit(solution)/shard_map/ppermute | solution.py:86
  16.4 6.0 %copy-start = (bf16[2,128,512]{2,1,0:T(8,128)(2,1)S(1)}, bf16[2,128,512]{2,1,0:T(8,128)(2,1)}, u32[]{:S(2)}) copy-start(bf16[2,128,512]{2,1,0:T(8,128)(2,1)} %param.11) | copy-start | bytes 786436
  19.4 1.4 %collective-permute-start.7 = (bf16[32,16,128]{2,1,0:T(8,128)(2,1)S(1)}, bf16[32,16,128]{2,1,0:T(8,128)(2,1)S(1)}, u32[]{:S(2)}, u32[]{:S(2)}) collective-permute-start(bf16[32,16,128]{2,1,0:T(8,128)(2,1)S(1)} %bitcast_select_fusion), channel_id=1, source_target_pairs={{0,1},{1,0},{2,3},{3,2},{4,5},{5,4},{6,7},{7,6},{8,9},{9,8},{10,11... | collective-permute-start | bytes 393224 | tf_op jit(solution)/shard_map/ppermute | solution.py:98
  30.8 3.9 %copy-start.4 = (bf16[2,128,128]{2,1,0:T(8,128)(2,1)S(1)}, bf16[2,128,128]{2,1,0:T(8,128)(2,1)}, u32[]{:S(2)}) copy-start(bf16[2,128,128]{2,1,0:T(8,128)(2,1)} %param.12) | copy-start | bytes 196612
  32.1 3.0 %copy-start.2 = (bf16[2,128,128]{2,1,0:T(8,128)(2,1)S(1)}, bf16[2,128,128]{2,1,0:T(8,128)(2,1)}, u32[]{:S(2)}) copy-start(bf16[2,128,128]{2,1,0:T(8,128)(2,1)} %param.13) | copy-start | bytes 196612

commit v2 on v1

--- a/solution.py
+++ b/solution.py
@@ -79,14 +79,8 @@
 
 
 def gather_rows(block):
-    n = lax.axis_size("row")
-    me = lax.axis_index("row")
-    parts = [block]
-    for s in range(1, n):
-        parts.append(lax.ppermute(block, "row", [(i, (i + s) % n) for i in range(n)]))
-    stacked = jnp.stack(parts)
-    order = lax.rem(me - jnp.arange(n) + n, n)
-    return jnp.take(stacked, order, axis=0).reshape((-1,) + block.shape[1:])
+    copies = jnp.broadcast_to(block, (lax.axis_size("row"),) + block.shape)
+    return lax.all_to_all(copies, "row", split_axis=0, concat_axis=0, tiled=True).reshape((-1,) + block.shape[1:])
 
 
 def whole_crop_plan(pair, token_mask, chains, chain_bias, proj_weight, gate_weight, out_weight):
@@ -94,12 +88,11 @@
     row_start = lax.axis_index("row") * rows
     col = lax.axis_index("col")
     col_start = col * cols
-    mine = gather_rows(pair.astype(jnp.bfloat16))
+    mine = gather_rows(pair)
     other = lax.ppermute(mine, "col", [(0, 1), (1, 0)])
     first = jnp.where(col == 0, mine, other)
     second = jnp.where(col == 0, other, mine)
-    whole = jnp.concatenate([first, second], axis=1).astype(jnp.float32)
-    whole = lax.dynamic_update_slice(whole, pair, (row_start, col_start, 0))
+    whole = jnp.concatenate([first, second], axis=1)
     same = (chains[:, None] == chains[None, :]).astype(jnp.float32)
     state = whole + same[..., None] * chain_bias
     mask = token_mask.astype(jnp.float32)

time: 39.7 us -> 38.6 us (0.972)
  starting transfers between devices: 13.8 us -> 7.28 us
  waiting for transfers between devices: 3.37 us -> 8.69 us
  local copies, waits for them, and re-layouts: 9.39 us -> 10.1 us
  other arithmetic: 7.47 us -> 7.04 us
    ppermute x7 -> x0, starting transfers between devices: 13.8 us -> none  [gather_rows(): lax.ppermute(block, 'row', [(i, (i + s) % n) for i in range(n)])]
    all_to_all x0 -> x1, waiting for transfers between devices: none -> 8.11 us  [gather_rows(): lax.all_to_all(copies, 'row', split_axis=0, concat_axis=0, tiled=True)]
    all_to_all x0 -> x1, starting transfers between devices: none -> 7.28 us  [gather_rows(): lax.all_to_all(copies, 'row', split_axis=0, concat_axis=0, tiled=True)]
    ppermute x7 -> x0, waiting for transfers between devices: 2.26 us -> none  [gather_rows(): lax.ppermute(block, 'row', [(i, (i + s) % n) for i in range(n)])]
    broadcast_in_dim x2 -> x1, local copies, waits for them, and re-layouts: 0.17 us -> 1.51 us  [gather_rows(): copies = jnp.broadcast_to(block, (lax.axis_size('row'),) + block.shape)]
    unnamed x1 -> x0, other arithmetic: 0.83 us -> none
    reduce_sum x4, other arithmetic: 0.73 us -> 1.38 us  [layer_norm(): mean = jnp.mean(values, -1, keepdims=True)]
    gather x1 -> x0, local copies, waits for them, and re-layouts: 0.57 us -> none  [gather_rows(): return jnp.take(stacked, order, axis=0).reshape((-1,) + block.shape[1:])]
  transfers between devices with their start and end apart: 8 -> 2, of which waited for: 3 -> 2; matrix products, arithmetic and copies ran while one was open for 5% -> 5% of each run, Pallas kernels for 0% -> 0%
where the time goes in v2:
time: 38.6 us; the launch traced here: 38.3 us
  local copies, waits for them, and re-layouts  10.1 us (26%)
  waiting for transfers between devices  8.69 us (23%)
  starting transfers between devices  7.28 us (19%)
  other arithmetic  7.04 us (18%)
  matrix products  4.95 us (13%)
    all_to_all x1, waiting for transfers between devices, gather_rows(): lax.all_to_all(copies, 'row', split_axis=0, concat_axis=0, tiled=True)  8.11 us
    all_to_all x1, starting transfers between devices, gather_rows(): lax.all_to_all(copies, 'row', split_axis=0, concat_axis=0, tiled=True)  7.28 us
    convert_element_type x4, local copies, waits for them, and re-layouts, edge(): (jax.nn.sigmoid(proj[..., :hidden]) * proj[..., hidden:] * mask[..., None...  5.28 us
    convert_element_type x1, local copies, waits for them, and re-layouts, finish(): tnorm = layer_norm(tri).astype(jnp.bfloat16)  2.65 us
    dot_general x8, matrix products, flat_dot(): jnp.dot(values.reshape(-1, shape[-1]), weight, preferred_element_type=jnp...  2.38 us
    dot_general x1, matrix products, whole_crop_plan(): jnp.einsum('ikh,jkh->ijh', left, right, preferred_element_type=jnp.float32)  2.2 us
    broadcast_in_dim x1, local copies, waits for them, and re-layouts, gather_rows(): copies = jnp.broadcast_to(block, (lax.axis_size('row'),) + block.shape)  1.51 us
    reduce_sum x5, other arithmetic, layer_norm(): var = jnp.mean(centred * centred, -1, keepdims=True)  1.4 us
  transfers between devices with their start and end apart: 2, of which 2 were waited for; matrix products, arithmetic and copies ran while one was open for 5% of the time, Pallas kernels for 0%

profile of v2, /device:TPU:0, one launch (start us, length us, event | category | flops | bytes accessed | tf_op | source)
XLA Modules:
  0.0 38.3 jit_solution(442554405253613719)
XLA Ops:
  0.0 1.5 %broadcast_in_dim.2 = f32[8,4,16,128]{3,2,1,0:T(8,128)} broadcast(f32[4,16,128]{2,1,0:T(8,128)} %param.7), dimensions={1,2,3} | broadcast | bytes 294912 | tf_op jit(solution)/shard_map/broadcast_in_dim | solution.py:82
  1.5 7.3 %all-to-all-start = ((f32[8,4,16,128]{3,2,1,0:T(8,128)}), f32[8,4,16,128]{3,2,1,0:T(8,128)S(1)}, u32[]{:S(2)}, u32[]{:S(2)}) async-start(f32[8,4,16,128]{3,2,1,0:T(8,128)} %broadcast_in_dim.2), calls=%async_computation | async-start | bytes 524288 | tf_op jit(solution)/shard_map/all_to_all | solution.py:83
  8.8 0.7 %convert_element_type.49 = f32[32]{0:T(128)S(1)} convert(s32[32]{0:T(128)} %param.8) | non-fusion elementwise | flops 32 | bytes 256 | tf_op jit(solution)/shard_map/convert_element_type | solution.py:98
  9.6 8.1 %all-to-all-done = f32[8,4,16,128]{3,2,1,0:T(8,128)S(1)} async-done(((f32[8,4,16,128]{3,2,1,0:T(8,128)}), f32[8,4,16,128]{3,2,1,0:T(8,128)S(1)}, u32[]{:S(2)}, u32[]{:S(2)}) %all-to-all-start) | async-done | bytes 262176 | tf_op jit(solution)/shard_map/all_to_all | solution.py:83
  17.9 0.8 %compare_convert_fusion = f32[32,32]{1,0:T(8,128)S(1)} fusion(s32[32]{0:T(128)} %param.9), kind=kLoop, calls=%fused_computation.88 | loop fusion | flops 2048 | bytes 4224 | tf_op jit(solution)/shard_map/convert_element_type | solution.py:96
  18.7 0.6 %collective-permute-done = f32[32,16,128]{2,1,0:T(8,128)S(1)} collective-permute-done((f32[32,16,128]{2,1,0:T(8,128)S(1)}, f32[32,16,128]{2,1,0:T(8,128)S(1)}, u32[]{:S(2)}, u32[]{:S(2)}) %collective-permute-start) | collective-permute-done | bytes 262176 | tf_op jit(solution)/shard_map/ppermute | solution.py:92
  19.3 1.0 %fusion.40 = f32[32,32]{1,0:T(8,128)S(1)} fusion(f32[128]{0:T(128)} %param.10, f32[32,32]{1,0:T(8,128)S(1)} %compare_convert_fusion, f32[32,16,128]{2,1,0:T(8,128)S(1)} %get-tuple-element.6, f32[32,16,128]{2,1,0:T(8,128)S(1)} %get-tuple-element.5), kind=kLoop, calls=%fused_computation.67 | loop fusion | flops 523264 | bytes 532992 | tf_op jit(solution)/shard_map/reduce_sum | solution.py:8
  20.4 0.5 %multiply_reduce_fusion.1 = f32[32,32]{1,0:T(8,128)S(1)} fusion(f32[32,32]{1,0:T(8,128)S(1)} %broadcast_multiply_fusion.4, f32[128]{0:T(128)S(1)} %copy-done.2, f32[32,32]{1,0:T(8,128)S(1)} %compare_convert_fusion, f32[32,16,128]{2,1,0:T(8,128)S(1)} %get-tuple-element.6, f32[32,16,128]{2,1,0:T(8,128)S(1)} %get-tuple-element.5), kind=kLoop, calls=%fused_computation.32 | loop fusion | flops 785408 | bytes 537088 | tf_op jit(solution)/shard_map/reduce_sum | solution.py:10
  20.9 0.5 %multiply_convert_fusion.1 = bf16[32,32,128]{2,1,0:T(8,128)(2,1)S(1)} fusion(f32[32,32]{1,0:T(8,128)S(1)} %add_rsqrt_fusion.3, f32[32,32]{1,0:T(8,128)S(1)} %broadcast_multiply_fusion.4, f32[128]{0:T(128)S(1)} %copy-done.2, f32[32,32]{1,0:T(8,128)S(1)} %compare_convert_fusion, f32[32,16,128]{2,1,0:T(8,128)S(1)} %get-tuple-element.6, ...), kind=kLoop, calls=%fused_computation.31 | loop fusion | flops 786432 | bytes 799232 | tf_op jit(solution)/shard_map/convert_element_type | solution.py:101
  21.4 0.3 fusion.32
  21.6 0.3 fusion.34
  21.9 0.3 fusion.9
  22.2 2.3 %copy.40 = bf16[32,32,128]{1,0,2:T(8,128)(2,1)} copy(bf16[32,32,128]{2,1,0:T(8,128)(2,1)S(1)} %get-tuple-element.8) | data formatting | bytes 524288 | tf_op jit(solution)/shard_map/convert_element_type | solution.py:23
  24.6 2.4 %copy.41 = bf16[32,32,128]{1,0,2:T(8,128)(2,1)} copy(bf16[32,32,128]{2,1,0:T(8,128)(2,1)S(1)} %get-tuple-element.7) | data formatting | bytes 524288 | tf_op jit(solution)/shard_map/convert_element_type | solution.py:23
  26.9 2.2 %bitcast_reduce_fusion = (f32[32,32]{0,1:T(8,128)S(1)}, f32[128,32,32]{2,1,0:T(8,128)S(1)}) fusion(bf16[32,32,128]{1,0,2:T(8,128)(2,1)} %copy.40, bf16[32,32,128]{1,0,2:T(8,128)(2,1)} %copy.41), kind=kOutput, calls=%fused_computation.1 | convolution fusion | flops 8518656 | bytes 1052672 | tf_op jit(solution)/shard_map/ikh,jkh->ijh/dot_general | solution.py:104
  29.3 0.3 multiply_reduce_fusion
  29.8 1.3 %multiply_convert_fusion = bf16[32,32,128]{0,1,2:T(8,128)(2,1)} fusion(f32[128,32,32]{2,1,0:T(8,128)S(1)} %get-tuple-element.10, f32[32,32]{0,1:T(8,128)S(1)} %copy.45, f32[32,32]{0,1:T(8,128)S(1)} %copy.43), kind=kLoop, calls=%fused_computation.2 | loop fusion | flops 393216 | bytes 794624 | tf_op jit(solution)/shard_map/convert_element_type | solution.py:27
  31.0 2.7 %copy.46 = bf16[32,32,128]{2,1,0:T(8,128)(2,1)S(1)} copy(bf16[32,32,128]{0,1,2:T(8,128)(2,1)} %multiply_convert_fusion) | data formatting | bytes 524288 | tf_op jit(solution)/shard_map/convert_element_type | solution.py:27
  33.7 0.3 fusion.2
  34.0 0.2 fusion.3
  34.5 0.2 multiply_reduce_fusion.2
  36.3 0.5 %copy.49 = bf16[32,16,128]{0,1,2:T(8,128)(2,1)S(1)} copy(bf16[32,16,128]{2,1,0:T(8,128)(2,1)S(1)} %fusion.19) | data formatting | bytes 262144 | tf_op jit(solution)/shard_map/convert_element_type | solution.py:23
  36.7 0.4 fusion.54
  37.5 0.8 %fusion.4 = f32[4,16,128]{2,1,0:T(8,128)} fusion(f32[4,16,128]{2,1,0:T(8,128)S(1)} %fusion.7, bf16[2,128,128]{2,1,0:T(8,128)(2,1)S(1)} %copy-done.1, f32[32,32,128]{2,1,0:T(8,128)S(1)} %fusion.3, s32[]{:T(128)S(6)} %select_n.30, s32[]{:T(128)S(6)} %select_n.32, f32[128,16,4]{0,1,2:T(8,128)S(1)} %copy.51, f32[4,16]{1,0:T(4,128)S(1)} %add_rsqrt_fusion.4, ...), kind=kOutput, calls=%fused_computation.11 | convolution fusion | flops 2138112 | bytes 167944 | tf_op jit(solution)/shard_map/dot_general | solution.py:16
  (42 shorter events, 2.7 us)
Async XLA Ops:
  0.0 20.3 %copy-start.2 = (f32[128]{0:T(128)S(1)}, f32[128]{0:T(128)}, u32[]{:S(2)}) copy-start(f32[128]{0:T(128)} %param.10) | copy-start | bytes 1540
  0.0 21.3 %copy-start = (bf16[2,128,512]{2,1,0:T(8,128)(2,1)S(1)}, bf16[2,128,512]{2,1,0:T(8,128)(2,1)}, u32[]{:S(2)}) copy-start(bf16[2,128,512]{2,1,0:T(8,128)(2,1)} %param.11) | copy-start | bytes 786436
  1.5 16.2 %all-to-all-start = ((f32[8,4,16,128]{3,2,1,0:T(8,128)}), f32[8,4,16,128]{3,2,1,0:T(8,128)S(1)}, u32[]{:S(2)}, u32[]{:S(2)}) async-start(f32[8,4,16,128]{3,2,1,0:T(8,128)} %broadcast_in_dim.2), calls=%async_computation | async-start | bytes 524288 | tf_op jit(solution)/shard_map/all_to_all | solution.py:83
  17.7 1.5 %collective-permute-start = (f32[32,16,128]{2,1,0:T(8,128)S(1)}, f32[32,16,128]{2,1,0:T(8,128)S(1)}, u32[]{:S(2)}, u32[]{:S(2)}) collective-permute-start(f32[32,16,128]{2,1,0:T(8,128)S(1)} %bitcast.59), channel_id=1, source_target_pairs={{0,1},{1,0},{2,3},{3,2},{4,5},{5,4},{6,7},{7,6},{8,9},{9,8},{10,11... | collective-permute-start | bytes 786440 | tf_op jit(solution)/shard_map/ppermute | solution.py:92
  29.8 3.9 %copy-start.3 = (bf16[2,128,128]{2,1,0:T(8,128)(2,1)S(1)}, bf16[2,128,128]{2,1,0:T(8,128)(2,1)}, u32[]{:S(2)}) copy-start(bf16[2,128,128]{2,1,0:T(8,128)(2,1)} %param.12) | copy-start | bytes 196612
  31.0 3.0 %copy-start.1 = (bf16[2,128,128]{2,1,0:T(8,128)(2,1)S(1)}, bf16[2,128,128]{2,1,0:T(8,128)(2,1)}, u32[]{:S(2)}) copy-start(bf16[2,128,128]{2,1,0:T(8,128)(2,1)} %param.13) | copy-start | bytes 196612

commit v3 on v0

--- a/solution.py
+++ b/solution.py
@@ -1,6 +1,9 @@
+import functools
 import jax
 import jax.numpy as jnp
 from jax import lax
+from jax.experimental import pallas as pl
+from jax.experimental.pallas import tpu as pltpu
 from jax.sharding import PartitionSpec as P
 
 
@@ -36,7 +39,7 @@
     return state + gate * flat_dot(tnorm, o_weight)
 
 
-def shards(pair, token_mask, chains, chain_bias, proj_weight, gate_weight, out_weight):
+def sharded_plan(pair, token_mask, chains, chain_bias, proj_weight, gate_weight, out_weight):
     rows, cols, width = pair.shape
     row_start = lax.axis_index("row") * rows
     col_start = lax.axis_index("col") * cols
@@ -72,6 +75,211 @@
     return finish(state, normed, tri, gate_weight[1], out_weight[1])
 
 
+def tile_norm(values):
+    mean = jnp.mean(values, -1, keepdims=True)
+    centred = values - mean
+    var = jnp.mean(centred * centred, -1, keepdims=True)
+    return centred * lax.rsqrt(var + 1e-05)
+
+
+def gate_of(values):
+    return 0.5 * jnp.tanh(0.5 * values) + 0.5
+
+
+def dot(values, weight):
+    return jnp.dot(values, weight, preferred_element_type=jnp.float32)
+
+
+def rounded(values):
+    return values.astype(jnp.bfloat16).astype(jnp.float32)
+
+
+def crop_kernel(
+    masks,
+    chains_s,
+    mask_s,
+    mine,
+    other,
+    chains_v,
+    mask_v,
+    bias,
+    proj_w,
+    gate_w,
+    out_w,
+    updated,
+    start,
+    left,
+    right,
+    gates,
+    tris,
+    left1,
+    right1,
+):
+    ranks, rows, cols, width = mine.shape
+    tokens = ranks * rows
+    me = lax.axis_index("row")
+    col = lax.axis_index("col")
+    chunk = min(4, ranks)
+    bias_v = bias[...]
+    hidden = proj_w.shape[2] // 4
+
+    for half, source in enumerate((mine, other)):
+        first = pl.multiple_of(jnp.where(col == half, 0, cols), cols)
+        chain_cols = chains_v[pl.ds(first, cols), :]
+        mask_cols = mask_v[pl.ds(first, cols), :]
+        for base in range(0, ranks, chunk):
+            states, pmasks = [], []
+            for slot in range(base, base + chunk):
+                for t in range(rows):
+                    token = (me ^ masks[slot]) * rows + t
+                    same = chain_cols == chains_s[token]
+                    states.append(source[slot, t] + jnp.where(same, bias_v, 0.0))
+                    pmasks.append(mask_cols * mask_s[token].astype(jnp.float32))
+            state = jnp.concatenate(states, 0)
+            pmask = jnp.concatenate(pmasks, 0)
+            start[half, pl.ds(base * rows * cols, chunk * rows * cols), :] = state
+            normed = tile_norm(state).astype(jnp.bfloat16)
+            proj = dot(normed, proj_w[0])
+            gates[half, pl.ds(base * rows * cols, chunk * rows * cols), :] = dot(normed, gate_w[0])
+            lft = rounded(gate_of(proj[:, :hidden]) * proj[:, hidden : 2 * hidden] * pmask)
+            rgt = rounded(gate_of(proj[:, 2 * hidden : 3 * hidden]) * proj[:, 3 * hidden :] * pmask)
+            for n in range(chunk * rows):
+                k = base * rows + n
+                left[pl.ds(k * tokens + half * cols, cols), :] = lft[n * cols : (n + 1) * cols]
+                slot, t = divmod(k, rows)
+                token = (me ^ masks[slot]) * rows + t
+                right[pl.ds(half * cols * tokens + token, cols, tokens), :] = rgt[n * cols : (n + 1) * cols]
+
+    low = me * rows // 8 * 8
+    groups = [col * cols + 8 * n for n in range(cols // 8)] + [low]
+    groups = [pl.multiple_of(g, 8) for g in groups]
+    count = len(groups)
+    block = 8
+
+    def tri_block(step, carry):
+        k0 = step * block
+        acc = [[None] * count for _ in range(block)]
+        for l in range(tokens):
+            cells = [right[pl.ds(pl.multiple_of(l * tokens + g, 8), 8), :] for g in groups]
+            for k in range(block):
+                row = left[pl.ds((k0 + k) * tokens + l, 1), :]
+                for n in range(count):
+                    term = row * cells[n]
+                    acc[k][n] = term if l == 0 else acc[k][n] + term
+        for n in range(count):
+            for k in range(block):
+                tris[n, pl.ds(pl.multiple_of((k0 + k) * 8, 8), 8), :] = acc[k][n]
+        return carry
+
+    lax.fori_loop(0, tokens // block, tri_block, 0)
+
+    own_half = jnp.where(low // cols == col, 0, 1)
+    low_off = lax.rem(low, cols)
+    mask_left = mask_v[pl.ds(pl.multiple_of(low, 8), 8), :]
+    mask_right = mask_v[pl.ds(pl.multiple_of(col * cols, cols), cols), :]
+
+    def gather(source, n, k):
+        if n < count - 1:
+            return source[0, pl.ds(k * cols + 8 * n, 8), :]
+        return source[own_half, pl.ds(pl.multiple_of(k * cols + low_off, 8), 8), :]
+
+    def updated_state(n):
+        tri = tris[n]
+        tnorm = tile_norm(tri).astype(jnp.bfloat16)
+        gate = gate_of(jnp.concatenate([gather(gates, n, k) for k in range(tokens)], 0))
+        state = jnp.concatenate([gather(start, n, k) for k in range(tokens)], 0)
+        return state + gate * dot(tnorm, out_w[0])
+
+    row_masks = []
+    for slot in range(ranks):
+        for t in range(rows):
+            row_masks.append(mask_s[(me ^ masks[slot]) * rows + t].astype(jnp.float32))
+
+    normed = tile_norm(updated_state(count - 1)).astype(jnp.bfloat16)
+    proj = dot(normed, proj_w[1, :, : 2 * hidden])
+    edge = gate_of(proj[:, :hidden]) * proj[:, hidden:]
+    pm = jnp.concatenate([mask_left * m for m in row_masks], 0)
+    left1[...] = rounded(edge * pm)
+
+    own_state, own_logits = [], []
+    for n in range(count - 1):
+        state = updated_state(n)
+        normed = tile_norm(state).astype(jnp.bfloat16)
+        own_state.append(state[: rows * 8])
+        own_logits.append(dot(normed[: rows * 8], gate_w[1]))
+        proj = dot(normed, proj_w[1, :, 2 * hidden :])
+        edge = gate_of(proj[:, :hidden]) * proj[:, hidden:]
+        pm = jnp.concatenate([mask_right[8 * n : 8 * n + 8] * m for m in row_masks], 0)
+        right1[n] = rounded(edge * pm)
+
+    shift = lax.rem(me * rows, 8)
+    acc = [[None] * (count - 1) for _ in range(rows)]
+    for k in range(tokens):
+        cells = [right1[n, pl.ds(k * 8, 8), :] for n in range(count - 1)]
+        for t in range(rows):
+            row = left1[pl.ds(k * 8 + shift + t, 1), :]
+            for n in range(count - 1):
+                term = row * cells[n]
+                acc[t][n] = term if k == 0 else acc[t][n] + term
+    for n in range(count - 1):
+        tri = jnp.concatenate([acc[t][n] for t in range(rows)], 0)
+        tnorm = tile_norm(tri).astype(jnp.bfloat16)
+        out = own_state[n] + gate_of(own_logits[n]) * dot(tnorm, out_w[1])
+        for t in range(rows):
+            updated[t, pl.ds(8 * n, 8), :] = out[8 * t : 8 * t + 8]
+
+
+def exchange(block, bits):
+    ranks = lax.axis_size("row")
+    return lax.ppermute(block, "row", [(i, i ^ bits) for i in range(ranks)])
+
+
+def whole_crop_plan(pair, token_mask, chains, chain_bias, proj_weight, gate_weight, out_weight):
+    rows, cols, width = pair.shape
+    ranks = lax.axis_size("row")
+    tokens = token_mask.shape[0]
+    hidden = proj_weight.shape[2] // 4
+    top = ranks // 2
+    two = jnp.stack([pair, exchange(pair, top)])
+    masks = [0, top]
+    parts = [two]
+    for bits in list(range(top - 1, 0, -1)):
+        parts.append(exchange(two, bits))
+        masks += [bits, bits ^ top]
+    mine = jnp.concatenate(parts, 0)
+    other = lax.ppermute(mine, "col", [(0, 1), (1, 0)])
+    chains_v = jnp.broadcast_to(chains[:, None], (tokens, width))
+    mask_v = jnp.broadcast_to(token_mask.astype(jnp.float32)[:, None], (tokens, width))
+    groups = cols // 8 + 1
+    smem = pl.BlockSpec(memory_space=pltpu.SMEM)
+    vmem = pl.BlockSpec(memory_space=pltpu.VMEM)
+    return pl.pallas_call(
+        functools.partial(crop_kernel, masks),
+        out_shape=jax.ShapeDtypeStruct(pair.shape, jnp.float32),
+        in_specs=[smem, smem] + [vmem] * 8,
+        out_specs=vmem,
+        scratch_shapes=[
+            pltpu.VMEM((2, tokens * cols, width), jnp.float32),
+            pltpu.VMEM((tokens * tokens, hidden), jnp.float32),
+            pltpu.VMEM((tokens * tokens, hidden), jnp.float32),
+            pltpu.VMEM((2, tokens * cols, width), jnp.float32),
+            pltpu.VMEM((groups, tokens * 8, hidden), jnp.float32),
+            pltpu.VMEM((tokens * 8, hidden), jnp.float32),
+            pltpu.VMEM((groups - 1, tokens * 8, hidden), jnp.float32),
+        ],
+        compiler_params=pltpu.CompilerParams(vmem_limit_bytes=32 << 20),
+        name="crop",
+    )(chains, token_mask, mine, other, chains_v, mask_v, chain_bias[None, :], proj_weight, gate_weight, out_weight)
+
+
+def shards(pair, token_mask, *rest):
+    tokens = token_mask.shape[0]
+    ranks = lax.axis_size("row")
+    small = tokens * tokens * pair.shape[2] <= 1 << 18 and ranks & (ranks - 1) == 0 and tokens % 16 == 0
+    plan = whole_crop_plan if small and lax.axis_size("col") == 2 else sharded_plan
+    return plan(pair, token_mask, *rest)
+
+
 def solution(mesh):
     placed = (P(("group", "row"), "col", None), P("group"), P("group"), P(), P(), P(), P())
     return jax.shard_map(

time: 88.6 us -> 21.6 us (0.24)
  blocking collectives: 69.2 us -> 0 us
  waiting for transfers between devices: 0.01 us -> 7.1 us
  local copies, waits for them, and re-layouts: 6.71 us -> 1.63 us
  Pallas kernels: 0 us -> 4.9 us
  matrix products: 3.87 us -> 0 us
  other arithmetic: 2.83 us -> 0.01 us
  starting transfers between devices: 5.5 us -> 7.66 us
    all_gather x5 -> x0, blocking collectives: 69.2 us -> none  [the longest x1 32.4 us: shards(): lax.all_gather(right_rows, 'row', axis=0, tiled=True)]
    ppermute x0 -> x5, starting transfers between devices: none -> 7.66 us  [the longest x4 7.59 us: exchange(): return lax.ppermute(block, 'row', [(i, i ^ bits) for i in range(ranks)])]
    ppermute x0 -> x5, waiting for transfers between devices: none -> 7.1 us  [the longest x4 5.6 us: exchange(): return lax.ppermute(block, 'row', [(i, i ^ bits) for i in range(ranks)])]
    all_to_all x1 -> x0, starting transfers between devices: 5.5 us -> none  [shards(): lax.all_to_all(left_rows, 'row', split_axis=1, concat_axis=0, tiled=True)]
    pallas_call x0 -> x1, Pallas kernels: none -> 4.9 us  [whole_crop_plan(): pl.pallas_call(functools.partial(crop_kernel, masks), out_shape=jax.Shape...]
    dot_general x8 -> x0, matrix products: 3.87 us -> none  [the longest x6 2.86 us: flat_dot(): jnp.dot(values.reshape(-1, shape[-1]), weight, preferred_element_type=jnp...]
    all_gather x4 -> x0, local copies, waits for them, and re-layouts: 3.65 us -> none  [the longest x1 1.45 us: shards(): lax.all_gather(right_rows, 'row', axis=0, tiled=True)]
    convert_element_type x5 -> x1, other arithmetic: 1.71 us -> 0.01 us  [whole_crop_plan(): token_mask.astype(jnp.float32)[:, None]]
  transfers between devices with their start and end apart: 1 -> 5, of which waited for: 0 -> 5; matrix products, arithmetic and copies ran while one was open for 2% -> 4% of each run, Pallas kernels for 0% -> 0%
where the time goes in v3:
time: 21.6 us; the launch traced here: 21.4 us
  starting transfers between devices  7.66 us (35%)
  waiting for transfers between devices  7.1 us (33%)
  Pallas kernels  4.9 us (23%)
  local copies, waits for them, and re-layouts  1.63 us (8%)
    ppermute x4, starting transfers between devices, exchange(): return lax.ppermute(block, 'row', [(i, i ^ bits) for i in range(ranks)])  7.59 us
    ppermute x4, waiting for transfers between devices, exchange(): return lax.ppermute(block, 'row', [(i, i ^ bits) for i in range(ranks)])  5.6 us
    pallas_call x1, Pallas kernels, whole_crop_plan(): pl.pallas_call(functools.partial(crop_kernel, masks), out_shape=jax.Shape...  4.9 us
    ppermute x1, waiting for transfers between devices, whole_crop_plan(): other = lax.ppermute(mine, 'col', [(0, 1), (1, 0)])  1.5 us
    unnamed x18, local copies, waits for them, and re-layouts  1.48 us
  transfers between devices with their start and end apart: 5, of which 5 were waited for; matrix products, arithmetic and copies ran while one was open for 4% of the time, Pallas kernels for 0%

profile of v3, /device:TPU:0, one launch (start us, length us, event | category | flops | bytes accessed | tf_op | source)
XLA Modules:
  0.0 21.4 jit_solution(14571072466074880405)
XLA Ops:
  0.0 4.0 %collective-permute-start = (f32[4,16,128]{2,1,0:T(8,128)}, f32[4,16,128]{2,1,0:T(8,128)S(1)}, u32[]{:S(2)}, u32[]{:S(2)}) collective-permute-start(f32[4,16,128]{2,1,0:T(8,128)} %param.7), channel_id=1, source_target_pairs={{0,8},{2,10},{4,12},{6,14},{8,0},{10,2},{12,4},{14,6},{1,9},{3,11}... | collective-permute-start | bytes 98312 | tf_op jit(solution)/shard_map/ppermute | solution.py:234
  4.0 0.8 %constant_dynamic-update-slice_fusion.4 = f32[8,4,16,128]{3,2,1,0:T(8,128)S(1)} fusion(f32[4,16,128]{2,1,0:T(8,128)} %param.7), kind=kLoop, calls=%fused_computation.5 | loop fusion | bytes 65536
  4.8 1.7 %collective-permute-done = f32[4,16,128]{2,1,0:T(8,128)S(1)} collective-permute-done((f32[4,16,128]{2,1,0:T(8,128)}, f32[4,16,128]{2,1,0:T(8,128)S(1)}, u32[]{:S(2)}, u32[]{:S(2)}) %collective-permute-start) | collective-permute-done | bytes 32800 | tf_op jit(solution)/shard_map/ppermute | solution.py:234
  6.6 0.0 copy-done.6
  6.6 0.0 copy-start
  6.6 2.5 %collective-permute-start.1 = (f32[2,4,16,128]{3,2,1,0:T(8,128)S(1)}, f32[2,4,16,128]{3,2,1,0:T(8,128)S(1)}, u32[]{:S(2)}, u32[]{:S(2)}) collective-permute-start(f32[2,4,16,128]{3,2,1,0:T(8,128)S(1)} %pad_maximum_fusion), channel_id=1, source_target_pairs={{0,6},{2,4},{4,2},{6,0},{8,14},{10,12},{12,10},{14,8},{1,7},{3,5},... | collective-permute-start | bytes 196616 | tf_op jit(solution)/shard_map/ppermute | solution.py:234
  9.1 0.7 %collective-permute-start.2 = (f32[2,4,16,128]{3,2,1,0:T(8,128)S(1)}, f32[2,4,16,128]{3,2,1,0:T(8,128)S(1)}, u32[]{:S(2)}, u32[]{:S(2)}) collective-permute-start(f32[2,4,16,128]{3,2,1,0:T(8,128)S(1)} %pad_maximum_fusion), channel_id=1, source_target_pairs={{0,4},{2,6},{4,0},{6,2},{8,12},{10,14},{12,8},{14,10},{1,5},{3,7},... | collective-permute-start | bytes 196616 | tf_op jit(solution)/shard_map/ppermute | solution.py:234
  9.8 0.3 %collective-permute-start.3 = (f32[2,4,16,128]{3,2,1,0:T(8,128)S(1)}, f32[2,4,16,128]{3,2,1,0:T(8,128)S(1)}, u32[]{:S(2)}, u32[]{:S(2)}) collective-permute-start(f32[2,4,16,128]{3,2,1,0:T(8,128)S(1)} %pad_maximum_fusion), channel_id=1, source_target_pairs={{0,2},{2,0},{4,6},{6,4},{8,10},{10,8},{12,14},{14,12},{1,3},{3,1},... | collective-permute-start | bytes 196616 | tf_op jit(solution)/shard_map/ppermute | solution.py:234
  10.1 1.7 %collective-permute-done.1 = f32[2,4,16,128]{3,2,1,0:T(8,128)S(1)} collective-permute-done((f32[2,4,16,128]{3,2,1,0:T(8,128)S(1)}, f32[2,4,16,128]{3,2,1,0:T(8,128)S(1)}, u32[]{:S(2)}, u32[]{:S(2)}) %collective-permute-start.1) | collective-permute-done | bytes 65568 | tf_op jit(solution)/shard_map/ppermute | solution.py:234
  11.8 1.5 %collective-permute-done.2 = f32[2,4,16,128]{3,2,1,0:T(8,128)S(1)} collective-permute-done((f32[2,4,16,128]{3,2,1,0:T(8,128)S(1)}, f32[2,4,16,128]{3,2,1,0:T(8,128)S(1)}, u32[]{:S(2)}, u32[]{:S(2)}) %collective-permute-start.2) | collective-permute-done | bytes 65568 | tf_op jit(solution)/shard_map/ppermute | solution.py:234
  13.4 0.0 copy-start.1
  13.4 0.0 copy-start.2
  13.4 0.7 %collective-permute-done.3 = f32[2,4,16,128]{3,2,1,0:T(8,128)S(1)} collective-permute-done((f32[2,4,16,128]{3,2,1,0:T(8,128)S(1)}, f32[2,4,16,128]{3,2,1,0:T(8,128)S(1)}, u32[]{:S(2)}, u32[]{:S(2)}) %collective-permute-start.3) | collective-permute-done | bytes 65568 | tf_op jit(solution)/shard_map/ppermute | solution.py:234
  14.1 0.1 collective-permute-start.4
  14.1 0.0 copy-done.4
  14.2 1.5 %collective-permute-done.4.other = f32[8,4,16,128]{3,2,1,0:T(8,128)S(1)} collective-permute-done((f32[8,4,16,128]{3,2,1,0:T(8,128)S(1)}, f32[8,4,16,128]{3,2,1,0:T(8,128)S(1)}, u32[]{:S(2)}, u32[]{:S(2)}) %collective-permute-start.4) | collective-permute-done | bytes 262176 | tf_op jit(solution)/shard_map/ppermute | solution.py:250
  15.7 0.0 copy-done.3
  15.7 0.1 broadcast_in_dim.6.chains_v
  15.7 0.1 broadcast_in_dim.7.mask_v
  15.8 0.0 copy-done
  15.8 0.0 copy-done.1
  15.8 0.0 copy-done.2
  15.8 0.6 %copy-done.5 = f32[128]{0:T(128)S(1)} copy-done((f32[128]{0:T(128)S(1)}, f32[128]{0:T(128)}, u32[]{:S(2)}) %copy-start.5) | copy-done | bytes 536
  16.5 4.9 %crop.1 = f32[4,16,128]{2,1,0:T(8,128)} custom-call(s32[32]{0:T(128)S(1)} %copy-done.3, s32[32]{0:T(128)S(1)} %copy-done.4, f32[8,4,16,128]{3,2,1,0:T(8,128)S(1)} %constant_dynamic-update-slice_fusion.mine, f32[8,4,16,128]{3,2,1,0:T(8,128)S(1)} %collective-permute-done.4.other, s32[32,128]{1,0:T(8,128)S(1)} %broadcast_in_dim.6.chains_v, ...), custom_call_target="tpu_custom_call" | custom-call | tf_op jit(solution)/shard_map/crop/pallas_call | solution.py:256
  (10 shorter events, 0.0 us)
Async XLA Ops:
  0.0 6.6 %copy-start.6 = (f32[4,16,128]{2,1,0:T(8,128)S(1)}, f32[4,16,128]{2,1,0:T(8,128)}, u32[]{:S(2)}) copy-start(f32[4,16,128]{2,1,0:T(8,128)} %param.7) | copy-start | bytes 98308
  0.0 6.6 %collective-permute-start = (f32[4,16,128]{2,1,0:T(8,128)}, f32[4,16,128]{2,1,0:T(8,128)S(1)}, u32[]{:S(2)}, u32[]{:S(2)}) collective-permute-start(f32[4,16,128]{2,1,0:T(8,128)} %param.7), channel_id=1, source_target_pairs={{0,8},{2,10},{4,12},{6,14},{8,0},{10,2},{12,4},{14,6},{1,9},{3,11}... | collective-permute-start | bytes 98312 | tf_op jit(solution)/shard_map/ppermute | solution.py:234
  6.6 9.2 %copy-start = (bf16[2,128,512]{2,1,0:T(8,128)(2,1)S(1)}, bf16[2,128,512]{2,1,0:T(8,128)(2,1)}, u32[]{:S(2)}) copy-start(bf16[2,128,512]{2,1,0:T(8,128)(2,1)} %proj_w.1) | copy-start | bytes 786436
  6.6 5.2 %collective-permute-start.1 = (f32[2,4,16,128]{3,2,1,0:T(8,128)S(1)}, f32[2,4,16,128]{3,2,1,0:T(8,128)S(1)}, u32[]{:S(2)}, u32[]{:S(2)}) collective-permute-start(f32[2,4,16,128]{3,2,1,0:T(8,128)S(1)} %pad_maximum_fusion), channel_id=1, source_target_pairs={{0,6},{2,4},{4,2},{6,0},{8,14},{10,12},{12,10},{14,8},{1,7},{3,5},... | collective-permute-start | bytes 196616 | tf_op jit(solution)/shard_map/ppermute | solution.py:234
  9.1 4.3 %collective-permute-start.2 = (f32[2,4,16,128]{3,2,1,0:T(8,128)S(1)}, f32[2,4,16,128]{3,2,1,0:T(8,128)S(1)}, u32[]{:S(2)}, u32[]{:S(2)}) collective-permute-start(f32[2,4,16,128]{3,2,1,0:T(8,128)S(1)} %pad_maximum_fusion), channel_id=1, source_target_pairs={{0,4},{2,6},{4,0},{6,2},{8,12},{10,14},{12,8},{14,10},{1,5},{3,7},... | collective-permute-start | bytes 196616 | tf_op jit(solution)/shard_map/ppermute | solution.py:234
  9.8 4.3 %collective-permute-start.3 = (f32[2,4,16,128]{3,2,1,0:T(8,128)S(1)}, f32[2,4,16,128]{3,2,1,0:T(8,128)S(1)}, u32[]{:S(2)}, u32[]{:S(2)}) collective-permute-start(f32[2,4,16,128]{3,2,1,0:T(8,128)S(1)} %pad_maximum_fusion), channel_id=1, source_target_pairs={{0,2},{2,0},{4,6},{6,4},{8,10},{10,8},{12,14},{14,12},{1,3},{3,1},... | collective-permute-start | bytes 196616 | tf_op jit(solution)/shard_map/ppermute | solution.py:234
  13.4 0.8 %copy-start.4 = (s32[32]{0:T(128)S(1)}, s32[32]{0:T(128)}, u32[]{:S(2)}) copy-start(s32[32]{0:T(128)} %mask_s.1) | copy-start | bytes 388
  13.4 2.4 %copy-start.1 = (bf16[2,128,128]{2,1,0:T(8,128)(2,1)S(1)}, bf16[2,128,128]{2,1,0:T(8,128)(2,1)}, u32[]{:S(2)}) copy-start(bf16[2,128,128]{2,1,0:T(8,128)(2,1)} %gate_w.1) | copy-start | bytes 196612
  13.4 2.4 %copy-start.2 = (bf16[2,128,128]{2,1,0:T(8,128)(2,1)S(1)}, bf16[2,128,128]{2,1,0:T(8,128)(2,1)}, u32[]{:S(2)}) copy-start(bf16[2,128,128]{2,1,0:T(8,128)(2,1)} %out_w.1) | copy-start | bytes 196612
  14.1 1.6 %copy-start.3 = (s32[32]{0:T(128)S(1)}, s32[32]{0:T(128)}, u32[]{:S(2)}) copy-start(s32[32]{0:T(128)} %chains_s.1) | copy-start | bytes 388
  14.1 1.6 %collective-permute-start.4 = (f32[8,4,16,128]{3,2,1,0:T(8,128)S(1)}, f32[8,4,16,128]{3,2,1,0:T(8,128)S(1)}, u32[]{:S(2)}, u32[]{:S(2)}) collective-permute-start(f32[8,4,16,128]{3,2,1,0:T(8,128)S(1)} %constant_dynamic-update-slice_fusion.mine), channel_id=1, source_target_pairs={{0,1},{1,0},{2,3},{3,2},{4,5},{5,4},{6,7},{7,6},{8,9},{9,8},{10,11... | collective-permute-start | bytes 786440 | tf_op jit(solution)/shard_map/ppermute | solution.py:250
  15.8 0.7 %copy-start.5 = (f32[128]{0:T(128)S(1)}, f32[128]{0:T(128)}, u32[]{:S(2)}) copy-start(f32[128]{0:T(128)} %param.10) | copy-start | bytes 1540

commit v4 on v3

--- a/solution.py
+++ b/solution.py
@@ -94,61 +94,111 @@
     return values.astype(jnp.bfloat16).astype(jnp.float32)
 
 
-def crop_kernel(
+def table(row, out):
+    tokens, width = out.shape
+    at = lax.broadcasted_iota(jnp.int32, (tokens, tokens), 0)
+    lane = lax.broadcasted_iota(jnp.int32, (tokens, tokens), 1)
+    spread = jnp.where(at == lane, jnp.broadcast_to(row[...].astype(jnp.float32), (tokens, tokens)), 0.0)
+    out[...] = jnp.broadcast_to(jnp.sum(spread, -1, keepdims=True), (tokens, width))
+
+
+def edges(masks, slots, half_start, source, chains, mask, bias, proj_w, gate_w, start, gates, left, right):
+    rows, cols, width = source.shape[-3:]
+    tokens = chains.shape[0]
+    me = lax.axis_index("row")
+    chunk = min(4, len(slots))
+    bias_v = bias[...]
+    hidden = proj_w.shape[2] // 4
+    half_start = pl.multiple_of(half_start, cols)
+    chain_cols = chains[pl.ds(half_start, cols), :]
+    mask_cols = mask[pl.ds(half_start, cols), :]
+    for at in range(0, len(slots), chunk):
+        base, chunk_slots = slots[at], slots[at : at + chunk]
+        states, pmasks = [], []
+        for slot in chunk_slots:
+            for t in range(rows):
+                token = (me ^ masks[slot]) * rows + t
+                same = chain_cols == chains[pl.ds(token, 1), :]
+                cell = source[slot, t] if len(source.shape) == 4 else source[t]
+                states.append(cell + jnp.where(same, bias_v, 0.0))
+                pmasks.append(mask_cols * mask[pl.ds(token, 1), :])
+        state = jnp.concatenate(states, 0)
+        pmask = jnp.concatenate(pmasks, 0)
+        count = len(chunk_slots) * rows
+        span = pl.ds(base * rows * cols, count * cols)
+        start[span, :] = state
+        normed = tile_norm(state).astype(jnp.bfloat16)
+        proj = dot(normed, proj_w[0])
+        gates[span, :] = dot(normed, gate_w[0])
+        left[span, :] = rounded(gate_of(proj[:, :hidden]) * proj[:, hidden : 2 * hidden] * pmask)
+        rgt = rounded(gate_of(proj[:, 2 * hidden : 3 * hidden]) * proj[:, 3 * hidden :] * pmask)
+        for n in range(count):
+            slot, t = divmod(base * rows + n, rows)
+            token = (me ^ masks[slot]) * rows + t
+            right[pl.ds(token, cols, tokens), :] = rgt[n * cols : (n + 1) * cols]
+
+
+def own_kernel(masks, *refs):
+    pair, chains_row, mask_row, bias, proj_w, gate_w, out_w = refs[:7]
+    bias_v, proj_v, gate_v, out_v, copied, chains, mask, start, gates, left, right, chains_v, mask_v, sems = refs[7:]
+    loads = [
+        pltpu.make_async_copy(source, target, sems.at[n])
+        for n, (source, target) in enumerate(
+            (
+                (pair, copied),
+                (chains_row, chains_v),
+                (mask_row, mask_v),
+                (bias, bias_v),
+                (proj_w, proj_v),
+                (gate_w, gate_v),
+                (out_w, out_v),
+            )
+        )
+    ]
+    for load in loads:
+        load.start()
+    for load in loads:
+        load.wait()
+    table(chains_v, chains)
+    table(mask_v, mask)
+    half_start = lax.axis_index("col") * copied.shape[1]
+    edges(masks, [0], half_start, copied, chains, mask, bias_v, proj_v, gate_v, start, gates, left, right)
+
+
+def mine_kernel(masks, mine, chains, mask, bias, proj_w, gate_w, s_in, g_in, l_in, r_in, start, gates, left, right):
+    half_start = lax.axis_index("col") * mine.shape[2]
+    slots = list(range(1, mine.shape[0]))
+    edges(masks, slots, half_start, mine, chains, mask, bias, proj_w, gate_w, start, gates, left, right)
+
+
+def second_kernel(
     masks,
-    chains_s,
-    mask_s,
-    mine,
     other,
-    chains_v,
-    mask_v,
+    chains,
+    mask,
     bias,
     proj_w,
     gate_w,
     out_w,
+    start_m,
+    gates_m,
+    left_m,
+    right_m,
     updated,
-    start,
-    left,
-    right,
-    gates,
+    start_o,
+    gates_o,
+    left_o,
+    right_o,
     tris,
     left1,
     right1,
 ):
-    ranks, rows, cols, width = mine.shape
+    ranks, rows, cols, width = other.shape
     tokens = ranks * rows
     me = lax.axis_index("row")
     col = lax.axis_index("col")
-    chunk = min(4, ranks)
-    bias_v = bias[...]
     hidden = proj_w.shape[2] // 4
-
-    for half, source in enumerate((mine, other)):
-        first = pl.multiple_of(jnp.where(col == half, 0, cols), cols)
-        chain_cols = chains_v[pl.ds(first, cols), :]
-        mask_cols = mask_v[pl.ds(first, cols), :]
-        for base in range(0, ranks, chunk):
-            states, pmasks = [], []
-            for slot in range(base, base + chunk):
-                for t in range(rows):
-                    token = (me ^ masks[slot]) * rows + t
-                    same = chain_cols == chains_s[token]
-                    states.append(source[slot, t] + jnp.where(same, bias_v, 0.0))
-                    pmasks.append(mask_cols * mask_s[token].astype(jnp.float32))
-            state = jnp.concatenate(states, 0)
-            pmask = jnp.concatenate(pmasks, 0)
-            start[half, pl.ds(base * rows * cols, chunk * rows * cols), :] = state
-            normed = tile_norm(state).astype(jnp.bfloat16)
-            proj = dot(normed, proj_w[0])
-            gates[half, pl.ds(base * rows * cols, chunk * rows * cols), :] = dot(normed, gate_w[0])
-            lft = rounded(gate_of(proj[:, :hidden]) * proj[:, hidden : 2 * hidden] * pmask)
-            rgt = rounded(gate_of(proj[:, 2 * hidden : 3 * hidden]) * proj[:, 3 * hidden :] * pmask)
-            for n in range(chunk * rows):
-                k = base * rows + n
-                left[pl.ds(k * tokens + half * cols, cols), :] = lft[n * cols : (n + 1) * cols]
-                slot, t = divmod(k, rows)
-                token = (me ^ masks[slot]) * rows + t
-                right[pl.ds(half * cols * tokens + token, cols, tokens), :] = rgt[n * cols : (n + 1) * cols]
+    edges(masks, list(range(ranks)), (1 - col) * cols, other, chains, mask, bias, proj_w, gate_w, start_o, gates_o, left_o, right_o)
 
     low = me * rows // 8 * 8
     groups = [col * cols + 8 * n for n in range(cols // 8)] + [low]
@@ -159,13 +209,14 @@
     def tri_block(step, carry):
         k0 = step * block
         acc = [[None] * count for _ in range(block)]
-        for l in range(tokens):
-            cells = [right[pl.ds(pl.multiple_of(l * tokens + g, 8), 8), :] for g in groups]
-            for k in range(block):
-                row = left[pl.ds((k0 + k) * tokens + l, 1), :]
-                for n in range(count):
-                    term = row * cells[n]
-                    acc[k][n] = term if l == 0 else acc[k][n] + term
+        for half, (left, right) in enumerate(((left_m, right_m), (left_o, right_o))):
+            for l in range(cols):
+                cells = [right[pl.ds(pl.multiple_of(l * tokens + g, 8), 8), :] for g in groups]
+                for k in range(block):
+                    row = left[pl.ds((k0 + k) * cols + l, 1), :]
+                    for n in range(count):
+                        term = row * cells[n]
+                        acc[k][n] = term if half + l == 0 else acc[k][n] + term
         for n in range(count):
             for k in range(block):
                 tris[n, pl.ds(pl.multiple_of((k0 + k) * 8, 8), 8), :] = acc[k][n]
@@ -173,27 +224,28 @@
 
     lax.fori_loop(0, tokens // block, tri_block, 0)
 
-    own_half = jnp.where(low // cols == col, 0, 1)
+    low_mine = low // cols == col
     low_off = lax.rem(low, cols)
-    mask_left = mask_v[pl.ds(pl.multiple_of(low, 8), 8), :]
-    mask_right = mask_v[pl.ds(pl.multiple_of(col * cols, cols), cols), :]
-
-    def gather(source, n, k):
+    mask_left = mask[pl.ds(pl.multiple_of(low, 8), 8), :]
+    mask_right = mask[pl.ds(pl.multiple_of(col * cols, cols), cols), :]
+
+    def gather(mine, other, n, k):
         if n < count - 1:
-            return source[0, pl.ds(k * cols + 8 * n, 8), :]
-        return source[own_half, pl.ds(pl.multiple_of(k * cols + low_off, 8), 8), :]
+            return mine[pl.ds(k * cols + 8 * n, 8), :]
+        span = pl.ds(pl.multiple_of(k * cols + low_off, 8), 8)
+        return jnp.where(low_mine, mine[span, :], other[span, :])
 
     def updated_state(n):
         tri = tris[n]
         tnorm = tile_norm(tri).astype(jnp.bfloat16)
-        gate = gate_of(jnp.concatenate([gather(gates, n, k) for k in range(tokens)], 0))
-        state = jnp.concatenate([gather(start, n, k) for k in range(tokens)], 0)
+        gate = gate_of(jnp.concatenate([gather(gates_m, gates_o, n, k) for k in range(tokens)], 0))
+        state = jnp.concatenate([gather(start_m, start_o, n, k) for k in range(tokens)], 0)
         return state + gate * dot(tnorm, out_w[0])
 
     row_masks = []
     for slot in range(ranks):
         for t in range(rows):
-            row_masks.append(mask_s[(me ^ masks[slot]) * rows + t].astype(jnp.float32))
+            row_masks.append(mask[pl.ds((me ^ masks[slot]) * rows + t, 1), :])
 
     normed = tile_norm(updated_state(count - 1)).astype(jnp.bfloat16)
     proj = dot(normed, proj_w[1, :, : 2 * hidden])
@@ -234,42 +286,74 @@
     return lax.ppermute(block, "row", [(i, i ^ bits) for i in range(ranks)])
 
 
+def call(body, inputs, outputs, scratch, name, flops, aliases={}, space=pltpu.VMEM):
+    return pl.pallas_call(
+        body,
+        out_shape=outputs,
+        in_specs=[pl.BlockSpec(memory_space=space)] * len(inputs),
+        out_specs=[pl.BlockSpec(memory_space=pltpu.VMEM)] * len(outputs),
+        scratch_shapes=scratch,
+        compiler_params=pltpu.CompilerParams(vmem_limit_bytes=32 << 20),
+        input_output_aliases=aliases,
+        cost_estimate=pl.CostEstimate(flops=flops, bytes_accessed=1 << 21, transcendentals=0),
+        name=name,
+    )(*inputs)
+
+
+def floats(*shapes):
+    return [jax.ShapeDtypeStruct(shape, jnp.float32) for shape in shapes]
+
+
+def like(*arrays):
+    return [jax.ShapeDtypeStruct(array.shape, array.dtype) for array in arrays]
+
+
 def whole_crop_plan(pair, token_mask, chains, chain_bias, proj_weight, gate_weight, out_weight):
     rows, cols, width = pair.shape
     ranks = lax.axis_size("row")
     tokens = token_mask.shape[0]
     hidden = proj_weight.shape[2] // 4
+    bias = chain_bias[None, :]
+    half = floats((tokens * cols, width), (tokens * cols, width), (tokens * cols, hidden), (tokens * cols, hidden))
+    flops = 2 * tokens * cols * width * 5 * hidden
     top = ranks // 2
-    two = jnp.stack([pair, exchange(pair, top)])
     masks = [0, top]
-    parts = [two]
-    for bits in list(range(top - 1, 0, -1)):
-        parts.append(exchange(two, bits))
+    for bits in range(top - 1, 0, -1):
         masks += [bits, bits ^ top]
-    mine = jnp.concatenate(parts, 0)
+    far = exchange(pair, top)
+    own_inputs = (pair, chains[None, :], token_mask[None, :], bias, proj_weight, gate_weight, out_weight)
+    own_inputs = [pltpu.with_memory_space_constraint(each, pltpu.HBM) for each in own_inputs]
+    bias, proj_weight, gate_weight, out_weight, own, chains_t, mask_t, *partial = call(
+        functools.partial(own_kernel, masks),
+        own_inputs,
+        like(bias, proj_weight, gate_weight, out_weight, pair) + floats((tokens, width), (tokens, width)) + half,
+        [pltpu.VMEM((1, tokens), jnp.int32), pltpu.VMEM((1, tokens), jnp.int32), pltpu.SemaphoreType.DMA((7,))],
+        "own",
+        flops // ranks,
+        space=pltpu.HBM,
+    )
+    two = jnp.stack([own, far])
+    mine = jnp.concatenate([two] + [exchange(two, bits) for bits in range(top - 1, 0, -1)], 0)
     other = lax.ppermute(mine, "col", [(0, 1), (1, 0)])
-    chains_v = jnp.broadcast_to(chains[:, None], (tokens, width))
-    mask_v = jnp.broadcast_to(token_mask.astype(jnp.float32)[:, None], (tokens, width))
+    mine_edges = call(
+        functools.partial(mine_kernel, masks),
+        (mine, chains_t, mask_t, bias, proj_weight, gate_weight, *partial),
+        half,
+        [],
+        "mine",
+        flops,
+        {6: 0, 7: 1, 8: 2, 9: 3},
+    )
     groups = cols // 8 + 1
-    smem = pl.BlockSpec(memory_space=pltpu.SMEM)
-    vmem = pl.BlockSpec(memory_space=pltpu.VMEM)
-    return pl.pallas_call(
-        functools.partial(crop_kernel, masks),
-        out_shape=jax.ShapeDtypeStruct(pair.shape, jnp.float32),
-        in_specs=[smem, smem] + [vmem] * 8,
-        out_specs=vmem,
-        scratch_shapes=[
-            pltpu.VMEM((2, tokens * cols, width), jnp.float32),
-            pltpu.VMEM((tokens * tokens, hidden), jnp.float32),
-            pltpu.VMEM((tokens * tokens, hidden), jnp.float32),
-            pltpu.VMEM((2, tokens * cols, width), jnp.float32),
-            pltpu.VMEM((groups, tokens * 8, hidden), jnp.float32),
-            pltpu.VMEM((tokens * 8, hidden), jnp.float32),
-            pltpu.VMEM((groups - 1, tokens * 8, hidden), jnp.float32),
-        ],
-        compiler_params=pltpu.CompilerParams(vmem_limit_bytes=32 << 20),
-        name="crop",
-    )(chains, token_mask, mine, other, chains_v, mask_v, chain_bias[None, :], proj_weight, gate_weight, out_weight)
+    extra = [(groups, tokens * 8, hidden), (tokens * 8, hidden), (groups - 1, tokens * 8, hidden)]
+    return call(
+        functools.partial(second_kernel, masks),
+        (other, chains_t, mask_t, bias, proj_weight, gate_weight, out_weight, *mine_edges),
+        floats(pair.shape),
+        [pltpu.VMEM(each.shape, jnp.float32) for each in half + floats(*extra)],
+        "crop",
+        4 * flops,
+    )[0]
 
 
 def shards(pair, token_mask, *rest):

time: 21.6 us -> 20.5 us (0.949)
  local copies, waits for them, and re-layouts: 1.63 us -> 0.03 us
  Pallas kernels: 4.9 us -> 6.15 us
  waiting for transfers between devices: 7.1 us -> 6.5 us
    unnamed x18 -> x4, local copies, waits for them, and re-layouts: 1.48 us -> 0.02 us
    pallas_call x1 -> x3, Pallas kernels: 4.9 us -> 6.15 us  [call(): pl.pallas_call(body, out_shape=outputs, in_specs=[pl.BlockSpec(memory_spa...]
    ppermute x1, waiting for transfers between devices: 1.5 us -> 0.82 us  [whole_crop_plan(): other = lax.ppermute(mine, 'col', [(0, 1), (1, 0)])]
  transfers between devices with their start and end apart: 5 -> 5, of which waited for: 5 -> 3; matrix products, arithmetic and copies ran while one was open for 4% -> 0% of each run, Pallas kernels for 0% -> 11%
where the time goes in v4:
time: 20.5 us; the launch traced here: 20.3 us
  starting transfers between devices  7.6 us (37%)
  waiting for transfers between devices  6.5 us (32%)
  Pallas kernels  6.15 us (30%)
    ppermute x4, starting transfers between devices, exchange(): return lax.ppermute(block, 'row', [(i, i ^ bits) for i in range(ranks)])  7.52 us
    pallas_call x3, Pallas kernels, call(): pl.pallas_call(body, out_shape=outputs, in_specs=[pl.BlockSpec(memory_spa...  6.15 us
    ppermute x4, waiting for transfers between devices, exchange(): return lax.ppermute(block, 'row', [(i, i ^ bits) for i in range(ranks)])  5.68 us
    ppermute x1, waiting for transfers between devices, whole_crop_plan(): other = lax.ppermute(mine, 'col', [(0, 1), (1, 0)])  0.82 us
  transfers between devices with their start and end apart: 5, of which 3 were waited for; matrix products, arithmetic and copies ran while one was open for 0% of the time, Pallas kernels for 11%

profile of v4, /device:TPU:0, one launch (start us, length us, event | category | flops | bytes accessed | tf_op | source)
XLA Modules:
  0.0 20.3 jit_solution(15912393379805797549)
XLA Ops:
  0.0 4.0 %collective-permute-start = (f32[4,16,128]{2,1,0:T(8,128)}, f32[4,16,128]{2,1,0:T(8,128)S(1)}, u32[]{:S(2)}, u32[]{:S(2)}) collective-permute-start(f32[4,16,128]{2,1,0:T(8,128)} %refs_0_.1), channel_id=1, source_target_pairs={{0,8},{2,10},{4,12},{6,14},{8,0},{10,2},{12,4},{14,6},{1,9},{3,11}... | collective-permute-start | bytes 98312 | tf_op jit(solution)/shard_map/ppermute | solution.py:286
  4.0 1.5 %own.1 = (f32[1,128]{1,0:T(1,128)S(1)}, bf16[2,128,512]{2,1,0:T(8,128)(2,1)S(1)}, bf16[2,128,128]{2,1,0:T(8,128)(2,1)S(1)}, bf16[2,128,128]{2,1,0:T(8,128)(2,1)S...) custom-call(f32[4,16,128]{2,1,0:T(8,128)} %refs_0_.1, ...), custom_call_target="tpu_custom_call" | custom-call | flops 10485760 | bytes 2097152 | tf_op jit(solution)/shard_map/own/pallas_call | solution.py:290
  5.6 0.9 %collective-permute-done = f32[4,16,128]{2,1,0:T(8,128)S(1)} collective-permute-done((f32[4,16,128]{2,1,0:T(8,128)}, f32[4,16,128]{2,1,0:T(8,128)S(1)}, u32[]{:S(2)}, u32[]{:S(2)}) %collective-permute-start) | collective-permute-done | bytes 32800 | tf_op jit(solution)/shard_map/ppermute | solution.py:286
  6.5 1.7 %collective-permute-start.3 = (f32[2,4,16,128]{3,2,1,0:T(8,128)S(1)}, f32[2,4,16,128]{3,2,1,0:T(8,128)S(1)}, u32[]{:S(2)}, u32[]{:S(2)}) collective-permute-start(f32[2,4,16,128]{3,2,1,0:T(8,128)S(1)} %pad_maximum_fusion), channel_id=1, source_target_pairs={{0,2},{2,0},{4,6},{6,4},{8,10},{10,8},{12,14},{14,12},{1,3},{3,1},... | collective-permute-start | bytes 196616 | tf_op jit(solution)/shard_map/ppermute | solution.py:286
  8.2 1.3 %collective-permute-start.2 = (f32[2,4,16,128]{3,2,1,0:T(8,128)S(1)}, f32[2,4,16,128]{3,2,1,0:T(8,128)S(1)}, u32[]{:S(2)}, u32[]{:S(2)}) collective-permute-start(f32[2,4,16,128]{3,2,1,0:T(8,128)S(1)} %pad_maximum_fusion), channel_id=1, source_target_pairs={{0,4},{2,6},{4,0},{6,2},{8,12},{10,14},{12,8},{14,10},{1,5},{3,7},... | collective-permute-start | bytes 196616 | tf_op jit(solution)/shard_map/ppermute | solution.py:286
  9.6 0.4 %collective-permute-start.1 = (f32[2,4,16,128]{3,2,1,0:T(8,128)S(1)}, f32[2,4,16,128]{3,2,1,0:T(8,128)S(1)}, u32[]{:S(2)}, u32[]{:S(2)}) collective-permute-start(f32[2,4,16,128]{3,2,1,0:T(8,128)S(1)} %pad_maximum_fusion), channel_id=1, source_target_pairs={{0,6},{2,4},{4,2},{6,0},{8,14},{10,12},{12,10},{14,8},{1,7},{3,5},... | collective-permute-start | bytes 196616 | tf_op jit(solution)/shard_map/ppermute | solution.py:286
  10.0 4.8 %collective-permute-done.1 = f32[2,4,16,128]{3,2,1,0:T(8,128)S(1)} collective-permute-done((f32[2,4,16,128]{3,2,1,0:T(8,128)S(1)}, f32[2,4,16,128]{3,2,1,0:T(8,128)S(1)}, u32[]{:S(2)}, u32[]{:S(2)}) %collective-permute-start.1) | collective-permute-done | bytes 65568 | tf_op jit(solution)/shard_map/ppermute | solution.py:286
  14.7 0.0 collective-permute-done.2
  14.8 0.0 collective-permute-done.3
  14.8 0.1 collective-permute-start.4
  14.9 0.7 %mine.1 = (f32[512,128]{1,0:T(8,128)S(1)}, f32[512,128]{1,0:T(8,128)S(1)}, f32[512,128]{1,0:T(8,128)S(1)}, f32[512,128]{1,0:T(8,128)S(1)}) custom-call(f32[8,4,16,128]{3,2,1,0:T(8,128)S(1)} %constant_dynamic-update-slice_fusion.mine, ...), custom_call_target="tpu_custom_call", output_to_operand_aliasing={{0}: (6, {}), {1}: (7, {}), {2}: (8, {}), {3}: (9, {})} | custom-call | flops 83886080 | bytes 2097152 | tf_op jit(solution)/shard_map/mine/pallas_call | solution.py:290
  15.6 0.8 %collective-permute-done.4.other = f32[8,4,16,128]{3,2,1,0:T(8,128)S(1)} collective-permute-done((f32[8,4,16,128]{3,2,1,0:T(8,128)S(1)}, f32[8,4,16,128]{3,2,1,0:T(8,128)S(1)}, u32[]{:S(2)}, u32[]{:S(2)}) %collective-permute-start.4) | collective-permute-done | bytes 262176 | tf_op jit(solution)/shard_map/ppermute | solution.py:337
  16.4 3.9 %crop.1 = f32[4,16,128]{2,1,0:T(8,128)} custom-call(f32[8,4,16,128]{3,2,1,0:T(8,128)S(1)} %collective-permute-done.4.other, f32[32,128]{1,0:T(8,128)S(1)} %get-tuple-element.21.chains, f32[32,128]{1,0:T(8,128)S(1)} %get-tuple-element.22.mask, f32[1,128]{1,0:T(1,128)S(1)} %get-tuple-element.23.bias, bf16[2,128,512]{2,1,0:T(8,128)(2,1)S(1)} %get-tuple-element.24.proj_w, ...), custom_call_target="tpu_custom_call" | custom-call | flops 335544320 | bytes 2097152 | tf_op jit(solution)/shard_map/crop/pallas_call | solution.py:290
  (6 shorter events, 0.0 us)
Async XLA Ops:
  0.0 6.5 %collective-permute-start = (f32[4,16,128]{2,1,0:T(8,128)}, f32[4,16,128]{2,1,0:T(8,128)S(1)}, u32[]{:S(2)}, u32[]{:S(2)}) collective-permute-start(f32[4,16,128]{2,1,0:T(8,128)} %refs_0_.1), channel_id=1, source_target_pairs={{0,8},{2,10},{4,12},{6,14},{8,0},{10,2},{12,4},{14,6},{1,9},{3,11}... | collective-permute-start | bytes 98312 | tf_op jit(solution)/shard_map/ppermute | solution.py:286
  6.5 8.3 %collective-permute-start.3 = (f32[2,4,16,128]{3,2,1,0:T(8,128)S(1)}, f32[2,4,16,128]{3,2,1,0:T(8,128)S(1)}, u32[]{:S(2)}, u32[]{:S(2)}) collective-permute-start(f32[2,4,16,128]{3,2,1,0:T(8,128)S(1)} %pad_maximum_fusion), channel_id=1, source_target_pairs={{0,2},{2,0},{4,6},{6,4},{8,10},{10,8},{12,14},{14,12},{1,3},{3,1},... | collective-permute-start | bytes 196616 | tf_op jit(solution)/shard_map/ppermute | solution.py:286
  8.2 6.5 %collective-permute-start.2 = (f32[2,4,16,128]{3,2,1,0:T(8,128)S(1)}, f32[2,4,16,128]{3,2,1,0:T(8,128)S(1)}, u32[]{:S(2)}, u32[]{:S(2)}) collective-permute-start(f32[2,4,16,128]{3,2,1,0:T(8,128)S(1)} %pad_maximum_fusion), channel_id=1, source_target_pairs={{0,4},{2,6},{4,0},{6,2},{8,12},{10,14},{12,8},{14,10},{1,5},{3,7},... | collective-permute-start | bytes 196616 | tf_op jit(solution)/shard_map/ppermute | solution.py:286
  9.6 5.2 %collective-permute-start.1 = (f32[2,4,16,128]{3,2,1,0:T(8,128)S(1)}, f32[2,4,16,128]{3,2,1,0:T(8,128)S(1)}, u32[]{:S(2)}, u32[]{:S(2)}) collective-permute-start(f32[2,4,16,128]{3,2,1,0:T(8,128)S(1)} %pad_maximum_fusion), channel_id=1, source_target_pairs={{0,6},{2,4},{4,2},{6,0},{8,14},{10,12},{12,10},{14,8},{1,7},{3,5},... | collective-permute-start | bytes 196616 | tf_op jit(solution)/shard_map/ppermute | solution.py:286
  14.8 1.6 %collective-permute-start.4 = (f32[8,4,16,128]{3,2,1,0:T(8,128)S(1)}, f32[8,4,16,128]{3,2,1,0:T(8,128)S(1)}, u32[]{:S(2)}, u32[]{:S(2)}) collective-permute-start(f32[8,4,16,128]{3,2,1,0:T(8,128)S(1)} %constant_dynamic-update-slice_fusion.mine), channel_id=1, source_target_pairs={{0,1},{1,0},{2,3},{3,2},{4,5},{5,4},{6,7},{7,6},{8,9},{9,8},{10,11... | collective-permute-start | bytes 786440 | tf_op jit(solution)/shard_map/ppermute | solution.py:337

commit v5 on v4

--- a/solution.py
+++ b/solution.py
@@ -316,11 +316,7 @@
     bias = chain_bias[None, :]
     half = floats((tokens * cols, width), (tokens * cols, width), (tokens * cols, hidden), (tokens * cols, hidden))
     flops = 2 * tokens * cols * width * 5 * hidden
-    top = ranks // 2
-    masks = [0, top]
-    for bits in range(top - 1, 0, -1):
-        masks += [bits, bits ^ top]
-    far = exchange(pair, top)
+    masks = [0] + sorted(range(1, ranks), key=lambda bits: -(bits ^ bits >> 1))
     own_inputs = (pair, chains[None, :], token_mask[None, :], bias, proj_weight, gate_weight, out_weight)
     own_inputs = [pltpu.with_memory_space_constraint(each, pltpu.HBM) for each in own_inputs]
     bias, proj_weight, gate_weight, out_weight, own, chains_t, mask_t, *partial = call(
@@ -332,8 +328,7 @@
         flops // ranks,
         space=pltpu.HBM,
     )
-    two = jnp.stack([own, far])
-    mine = jnp.concatenate([two] + [exchange(two, bits) for bits in range(top - 1, 0, -1)], 0)
+    mine = jnp.stack([own] + [exchange(pair, bits) for bits in masks[1:]])
     other = lax.ppermute(mine, "col", [(0, 1), (1, 0)])
     mine_edges = call(
         functools.partial(mine_kernel, masks),

time: 20.5 us -> 25.8 us (1.26)
  starting transfers between devices: 7.6 us -> 14.5 us
  waiting for transfers between devices: 6.5 us -> 4.97 us
    ppermute x4 -> x7, starting transfers between devices: 7.52 us -> 14.4 us  [exchange(): return lax.ppermute(block, 'row', [(i, i ^ bits) for i in range(ranks)])]
    ppermute x4 -> x7, waiting for transfers between devices: 5.68 us -> 4.15 us  [exchange(): return lax.ppermute(block, 'row', [(i, i ^ bits) for i in range(ranks)])]
  transfers between devices with their start and end apart: 5 -> 8, of which waited for: 3 -> 3; matrix products, arithmetic and copies ran while one was open for 0% -> 0% of each run, Pallas kernels for 11% -> 9%
where the time goes in v5:
time: 25.8 us; the launch traced here: 25.7 us
  starting transfers between devices  14.5 us (56%)
  Pallas kernels  6.14 us (24%)
  waiting for transfers between devices  4.97 us (19%)
    ppermute x7, starting transfers between devices, exchange(): return lax.ppermute(block, 'row', [(i, i ^ bits) for i in range(ranks)])  14.4 us
    pallas_call x3, Pallas kernels, call(): pl.pallas_call(body, out_shape=outputs, in_specs=[pl.BlockSpec(memory_spa...  6.14 us
    ppermute x7, waiting for transfers between devices, exchange(): return lax.ppermute(block, 'row', [(i, i ^ bits) for i in range(ranks)])  4.15 us
    ppermute x1, waiting for transfers between devices, whole_crop_plan(): other = lax.ppermute(mine, 'col', [(0, 1), (1, 0)])  0.82 us
  transfers between devices with their start and end apart: 8, of which 3 were waited for; matrix products, arithmetic and copies ran while one was open for 0% of the time, Pallas kernels for 9%

profile of v5, /device:TPU:0, one launch (start us, length us, event | category | flops | bytes accessed | tf_op | source)
XLA Modules:
  0.0 25.7 jit_solution(8204866414789096326)
XLA Ops:
  0.0 3.0 %collective-permute-start.4 = (f32[4,16,128]{2,1,0:T(8,128)}, f32[4,16,128]{2,1,0:T(8,128)S(1)}, u32[]{:S(2)}, u32[]{:S(2)}) collective-permute-start(f32[4,16,128]{2,1,0:T(8,128)} %refs_0_.1), channel_id=1, source_target_pairs={{0,4},{2,6},{4,0},{6,2},{8,12},{10,14},{12,8},{14,10},{1,5},{3,7},... | collective-permute-start | bytes 98312 | tf_op jit(solution)/shard_map/ppermute | solution.py:286
  3.0 3.4 %collective-permute-start.3 = (f32[4,16,128]{2,1,0:T(8,128)}, f32[4,16,128]{2,1,0:T(8,128)S(1)}, u32[]{:S(2)}, u32[]{:S(2)}) collective-permute-start(f32[4,16,128]{2,1,0:T(8,128)} %refs_0_.1), channel_id=1, source_target_pairs={{0,14},{2,12},{4,10},{6,8},{8,6},{10,4},{12,2},{14,0},{1,15},{3,13... | collective-permute-start | bytes 98312 | tf_op jit(solution)/shard_map/ppermute | solution.py:286
  6.5 1.3 %collective-permute-start.2 = (f32[4,16,128]{2,1,0:T(8,128)}, f32[4,16,128]{2,1,0:T(8,128)S(1)}, u32[]{:S(2)}, u32[]{:S(2)}) collective-permute-start(f32[4,16,128]{2,1,0:T(8,128)} %refs_0_.1), channel_id=1, source_target_pairs={{0,12},{2,14},{4,8},{6,10},{8,4},{10,6},{12,0},{14,2},{1,13},{3,15... | collective-permute-start | bytes 98312 | tf_op jit(solution)/shard_map/ppermute | solution.py:286
  7.8 0.8 %collective-permute-start.1 = (f32[4,16,128]{2,1,0:T(8,128)}, f32[4,16,128]{2,1,0:T(8,128)S(1)}, u32[]{:S(2)}, u32[]{:S(2)}) collective-permute-start(f32[4,16,128]{2,1,0:T(8,128)} %refs_0_.1), channel_id=1, source_target_pairs={{0,8},{2,10},{4,12},{6,14},{8,0},{10,2},{12,4},{14,6},{1,9},{3,11}... | collective-permute-start | bytes 98312 | tf_op jit(solution)/shard_map/ppermute | solution.py:286
  8.6 2.1 %collective-permute-start = (f32[4,16,128]{2,1,0:T(8,128)}, f32[4,16,128]{2,1,0:T(8,128)S(1)}, u32[]{:S(2)}, u32[]{:S(2)}) collective-permute-start(f32[4,16,128]{2,1,0:T(8,128)} %refs_0_.1), channel_id=1, source_target_pairs={{0,10},{2,8},{4,14},{6,12},{8,2},{10,0},{12,6},{14,4},{1,11},{3,9}... | collective-permute-start | bytes 98312 | tf_op jit(solution)/shard_map/ppermute | solution.py:286
  10.7 1.5 %own.1 = (f32[1,128]{1,0:T(1,128)S(1)}, bf16[2,128,512]{2,1,0:T(8,128)(2,1)S(1)}, bf16[2,128,128]{2,1,0:T(8,128)(2,1)S(1)}, bf16[2,128,128]{2,1,0:T(8,128)(2,1)S...) custom-call(f32[4,16,128]{2,1,0:T(8,128)} %refs_0_.1, ...), custom_call_target="tpu_custom_call" | custom-call | flops 10485760 | bytes 2097152 | tf_op jit(solution)/shard_map/own/pallas_call | solution.py:290
  12.2 0.0 copy-start
  12.2 2.3 %collective-permute-done = f32[4,16,128]{2,1,0:T(8,128)S(1)} collective-permute-done((f32[4,16,128]{2,1,0:T(8,128)}, f32[4,16,128]{2,1,0:T(8,128)S(1)}, u32[]{:S(2)}, u32[]{:S(2)}) %collective-permute-start) | collective-permute-done | bytes 32800 | tf_op jit(solution)/shard_map/ppermute | solution.py:286
  14.5 0.0 copy-done
  14.5 0.8 %collective-permute-start.6 = (f32[4,16,128]{2,1,0:T(8,128)S(1)}, f32[4,16,128]{2,1,0:T(8,128)S(1)}, u32[]{:S(2)}, u32[]{:S(2)}) collective-permute-start(f32[4,16,128]{2,1,0:T(8,128)S(1)} %copy-done), channel_id=1, source_target_pairs={{0,2},{2,0},{4,6},{6,4},{8,10},{10,8},{12,14},{14,12},{1,3},{3,1},... | collective-permute-start | bytes 98312 | tf_op jit(solution)/shard_map/ppermute | solution.py:286
  15.3 0.0 collective-permute-done.1
  15.3 2.9 %collective-permute-start.5 = (f32[4,16,128]{2,1,0:T(8,128)S(1)}, f32[4,16,128]{2,1,0:T(8,128)S(1)}, u32[]{:S(2)}, u32[]{:S(2)}) collective-permute-start(f32[4,16,128]{2,1,0:T(8,128)S(1)} %copy-done), channel_id=1, source_target_pairs={{0,6},{2,4},{4,2},{6,0},{8,14},{10,12},{12,10},{14,8},{1,7},{3,5},... | collective-permute-start | bytes 98312 | tf_op jit(solution)/shard_map/ppermute | solution.py:286
  18.2 0.0 collective-permute-done.2
  18.3 0.0 collective-permute-done.3
  18.3 0.0 collective-permute-done.4
  18.3 1.8 %collective-permute-done.5 = f32[4,16,128]{2,1,0:T(8,128)S(1)} collective-permute-done((f32[4,16,128]{2,1,0:T(8,128)S(1)}, f32[4,16,128]{2,1,0:T(8,128)S(1)}, u32[]{:S(2)}, u32[]{:S(2)}) %collective-permute-start.5) | collective-permute-done | bytes 32800 | tf_op jit(solution)/shard_map/ppermute | solution.py:286
  20.1 0.0 collective-permute-done.6
  20.2 0.1 collective-permute-start.7
  20.2 0.7 %mine.1 = (f32[512,128]{1,0:T(8,128)S(1)}, f32[512,128]{1,0:T(8,128)S(1)}, f32[512,128]{1,0:T(8,128)S(1)}, f32[512,128]{1,0:T(8,128)S(1)}) custom-call(f32[8,4,16,128]{3,2,1,0:T(8,128)S(1)} %bitcast_dynamic-update-slice_fusion.mine, f32[32,128]{1,0:T(8,128)S(1)} %get-tuple-element.21.chains, ...), custom_call_target="tpu_custom_call", output_to_operand_aliasing={{0}: (6, {}), {1}: (7, {}), {2}: (8, {}), {3}: (9, {})} | custom-call | flops 83886080 | bytes 2097152 | tf_op jit(solution)/shard_map/mine/pallas_call | solution.py:290
  20.9 0.8 %collective-permute-done.7.other = f32[8,4,16,128]{3,2,1,0:T(8,128)S(1)} collective-permute-done((f32[8,4,16,128]{3,2,1,0:T(8,128)S(1)}, f32[8,4,16,128]{3,2,1,0:T(8,128)S(1)}, u32[]{:S(2)}, u32[]{:S(2)}) %collective-permute-start.7) | collective-permute-done | bytes 262176 | tf_op jit(solution)/shard_map/ppermute | solution.py:332
  21.8 3.9 %crop.1 = f32[4,16,128]{2,1,0:T(8,128)} custom-call(f32[8,4,16,128]{3,2,1,0:T(8,128)S(1)} %collective-permute-done.7.other, f32[32,128]{1,0:T(8,128)S(1)} %get-tuple-element.21.chains, f32[32,128]{1,0:T(8,128)S(1)} %get-tuple-element.22.mask, f32[1,128]{1,0:T(1,128)S(1)} %get-tuple-element.23.bias, bf16[2,128,512]{2,1,0:T(8,128)(2,1)S(1)} %get-tuple-element.24.proj_w, ...), custom_call_target="tpu_custom_call" | custom-call | flops 335544320 | bytes 2097152 | tf_op jit(solution)/shard_map/crop/pallas_call | solution.py:290
  (8 shorter events, 0.0 us)
Async XLA Ops:
  0.0 18.3 %collective-permute-start.4 = (f32[4,16,128]{2,1,0:T(8,128)}, f32[4,16,128]{2,1,0:T(8,128)S(1)}, u32[]{:S(2)}, u32[]{:S(2)}) collective-permute-start(f32[4,16,128]{2,1,0:T(8,128)} %refs_0_.1), channel_id=1, source_target_pairs={{0,4},{2,6},{4,0},{6,2},{8,12},{10,14},{12,8},{14,10},{1,5},{3,7},... | collective-permute-start | bytes 98312 | tf_op jit(solution)/shard_map/ppermute | solution.py:286
  3.0 15.2 %collective-permute-start.3 = (f32[4,16,128]{2,1,0:T(8,128)}, f32[4,16,128]{2,1,0:T(8,128)S(1)}, u32[]{:S(2)}, u32[]{:S(2)}) collective-permute-start(f32[4,16,128]{2,1,0:T(8,128)} %refs_0_.1), channel_id=1, source_target_pairs={{0,14},{2,12},{4,10},{6,8},{8,6},{10,4},{12,2},{14,0},{1,15},{3,13... | collective-permute-start | bytes 98312 | tf_op jit(solution)/shard_map/ppermute | solution.py:286
  6.5 11.8 %collective-permute-start.2 = (f32[4,16,128]{2,1,0:T(8,128)}, f32[4,16,128]{2,1,0:T(8,128)S(1)}, u32[]{:S(2)}, u32[]{:S(2)}) collective-permute-start(f32[4,16,128]{2,1,0:T(8,128)} %refs_0_.1), channel_id=1, source_target_pairs={{0,12},{2,14},{4,8},{6,10},{8,4},{10,6},{12,0},{14,2},{1,13},{3,15... | collective-permute-start | bytes 98312 | tf_op jit(solution)/shard_map/ppermute | solution.py:286
  7.8 7.5 %collective-permute-start.1 = (f32[4,16,128]{2,1,0:T(8,128)}, f32[4,16,128]{2,1,0:T(8,128)S(1)}, u32[]{:S(2)}, u32[]{:S(2)}) collective-permute-start(f32[4,16,128]{2,1,0:T(8,128)} %refs_0_.1), channel_id=1, source_target_pairs={{0,8},{2,10},{4,12},{6,14},{8,0},{10,2},{12,4},{14,6},{1,9},{3,11}... | collective-permute-start | bytes 98312 | tf_op jit(solution)/shard_map/ppermute | solution.py:286
  8.6 5.9 %collective-permute-start = (f32[4,16,128]{2,1,0:T(8,128)}, f32[4,16,128]{2,1,0:T(8,128)S(1)}, u32[]{:S(2)}, u32[]{:S(2)}) collective-permute-start(f32[4,16,128]{2,1,0:T(8,128)} %refs_0_.1), channel_id=1, source_target_pairs={{0,10},{2,8},{4,14},{6,12},{8,2},{10,0},{12,6},{14,4},{1,11},{3,9}... | collective-permute-start | bytes 98312 | tf_op jit(solution)/shard_map/ppermute | solution.py:286
  12.2 2.3 %copy-start = (f32[4,16,128]{2,1,0:T(8,128)S(1)}, f32[4,16,128]{2,1,0:T(8,128)}, u32[]{:S(2)}) copy-start(f32[4,16,128]{2,1,0:T(8,128)} %refs_0_.1) | copy-start | bytes 98308
  14.5 5.6 %collective-permute-start.6 = (f32[4,16,128]{2,1,0:T(8,128)S(1)}, f32[4,16,128]{2,1,0:T(8,128)S(1)}, u32[]{:S(2)}, u32[]{:S(2)}) collective-permute-start(f32[4,16,128]{2,1,0:T(8,128)S(1)} %copy-done), channel_id=1, source_target_pairs={{0,2},{2,0},{4,6},{6,4},{8,10},{10,8},{12,14},{14,12},{1,3},{3,1},... | collective-permute-start | bytes 98312 | tf_op jit(solution)/shard_map/ppermute | solution.py:286
  15.3 4.8 %collective-permute-start.5 = (f32[4,16,128]{2,1,0:T(8,128)S(1)}, f32[4,16,128]{2,1,0:T(8,128)S(1)}, u32[]{:S(2)}, u32[]{:S(2)}) collective-permute-start(f32[4,16,128]{2,1,0:T(8,128)S(1)} %copy-done), channel_id=1, source_target_pairs={{0,6},{2,4},{4,2},{6,0},{8,14},{10,12},{12,10},{14,8},{1,7},{3,5},... | collective-permute-start | bytes 98312 | tf_op jit(solution)/shard_map/ppermute | solution.py:286
  20.2 1.6 %collective-permute-start.7 = (f32[8,4,16,128]{3,2,1,0:T(8,128)S(1)}, f32[8,4,16,128]{3,2,1,0:T(8,128)S(1)}, u32[]{:S(2)}, u32[]{:S(2)}) collective-permute-start(f32[8,4,16,128]{3,2,1,0:T(8,128)S(1)} %bitcast_dynamic-update-slice_fusion.mine), channel_id=1, source_target_pairs={{0,1},{1,0},{2,3},{3,2},{4,5},{5,4},{6,7},{7,6},{8,9},{9,8},{10,11... | collective-permute-start | bytes 786440 | tf_op jit(solution)/shard_map/ppermute | solution.py:332

commit v6 on v5

--- a/solution.py
+++ b/solution.py
@@ -102,103 +102,103 @@
     out[...] = jnp.broadcast_to(jnp.sum(spread, -1, keepdims=True), (tokens, width))
 
 
-def edges(masks, slots, half_start, source, chains, mask, bias, proj_w, gate_w, start, gates, left, right):
-    rows, cols, width = source.shape[-3:]
+def pick(pair):
+    return jnp.where(lax.axis_index("col") == 0, *pair)
+
+
+def edges(masks, slots, halves, source, chains, mask, bias, proj_w, gate_w, start, gates, left, right):
+    rows, cols, width = source(slots[0], 0).shape
     tokens = chains.shape[0]
     me = lax.axis_index("row")
-    chunk = min(4, len(slots))
     bias_v = bias[...]
     hidden = proj_w.shape[2] // 4
-    half_start = pl.multiple_of(half_start, cols)
-    chain_cols = chains[pl.ds(half_start, cols), :]
-    mask_cols = mask[pl.ds(half_start, cols), :]
-    for at in range(0, len(slots), chunk):
-        base, chunk_slots = slots[at], slots[at : at + chunk]
+    for h in halves:
+        col = lax.axis_index("col")
+        first = pl.multiple_of((col if h == 0 else 1 - col) * cols, cols)
+        chain_cols = chains[pl.ds(first, cols), :]
+        mask_cols = mask[pl.ds(first, cols), :]
         states, pmasks = [], []
-        for slot in chunk_slots:
+        for slot in slots:
+            block = source(slot, h)
             for t in range(rows):
-                token = (me ^ masks[slot]) * rows + t
+                token = (me ^ pick(masks[slot])) * rows + t
                 same = chain_cols == chains[pl.ds(token, 1), :]
-                cell = source[slot, t] if len(source.shape) == 4 else source[t]
-                states.append(cell + jnp.where(same, bias_v, 0.0))
+                states.append(block[t] + jnp.where(same, bias_v, 0.0))
                 pmasks.append(mask_cols * mask[pl.ds(token, 1), :])
         state = jnp.concatenate(states, 0)
         pmask = jnp.concatenate(pmasks, 0)
-        count = len(chunk_slots) * rows
-        span = pl.ds(base * rows * cols, count * cols)
-        start[span, :] = state
+        count = len(slots) * rows
+        span = pl.ds(slots[0] * rows * cols, count * cols)
+        start[h, span, :] = state
         normed = tile_norm(state).astype(jnp.bfloat16)
         proj = dot(normed, proj_w[0])
-        gates[span, :] = dot(normed, gate_w[0])
-        left[span, :] = rounded(gate_of(proj[:, :hidden]) * proj[:, hidden : 2 * hidden] * pmask)
+        gates[h, span, :] = dot(normed, gate_w[0])
+        left[h, span, :] = rounded(gate_of(proj[:, :hidden]) * proj[:, hidden : 2 * hidden] * pmask)
         rgt = rounded(gate_of(proj[:, 2 * hidden : 3 * hidden]) * proj[:, 3 * hidden :] * pmask)
         for n in range(count):
-            slot, t = divmod(base * rows + n, rows)
-            token = (me ^ masks[slot]) * rows + t
-            right[pl.ds(token, cols, tokens), :] = rgt[n * cols : (n + 1) * cols]
-
-
-def own_kernel(masks, *refs):
-    pair, chains_row, mask_row, bias, proj_w, gate_w, out_w = refs[:7]
-    bias_v, proj_v, gate_v, out_v, copied, chains, mask, start, gates, left, right, chains_v, mask_v, sems = refs[7:]
-    loads = [
-        pltpu.make_async_copy(source, target, sems.at[n])
-        for n, (source, target) in enumerate(
-            (
-                (pair, copied),
-                (chains_row, chains_v),
-                (mask_row, mask_v),
-                (bias, bias_v),
-                (proj_w, proj_v),
-                (gate_w, gate_v),
-                (out_w, out_v),
-            )
-        )
-    ]
+            at, t = divmod(n, rows)
+            token = (me ^ pick(masks[slots[at]])) * rows + t
+            right[h, pl.ds(token, cols, tokens), :] = rgt[n * cols : (n + 1) * cols]
+
+
+def prep_kernel(*refs):
+    sources, targets, (chains, mask, chains_v, mask_v, sems) = refs[:6], refs[6:10], refs[10:]
+    loads = []
+    for n, (source, target) in enumerate(zip(sources, targets + (chains_v, mask_v))):
+        loads.append(pltpu.make_async_copy(source, target, sems.at[n]))
     for load in loads:
         load.start()
     for load in loads:
         load.wait()
     table(chains_v, chains)
     table(mask_v, mask)
-    half_start = lax.axis_index("col") * copied.shape[1]
-    edges(masks, [0], half_start, copied, chains, mask, bias_v, proj_v, gate_v, start, gates, left, right)
-
-
-def mine_kernel(masks, mine, chains, mask, bias, proj_w, gate_w, s_in, g_in, l_in, r_in, start, gates, left, right):
-    half_start = lax.axis_index("col") * mine.shape[2]
-    slots = list(range(1, mine.shape[0]))
-    edges(masks, slots, half_start, mine, chains, mask, bias, proj_w, gate_w, start, gates, left, right)
-
-
-def second_kernel(
+
+
+def mine_kernel(masks, *refs):
+    blocks, rest = refs[: len(masks) // 2], refs[len(masks) // 2 :]
+
+    def source(slot, half):
+        return blocks[slot][half]
+
+    edges(masks, list(range(len(blocks))), (0, 1), source, *rest)
+
+
+def crop_kernel(
     masks,
-    other,
+    last,
+    swapped,
     chains,
     mask,
     bias,
     proj_w,
     gate_w,
     out_w,
-    start_m,
-    gates_m,
-    left_m,
-    right_m,
+    start_in,
+    gates_in,
+    left_in,
+    right_in,
     updated,
-    start_o,
-    gates_o,
-    left_o,
-    right_o,
+    start,
+    gates,
+    left,
+    right,
     tris,
     left1,
     right1,
 ):
-    ranks, rows, cols, width = other.shape
+    ranks = len(masks)
+    rows, cols, width = last.shape[1:]
     tokens = ranks * rows
     me = lax.axis_index("row")
     col = lax.axis_index("col")
     hidden = proj_w.shape[2] // 4
-    edges(masks, list(range(ranks)), (1 - col) * cols, other, chains, mask, bias, proj_w, gate_w, start_o, gates_o, left_o, right_o)
+
+    def source(slot, half):
+        there = swapped[slot - ranks // 2, 1 - half]
+        return jnp.where(col == 1, last[half], there) if slot == ranks - 1 else there
+
+    slots = list(range(ranks // 2, ranks))
+    edges(masks, slots, (0, 1), source, chains, mask, bias, proj_w, gate_w, start, gates, left, right)
 
     low = me * rows // 8 * 8
     groups = [col * cols + 8 * n for n in range(cols // 8)] + [low]
@@ -209,11 +209,11 @@
     def tri_block(step, carry):
         k0 = step * block
         acc = [[None] * count for _ in range(block)]
-        for half, (left, right) in enumerate(((left_m, right_m), (left_o, right_o))):
+        for half in range(2):
             for l in range(cols):
-                cells = [right[pl.ds(pl.multiple_of(l * tokens + g, 8), 8), :] for g in groups]
+                cells = [right[half, pl.ds(pl.multiple_of(l * tokens + g, 8), 8), :] for g in groups]
                 for k in range(block):
-                    row = left[pl.ds((k0 + k) * cols + l, 1), :]
+                    row = left[half, pl.ds((k0 + k) * cols + l, 1), :]
                     for n in range(count):
                         term = row * cells[n]
                         acc[k][n] = term if half + l == 0 else acc[k][n] + term
@@ -224,28 +224,27 @@
 
     lax.fori_loop(0, tokens // block, tri_block, 0)
 
-    low_mine = low // cols == col
+    low_half = jnp.where(low // cols == col, 0, 1)
     low_off = lax.rem(low, cols)
     mask_left = mask[pl.ds(pl.multiple_of(low, 8), 8), :]
     mask_right = mask[pl.ds(pl.multiple_of(col * cols, cols), cols), :]
 
-    def gather(mine, other, n, k):
+    def gather(values, n, k):
         if n < count - 1:
-            return mine[pl.ds(k * cols + 8 * n, 8), :]
-        span = pl.ds(pl.multiple_of(k * cols + low_off, 8), 8)
-        return jnp.where(low_mine, mine[span, :], other[span, :])
+            return values[0, pl.ds(k * cols + 8 * n, 8), :]
+        return values[low_half, pl.ds(pl.multiple_of(k * cols + low_off, 8), 8), :]
 
     def updated_state(n):
         tri = tris[n]
         tnorm = tile_norm(tri).astype(jnp.bfloat16)
-        gate = gate_of(jnp.concatenate([gather(gates_m, gates_o, n, k) for k in range(tokens)], 0))
-        state = jnp.concatenate([gather(start_m, start_o, n, k) for k in range(tokens)], 0)
+        gate = gate_of(jnp.concatenate([gather(gates, n, k) for k in range(tokens)], 0))
+        state = jnp.concatenate([gather(start, n, k) for k in range(tokens)], 0)
         return state + gate * dot(tnorm, out_w[0])
 
     row_masks = []
     for slot in range(ranks):
         for t in range(rows):
-            row_masks.append(mask[pl.ds((me ^ masks[slot]) * rows + t, 1), :])
+            row_masks.append(mask[pl.ds((me ^ pick(masks[slot])) * rows + t, 1), :])
 
     normed = tile_norm(updated_state(count - 1)).astype(jnp.bfloat16)
     proj = dot(normed, proj_w[1, :, : 2 * hidden])
@@ -281,9 +280,12 @@
             updated[t, pl.ds(8 * n, 8), :] = out[8 * t : 8 * t + 8]
 
 
-def exchange(block, bits):
+def exchange(block, pair):
     ranks = lax.axis_size("row")
-    return lax.ppermute(block, "row", [(i, i ^ bits) for i in range(ranks)])
+    hops = []
+    for c, bits in enumerate(pair):
+        hops += [(2 * i + c, 2 * (i ^ bits) + c) for i in range(ranks) if bits]
+    return lax.ppermute(block, ("row", "col"), hops)
 
 
 def call(body, inputs, outputs, scratch, name, flops, aliases={}, space=pltpu.VMEM):
@@ -314,40 +316,45 @@
     tokens = token_mask.shape[0]
     hidden = proj_weight.shape[2] // 4
     bias = chain_bias[None, :]
-    half = floats((tokens * cols, width), (tokens * cols, width), (tokens * cols, hidden), (tokens * cols, hidden))
+    half = [(2, tokens * cols, width), (2, tokens * cols, width), (2, tokens * cols, hidden), (2, tokens * cols, hidden)]
+    half = floats(*half)
     flops = 2 * tokens * cols * width * 5 * hidden
-    masks = [0] + sorted(range(1, ranks), key=lambda bits: -(bits ^ bits >> 1))
-    own_inputs = (pair, chains[None, :], token_mask[None, :], bias, proj_weight, gate_weight, out_weight)
-    own_inputs = [pltpu.with_memory_space_constraint(each, pltpu.HBM) for each in own_inputs]
-    bias, proj_weight, gate_weight, out_weight, own, chains_t, mask_t, *partial = call(
-        functools.partial(own_kernel, masks),
-        own_inputs,
-        like(bias, proj_weight, gate_weight, out_weight, pair) + floats((tokens, width), (tokens, width)) + half,
-        [pltpu.VMEM((1, tokens), jnp.int32), pltpu.VMEM((1, tokens), jnp.int32), pltpu.SemaphoreType.DMA((7,))],
-        "own",
+    peers = sorted(range(1, ranks), key=lambda bits: (bits & 1, bits))
+    zero, one = peers[: ranks // 2 - 1], peers[ranks // 2 - 1 :]
+    steps = list(zip(zero + [0], one))
+    masks = [(0, 0)] + steps[:-1] + [(b, a) for a, b in steps[:-1]] + [(one[-1], one[-1])]
+    chip = jnp.stack([pair, lax.ppermute(pair, "col", [(0, 1), (1, 0)])])
+    got = [exchange(chip, step) for step in steps]
+    swapped = lax.ppermute(jnp.stack(got), "col", [(0, 1), (1, 0)])
+    loaded = (bias, proj_weight, gate_weight, out_weight, chains[None, :], token_mask[None, :])
+    bias, proj_weight, gate_weight, out_weight, chains_t, mask_t = call(
+        prep_kernel,
+        [pltpu.with_memory_space_constraint(each, pltpu.HBM) for each in loaded],
+        like(*loaded[:4]) + floats((tokens, width), (tokens, width)),
+        [pltpu.VMEM((1, tokens), jnp.int32), pltpu.VMEM((1, tokens), jnp.int32), pltpu.SemaphoreType.DMA((6,))],
+        "prep",
         flops // ranks,
         space=pltpu.HBM,
     )
-    mine = jnp.stack([own] + [exchange(pair, bits) for bits in masks[1:]])
-    other = lax.ppermute(mine, "col", [(0, 1), (1, 0)])
-    mine_edges = call(
+    edge_inputs = (chains_t, mask_t, bias, proj_weight, gate_weight)
+    partial = call(
         functools.partial(mine_kernel, masks),
-        (mine, chains_t, mask_t, bias, proj_weight, gate_weight, *partial),
+        (chip, *got[:-1], *edge_inputs),
         half,
         [],
         "mine",
         flops,
-        {6: 0, 7: 1, 8: 2, 9: 3},
     )
     groups = cols // 8 + 1
     extra = [(groups, tokens * 8, hidden), (tokens * 8, hidden), (groups - 1, tokens * 8, hidden)]
     return call(
-        functools.partial(second_kernel, masks),
-        (other, chains_t, mask_t, bias, proj_weight, gate_weight, out_weight, *mine_edges),
-        floats(pair.shape),
-        [pltpu.VMEM(each.shape, jnp.float32) for each in half + floats(*extra)],
+        functools.partial(crop_kernel, masks),
+        (got[-1], swapped, *edge_inputs, out_weight, *partial),
+        floats(pair.shape) + half,
+        [pltpu.VMEM(each.shape, jnp.float32) for each in floats(*extra)],
         "crop",
         4 * flops,
+        {n + 8: n + 1 for n in range(4)},
     )[0]
 
 

time: 25.8 us -> 23.3 us (0.903)
  starting transfers between devices: 14.5 us -> 11.5 us
  other arithmetic: 0 us -> 0.78 us
  Pallas kernels: 6.14 us -> 5.7 us
    ppermute x8 -> x6, starting transfers between devices: 14.5 us -> 11.5 us  [the longest x4 6.22 us: exchange(): return lax.ppermute(block, ('row', 'col'), hops)]
    another operation x0 -> x2, other arithmetic: none -> 0.78 us  [the longest x1 0.76 us: whole_crop_plan(): chip = jnp.stack([pair, lax.ppermute(pair, 'col', [(0, 1), (1, 0)])])]
    pallas_call x3, Pallas kernels: 6.14 us -> 5.7 us  [call(): pl.pallas_call(body, out_shape=outputs, in_specs=[pl.BlockSpec(memory_spa...]
    ppermute x8 -> x6, waiting for transfers between devices: 4.97 us -> 4.98 us  [the longest x4 3.9 us: exchange(): return lax.ppermute(block, ('row', 'col'), hops)]
  transfers between devices with their start and end apart: 8 -> 6, of which waited for: 3 -> 3; matrix products, arithmetic and copies ran while one was open for 0% -> 0% of each run, Pallas kernels for 9% -> 8%
where the time goes in v6:
time: 23.3 us; the launch traced here: 23.1 us
  starting transfers between devices  11.5 us (49%)
  Pallas kernels  5.7 us (24%)
  waiting for transfers between devices  4.98 us (21%)
  other arithmetic  0.78 us (3%)
    ppermute x4, starting transfers between devices, exchange(): return lax.ppermute(block, ('row', 'col'), hops)  6.22 us
    pallas_call x3, Pallas kernels, call(): pl.pallas_call(body, out_shape=outputs, in_specs=[pl.BlockSpec(memory_spa...  5.7 us
    ppermute x1, starting transfers between devices, whole_crop_plan(): swapped = lax.ppermute(jnp.stack(got), 'col', [(0, 1), (1, 0)])  4.87 us
    ppermute x4, waiting for transfers between devices, exchange(): return lax.ppermute(block, ('row', 'col'), hops)  3.9 us
    ppermute x1, waiting for transfers between devices, whole_crop_plan(): chip = jnp.stack([pair, lax.ppermute(pair, 'col', [(0, 1), (1, 0)])])  1.07 us
    another operation x1, other arithmetic, whole_crop_plan(): chip = jnp.stack([pair, lax.ppermute(pair, 'col', [(0, 1), (1, 0)])])  0.76 us
  transfers between devices with their start and end apart: 6, of which 3 were waited for; matrix products, arithmetic and copies ran while one was open for 0% of the time, Pallas kernels for 8%

profile of v6, /device:TPU:0, one launch (start us, length us, event | category | flops | bytes accessed | tf_op | source)
XLA Modules:
  0.0 23.1 jit_solution(11223609192178285002)
XLA Ops:
  0.0 0.5 %collective-permute-start = (f32[4,16,128]{2,1,0:T(8,128)}, f32[4,16,128]{2,1,0:T(8,128)S(1)}, u32[]{:S(2)}, u32[]{:S(2)}) collective-permute-start(f32[4,16,128]{2,1,0:T(8,128)} %param.7), channel_id=1, source_target_pairs={{0,1},{1,0},{2,3},{3,2},{4,5},{5,4},{6,7},{7,6},{8,9},{9,8},{10,11... | collective-permute-start | bytes 98312 | tf_op jit(solution)/shard_map/ppermute | solution.py:326
  0.5 1.1 %collective-permute-done = f32[4,16,128]{2,1,0:T(8,128)S(1)} collective-permute-done((f32[4,16,128]{2,1,0:T(8,128)}, f32[4,16,128]{2,1,0:T(8,128)S(1)}, u32[]{:S(2)}, u32[]{:S(2)}) %collective-permute-start) | collective-permute-done | bytes 32800 | tf_op jit(solution)/shard_map/ppermute | solution.py:326
  1.5 0.8 %pad_maximum_fusion.1.refs_0_ = f32[2,4,16,128]{3,2,1,0:T(8,128)S(1)} fusion(f32[1,4,16,128]{3,2,1,0:T(8,128)S(1)} %bitcast.14, f32[1,4,16,128]{3,2,1,0:T(8,128)} %bitcast.13), kind=kLoop, calls=%fused_computation.1 | loop fusion | flops 16384 | bytes 131072 | tf_op jit(solution)/shard_map/stack | solution.py:326
  2.3 4.9 %collective-permute-start.4 = (f32[2,4,16,128]{3,2,1,0:T(8,128)S(1)}, f32[2,4,16,128]{3,2,1,0:T(8,128)S(1)}, u32[]{:S(2)}, u32[]{:S(2)}) collective-permute-start(f32[2,4,16,128]{3,2,1,0:T(8,128)S(1)} %pad_maximum_fusion.1.refs_0_), channel_id=1, source_target_pairs={{0,12},{2,14},{4,8},{6,10},{8,4},{10,6},{12,0},{14,2},{1,11},{3,9}... | collective-permute-start | bytes 196616 | tf_op jit(solution)/shard_map/ppermute | solution.py:288
  7.2 0.0 collective-permute-start.3
  7.2 0.6 %collective-permute-start.2 = (f32[2,4,16,128]{3,2,1,0:T(8,128)S(1)}, f32[2,4,16,128]{3,2,1,0:T(8,128)S(1)}, u32[]{:S(2)}, u32[]{:S(2)}) collective-permute-start(f32[2,4,16,128]{3,2,1,0:T(8,128)S(1)} %pad_maximum_fusion.1.refs_0_), channel_id=1, source_target_pairs={{0,4},{2,6},{4,0},{6,2},{8,12},{10,14},{12,8},{14,10},{1,3},{3,1},... | collective-permute-start | bytes 196616 | tf_op jit(solution)/shard_map/ppermute | solution.py:288
  7.9 0.7 %collective-permute-start.1 = (f32[2,4,16,128]{3,2,1,0:T(8,128)S(1)}, f32[2,4,16,128]{3,2,1,0:T(8,128)S(1)}, u32[]{:S(2)}, u32[]{:S(2)}) collective-permute-start(f32[2,4,16,128]{3,2,1,0:T(8,128)S(1)} %pad_maximum_fusion.1.refs_0_), channel_id=1, source_target_pairs={{1,15},{3,13},{5,11},{7,9},{9,7},{11,5},{13,3},{15,1},{17,31},{19,... | collective-permute-start | bytes 196616 | tf_op jit(solution)/shard_map/ppermute | solution.py:288
  8.5 1.4 %collective-permute-done.4.refs_3_ = f32[2,4,16,128]{3,2,1,0:T(8,128)S(1)} collective-permute-done((f32[2,4,16,128]{3,2,1,0:T(8,128)S(1)}, f32[2,4,16,128]{3,2,1,0:T(8,128)S(1)}, u32[]{:S(2)}, u32[]{:S(2)}) %collective-permute-start.4) | collective-permute-done | bytes 65568 | tf_op jit(solution)/shard_map/ppermute | solution.py:288
  9.9 2.5 %collective-permute-done.3.refs_2_ = f32[2,4,16,128]{3,2,1,0:T(8,128)S(1)} collective-permute-done((f32[2,4,16,128]{3,2,1,0:T(8,128)S(1)}, f32[2,4,16,128]{3,2,1,0:T(8,128)S(1)}, u32[]{:S(2)}, u32[]{:S(2)}) %collective-permute-start.3) | collective-permute-done | bytes 65568 | tf_op jit(solution)/shard_map/ppermute | solution.py:288
  12.4 0.0 collective-permute-done.2.refs_1_
  12.4 0.0 collective-permute-done.1.last
  12.5 4.9 %collective-permute-start.5 = (f32[4,2,4,16,128]{4,3,2,1,0:T(8,128)S(1)}, f32[4,2,4,16,128]{4,3,2,1,0:T(8,128)S(1)}, u32[]{:S(2)}, u32[]{:S(2)}) collective-permute-start(f32[4,2,4,16,128]{4,3,2,1,0:T(8,128)S(1)} %pad_maximum_fusion), channel_id=1, source_target_pairs={{0,1},{1,0},{2,3},{3,2},{4,5},{5,4},{6,7},{7,6},{8,9},{9,8},{10,11... | collective-permute-start | bytes 786440 | tf_op jit(solution)/shard_map/ppermute | solution.py:328
  17.3 1.1 %prep.1 = (f32[1,128]{1,0:T(1,128)S(1)}, bf16[2,128,512]{2,1,0:T(8,128)(2,1)S(1)}, bf16[2,128,128]{2,1,0:T(8,128)(2,1)S(1)}, bf16[2,128,128]{2,1,0:T(8,128)(2,1)...) custom-call(f32[1,128]{1,0:T(1,128)} %bitcast.15, bf16[2,128,512]{2,1,0:T(8,128)(2,1)} %refs_1_.1, ...), custom_call_target="tpu_custom_call" | custom-call | flops 10485760 | bytes 2097152 | tf_op jit(solution)/shard_map/prep/pallas_call | solution.py:292
  18.4 0.8 %mine.1 = (f32[2,512,128]{2,1,0:T(8,128)S(1)}, f32[2,512,128]{2,1,0:T(8,128)S(1)}, f32[2,512,128]{2,1,0:T(8,128)S(1)}, f32[2,512,128]{2,1,0:T(8,128)S(1)}) custom-call(f32[2,4,16,128]{3,2,1,0:T(8,128)S(1)} %pad_maximum_fusion.1.refs_0_, f32[2,4,16,128]{3,2,1,0:T(8,128)S(1)} %collective-permute-done.2.refs_1_, ...), custom_call_target="tpu_custom_call" | custom-call | flops 83886080 | bytes 2097152 | tf_op jit(solution)/shard_map/mine/pallas_call | solution.py:292
  19.2 0.0 collective-permute-done.5.swapped
  19.2 3.8 %crop.1 = (f32[4,16,128]{2,1,0:T(8,128)}, f32[2,512,128]{2,1,0:T(8,128)S(1)}, f32[2,512,128]{2,1,0:T(8,128)S(1)}, f32[2,512,128]{2,1,0:T(8,128)S(1)}, f32[2,512,128]{2,1,0:T(8,128)S(1)}) custom-call(f32[2,4,16,128]{3,2,1,0:T(8,128)S(1)} %collective-permute-done.1.last, ...), custom_call_target="tpu_custom_call", output_to_operand_aliasing={{1}: (8, {}), {2}: (9, {}), {3}: (10, {}), {4}: (11, {})} | custom-call | flops 335544320 | bytes 2097152 | tf_op jit(solution)/shard_map/crop/pallas_call | solution.py:292
  (1 shorter events, 0.0 us)
Async XLA Ops:
  0.0 1.5 %collective-permute-start = (f32[4,16,128]{2,1,0:T(8,128)}, f32[4,16,128]{2,1,0:T(8,128)S(1)}, u32[]{:S(2)}, u32[]{:S(2)}) collective-permute-start(f32[4,16,128]{2,1,0:T(8,128)} %param.7), channel_id=1, source_target_pairs={{0,1},{1,0},{2,3},{3,2},{4,5},{5,4},{6,7},{7,6},{8,9},{9,8},{10,11... | collective-permute-start | bytes 98312 | tf_op jit(solution)/shard_map/ppermute | solution.py:326
  2.3 7.6 %collective-permute-start.4 = (f32[2,4,16,128]{3,2,1,0:T(8,128)S(1)}, f32[2,4,16,128]{3,2,1,0:T(8,128)S(1)}, u32[]{:S(2)}, u32[]{:S(2)}) collective-permute-start(f32[2,4,16,128]{3,2,1,0:T(8,128)S(1)} %pad_maximum_fusion.1.refs_0_), channel_id=1, source_target_pairs={{0,12},{2,14},{4,8},{6,10},{8,4},{10,6},{12,0},{14,2},{1,11},{3,9}... | collective-permute-start | bytes 196616 | tf_op jit(solution)/shard_map/ppermute | solution.py:288
  7.2 5.2 %collective-permute-start.3 = (f32[2,4,16,128]{3,2,1,0:T(8,128)S(1)}, f32[2,4,16,128]{3,2,1,0:T(8,128)S(1)}, u32[]{:S(2)}, u32[]{:S(2)}) collective-permute-start(f32[2,4,16,128]{3,2,1,0:T(8,128)S(1)} %pad_maximum_fusion.1.refs_0_), channel_id=1, source_target_pairs={{0,8},{2,10},{4,12},{6,14},{8,0},{10,2},{12,4},{14,6},{1,7},{3,5},... | collective-permute-start | bytes 196616 | tf_op jit(solution)/shard_map/ppermute | solution.py:288
  7.2 5.2 %collective-permute-start.2 = (f32[2,4,16,128]{3,2,1,0:T(8,128)S(1)}, f32[2,4,16,128]{3,2,1,0:T(8,128)S(1)}, u32[]{:S(2)}, u32[]{:S(2)}) collective-permute-start(f32[2,4,16,128]{3,2,1,0:T(8,128)S(1)} %pad_maximum_fusion.1.refs_0_), channel_id=1, source_target_pairs={{0,4},{2,6},{4,0},{6,2},{8,12},{10,14},{12,8},{14,10},{1,3},{3,1},... | collective-permute-start | bytes 196616 | tf_op jit(solution)/shard_map/ppermute | solution.py:288
  7.9 4.6 %collective-permute-start.1 = (f32[2,4,16,128]{3,2,1,0:T(8,128)S(1)}, f32[2,4,16,128]{3,2,1,0:T(8,128)S(1)}, u32[]{:S(2)}, u32[]{:S(2)}) collective-permute-start(f32[2,4,16,128]{3,2,1,0:T(8,128)S(1)} %pad_maximum_fusion.1.refs_0_), channel_id=1, source_target_pairs={{1,15},{3,13},{5,11},{7,9},{9,7},{11,5},{13,3},{15,1},{17,31},{19,... | collective-permute-start | bytes 196616 | tf_op jit(solution)/shard_map/ppermute | solution.py:288
  12.5 6.8 %collective-permute-start.5 = (f32[4,2,4,16,128]{4,3,2,1,0:T(8,128)S(1)}, f32[4,2,4,16,128]{4,3,2,1,0:T(8,128)S(1)}, u32[]{:S(2)}, u32[]{:S(2)}) collective-permute-start(f32[4,2,4,16,128]{4,3,2,1,0:T(8,128)S(1)} %pad_maximum_fusion), channel_id=1, source_target_pairs={{0,1},{1,0},{2,3},{3,2},{4,5},{5,4},{6,7},{7,6},{8,9},{9,8},{10,11... | collective-permute-start | bytes 786440 | tf_op jit(solution)/shard_map/ppermute | solution.py:328

commit v7 on v6

--- a/solution.py
+++ b/solution.py
@@ -142,7 +142,7 @@
 
 
 def prep_kernel(*refs):
-    sources, targets, (chains, mask, chains_v, mask_v, sems) = refs[:6], refs[6:10], refs[10:]
+    sources, targets, (chains, mask, chains_v, mask_v, sems) = refs[:7], refs[7:12], refs[12:]
     loads = []
     for n, (source, target) in enumerate(zip(sources, targets + (chains_v, mask_v))):
         loads.append(pltpu.make_async_copy(source, target, sems.at[n]))
@@ -155,12 +155,12 @@
 
 
 def mine_kernel(masks, *refs):
-    blocks, rest = refs[: len(masks) // 2], refs[len(masks) // 2 :]
+    two, more, *rest = refs
 
     def source(slot, half):
-        return blocks[slot][half]
-
-    edges(masks, list(range(len(blocks))), (0, 1), source, *rest)
+        return two[slot, half] if slot < 2 else more[slot - 2, half]
+
+    edges(masks, list(range(4)), (0, 1), source, *rest)
 
 
 def crop_kernel(
@@ -187,15 +187,16 @@
     right1,
 ):
     ranks = len(masks)
-    rows, cols, width = last.shape[1:]
+    rows, cols, width = last.shape[2:]
     tokens = ranks * rows
     me = lax.axis_index("row")
     col = lax.axis_index("col")
     hidden = proj_w.shape[2] // 4
 
     def source(slot, half):
-        there = swapped[slot - ranks // 2, 1 - half]
-        return jnp.where(col == 1, last[half], there) if slot == ranks - 1 else there
+        at = slot - ranks // 2
+        there = swapped[at, 1 - half]
+        return there if at < 2 else jnp.where(col == 1, last[at - 2, half], there)
 
     slots = list(range(ranks // 2, ranks))
     edges(masks, slots, (0, 1), source, chains, mask, bias, proj_w, gate_w, start, gates, left, right)
@@ -319,37 +320,33 @@
     half = [(2, tokens * cols, width), (2, tokens * cols, width), (2, tokens * cols, hidden), (2, tokens * cols, hidden)]
     half = floats(*half)
     flops = 2 * tokens * cols * width * 5 * hidden
-    peers = sorted(range(1, ranks), key=lambda bits: (bits & 1, bits))
-    zero, one = peers[: ranks // 2 - 1], peers[ranks // 2 - 1 :]
-    steps = list(zip(zero + [0], one))
-    masks = [(0, 0)] + steps[:-1] + [(b, a) for a, b in steps[:-1]] + [(one[-1], one[-1])]
-    chip = jnp.stack([pair, lax.ppermute(pair, "col", [(0, 1), (1, 0)])])
-    got = [exchange(chip, step) for step in steps]
-    swapped = lax.ppermute(jnp.stack(got), "col", [(0, 1), (1, 0)])
-    loaded = (bias, proj_weight, gate_weight, out_weight, chains[None, :], token_mask[None, :])
-    bias, proj_weight, gate_weight, out_weight, chains_t, mask_t = call(
+    y, z1, z2 = 1, 2, 4
+    masks = [(0, 0), (y, z2), (z2, z1), (z2 | y, z2 | z1), (z1, y), (z2 | z1, z2 | y), (z1 | y,) * 2, (z2 | z1 | y,) * 2]
+    partner = lax.ppermute(pair, "col", [(0, 1), (1, 0)])
+    loaded = (pair, bias, proj_weight, gate_weight, out_weight, chains[None, :], token_mask[None, :])
+    own, bias, proj_weight, gate_weight, out_weight, chains_t, mask_t = call(
         prep_kernel,
         [pltpu.with_memory_space_constraint(each, pltpu.HBM) for each in loaded],
-        like(*loaded[:4]) + floats((tokens, width), (tokens, width)),
-        [pltpu.VMEM((1, tokens), jnp.int32), pltpu.VMEM((1, tokens), jnp.int32), pltpu.SemaphoreType.DMA((6,))],
+        like(*loaded[:5]) + floats((tokens, width), (tokens, width)),
+        [pltpu.VMEM((1, tokens), jnp.int32), pltpu.VMEM((1, tokens), jnp.int32), pltpu.SemaphoreType.DMA((7,))],
         "prep",
         flops // ranks,
         space=pltpu.HBM,
     )
+    chip = jnp.stack([own, partner])
+    first = exchange(chip, (y, z2))
+    two = jnp.stack([chip, first])
+    more = exchange(two, (z2, z1))
+    last = exchange(two, (0, z1 | y))
+    head = jnp.where(lax.axis_index("col") == 0, first, more[0])
+    swapped = lax.ppermute(jnp.concatenate([head[None], more[1:], last]), "col", [(0, 1), (1, 0)])
     edge_inputs = (chains_t, mask_t, bias, proj_weight, gate_weight)
-    partial = call(
-        functools.partial(mine_kernel, masks),
-        (chip, *got[:-1], *edge_inputs),
-        half,
-        [],
-        "mine",
-        flops,
-    )
+    partial = call(functools.partial(mine_kernel, masks), (two, more, *edge_inputs), half, [], "mine", flops)
     groups = cols // 8 + 1
     extra = [(groups, tokens * 8, hidden), (tokens * 8, hidden), (groups - 1, tokens * 8, hidden)]
     return call(
         functools.partial(crop_kernel, masks),
-        (got[-1], swapped, *edge_inputs, out_weight, *partial),
+        (last, swapped, *edge_inputs, out_weight, *partial),
         floats(pair.shape) + half,
         [pltpu.VMEM(each.shape, jnp.float32) for each in floats(*extra)],
         "crop",
@@ -361,7 +358,7 @@
 def shards(pair, token_mask, *rest):
     tokens = token_mask.shape[0]
     ranks = lax.axis_size("row")
-    small = tokens * tokens * pair.shape[2] <= 1 << 18 and ranks & (ranks - 1) == 0 and tokens % 16 == 0
+    small = tokens * tokens * pair.shape[2] <= 1 << 18 and ranks == 8 and pair.shape[1] % 8 == 0
     plan = whole_crop_plan if small and lax.axis_size("col") == 2 else sharded_plan
     return plan(pair, token_mask, *rest)
 

time: 23.3 us -> 20.8 us (0.89)
  starting transfers between devices: 11.5 us -> 9.84 us
  other arithmetic: 0.78 us -> 0.05 us
    ppermute x2, starting transfers between devices: 5.32 us -> 3.19 us  [the longest x1 2.74 us: whole_crop_plan(): lax.ppermute(jnp.concatenate([head[None], more[1:], last]), 'col', [(0, 1...]
    another operation x2, other arithmetic: 0.78 us -> 0.02 us  [whole_crop_plan(): two = jnp.stack([chip, first])]
    ppermute x2, waiting for transfers between devices: 1.07 us -> 0.41 us  [the longest x1 0.4 us: whole_crop_plan(): lax.ppermute(jnp.concatenate([head[None], more[1:], last]), 'col', [(0, 1...]
    ppermute x4 -> x3, waiting for transfers between devices: 3.9 us -> 4.54 us  [exchange(): return lax.ppermute(block, ('row', 'col'), hops)]
    ppermute x4 -> x3, starting transfers between devices: 6.22 us -> 6.65 us  [exchange(): return lax.ppermute(block, ('row', 'col'), hops)]
  transfers between devices with their start and end apart: 6 -> 5, of which waited for: 3 -> 3; matrix products, arithmetic and copies ran while one was open for 0% -> 0% of each run, Pallas kernels for 8% -> 9%
where the time goes in v7:
time: 20.8 us; the launch traced here: 20.6 us
  starting transfers between devices  9.84 us (47%)
  Pallas kernels  5.71 us (27%)
  waiting for transfers between devices  4.95 us (24%)
    ppermute x3, starting transfers between devices, exchange(): return lax.ppermute(block, ('row', 'col'), hops)  6.65 us
    pallas_call x3, Pallas kernels, call(): pl.pallas_call(body, out_shape=outputs, in_specs=[pl.BlockSpec(memory_spa...  5.71 us
    ppermute x3, waiting for transfers between devices, exchange(): return lax.ppermute(block, ('row', 'col'), hops)  4.54 us
    ppermute x1, starting transfers between devices, whole_crop_plan(): lax.ppermute(jnp.concatenate([head[None], more[1:], last]), 'col', [(0, 1...  2.74 us
    ppermute x1, starting transfers between devices, whole_crop_plan(): partner = lax.ppermute(pair, 'col', [(0, 1), (1, 0)])  0.45 us
  transfers between devices with their start and end apart: 5, of which 3 were waited for; matrix products, arithmetic and copies ran while one was open for 0% of the time, Pallas kernels for 9%

profile of v7, /device:TPU:0, one launch (start us, length us, event | category | flops | bytes accessed | tf_op | source)
XLA Modules:
  0.0 20.6 jit_solution(7755158203843094086)
XLA Ops:
  0.0 0.5 %collective-permute-start = (f32[4,16,128]{2,1,0:T(8,128)}, f32[4,16,128]{2,1,0:T(8,128)S(1)}, u32[]{:S(2)}, u32[]{:S(2)}) collective-permute-start(f32[4,16,128]{2,1,0:T(8,128)} %refs_0_.1), channel_id=1, source_target_pairs={{0,1},{1,0},{2,3},{3,2},{4,5},{5,4},{6,7},{7,6},{8,9},{9,8},{10,11... | collective-permute-start | bytes 98312 | tf_op jit(solution)/shard_map/ppermute | solution.py:325
  0.5 1.1 %prep.1 = (f32[4,16,128]{2,1,0:T(8,128)S(1)}, f32[1,128]{1,0:T(1,128)S(1)}, bf16[2,128,512]{2,1,0:T(8,128)(2,1)S(1)}, bf16[2,128,128]{2,1,0:T(8,128)(2,1)S(1)}, ...) custom-call(f32[4,16,128]{2,1,0:T(8,128)} %refs_0_.1, f32[1,128]{1,0:T(1,128)} %bitcast.19, ...), custom_call_target="tpu_custom_call" | custom-call | flops 10485760 | bytes 2097152 | tf_op jit(solution)/shard_map/prep/pallas_call | solution.py:293
  1.6 0.0 collective-permute-done
  1.6 2.8 %collective-permute-start.1 = (f32[2,4,16,128]{3,2,1,0:T(8,128)S(1)}, f32[2,4,16,128]{3,2,1,0:T(8,128)S(1)}, u32[]{:S(2)}, u32[]{:S(2)}) collective-permute-start(f32[2,4,16,128]{3,2,1,0:T(8,128)S(1)} %get-tuple-element.30), channel_id=1, source_target_pairs={{0,2},{2,0},{4,6},{6,4},{8,10},{10,8},{12,14},{14,12},{1,9},{3,11}... | collective-permute-start | bytes 196616 | tf_op jit(solution)/shard_map/ppermute | solution.py:289
  4.5 2.2 %collective-permute-done.1 = f32[2,4,16,128]{3,2,1,0:T(8,128)S(1)} collective-permute-done((f32[2,4,16,128]{3,2,1,0:T(8,128)S(1)}, f32[2,4,16,128]{3,2,1,0:T(8,128)S(1)}, u32[]{:S(2)}, u32[]{:S(2)}) %collective-permute-start.1) | collective-permute-done | bytes 65568 | tf_op jit(solution)/shard_map/ppermute | solution.py:289
  6.7 3.2 %collective-permute-start.3 = (f32[2,2,4,16,128]{4,3,2,1,0:T(8,128)S(1)}, f32[2,2,4,16,128]{4,3,2,1,0:T(8,128)S(1)}, u32[]{:S(2)}, u32[]{:S(2)}) collective-permute-start(f32[2,2,4,16,128]{4,3,2,1,0:T(8,128)S(1)} %pad_maximum_fusion.1.refs_0_), channel_id=1, source_target_pairs={{0,8},{2,10},{4,12},{6,14},{8,0},{10,2},{12,4},{14,6},{1,5},{3,7},... | collective-permute-start | bytes 393224 | tf_op jit(solution)/shard_map/ppermute | solution.py:289
  9.9 0.7 %collective-permute-start.2 = (f32[2,2,4,16,128]{4,3,2,1,0:T(8,128)S(1)}, f32[2,2,4,16,128]{4,3,2,1,0:T(8,128)S(1)}, u32[]{:S(2)}, u32[]{:S(2)}) collective-permute-start(f32[2,2,4,16,128]{4,3,2,1,0:T(8,128)S(1)} %pad_maximum_fusion.1.refs_0_), channel_id=1, source_target_pairs={{1,7},{3,5},{5,3},{7,1},{9,15},{11,13},{13,11},{15,9},{17,23},{19,... | collective-permute-start | bytes 393224 | tf_op jit(solution)/shard_map/ppermute | solution.py:289
  10.5 2.3 %collective-permute-done.3.refs_1_ = f32[2,2,4,16,128]{4,3,2,1,0:T(8,128)S(1)} collective-permute-done((f32[2,2,4,16,128]{4,3,2,1,0:T(8,128)S(1)}, f32[2,2,4,16,128]{4,3,2,1,0:T(8,128)S(1)}, u32[]{:S(2)}, u32[]{:S(2)}) %collective-permute-start.3) | collective-permute-done | bytes 131104 | tf_op jit(solution)/shard_map/ppermute | solution.py:289
  12.9 0.0 collective-permute-done.2.last
  12.9 2.7 %collective-permute-start.4 = (f32[4,2,4,16,128]{4,3,2,1,0:T(8,128)S(1)}, f32[4,2,4,16,128]{4,3,2,1,0:T(8,128)S(1)}, u32[]{:S(2)}, u32[]{:S(2)}) collective-permute-start(f32[4,2,4,16,128]{4,3,2,1,0:T(8,128)S(1)} %pad_maximum_fusion), channel_id=1, source_target_pairs={{0,1},{1,0},{2,3},{3,2},{4,5},{5,4},{6,7},{7,6},{8,9},{9,8},{10,11... | collective-permute-start | bytes 786440 | tf_op jit(solution)/shard_map/ppermute | solution.py:342
  15.6 0.7 %mine.1 = (f32[2,512,128]{2,1,0:T(8,128)S(1)}, f32[2,512,128]{2,1,0:T(8,128)S(1)}, f32[2,512,128]{2,1,0:T(8,128)S(1)}, f32[2,512,128]{2,1,0:T(8,128)S(1)}) custom-call(f32[2,2,4,16,128]{4,3,2,1,0:T(8,128)S(1)} %pad_maximum_fusion.1.refs_0_, f32[2,2,4,16,128]{4,3,2,1,0:T(8,128)S(1)} %collective-permute-done.3.refs_1_, ...), custom_call_target="tpu_custom_call" | custom-call | flops 83886080 | bytes 2097152 | tf_op jit(solution)/shard_map/mine/pallas_call | solution.py:293
  16.4 0.4 %collective-permute-done.4.swapped = f32[4,2,4,16,128]{4,3,2,1,0:T(8,128)S(1)} collective-permute-done((f32[4,2,4,16,128]{4,3,2,1,0:T(8,128)S(1)}, f32[4,2,4,16,128]{4,3,2,1,0:T(8,128)S(1)}, u32[]{:S(2)}, u32[]{:S(2)}) %collective-permute-start.4) | collective-permute-done | bytes 262176 | tf_op jit(solution)/shard_map/ppermute | solution.py:342
  16.8 3.8 %crop.1 = (f32[4,16,128]{2,1,0:T(8,128)}, f32[2,512,128]{2,1,0:T(8,128)S(1)}, f32[2,512,128]{2,1,0:T(8,128)S(1)}, f32[2,512,128]{2,1,0:T(8,128)S(1)}, f32[2,512,128]{2,1,0:T(8,128)S(1)}) custom-call(f32[2,2,4,16,128]{4,3,2,1,0:T(8,128)S(1)} %collective-permute-done.2.last, ...), custom_call_target="tpu_custom_call", output_to_operand_aliasing={{1}: (8, {}), {2}: (9, {}), {3}: (10, {}), {4}: (11, {})} | custom-call | flops 335544320 | bytes 2097152 | tf_op jit(solution)/shard_map/crop/pallas_call | solution.py:293
  (5 shorter events, 0.1 us)
Async XLA Ops:
  0.0 1.6 %collective-permute-start = (f32[4,16,128]{2,1,0:T(8,128)}, f32[4,16,128]{2,1,0:T(8,128)S(1)}, u32[]{:S(2)}, u32[]{:S(2)}) collective-permute-start(f32[4,16,128]{2,1,0:T(8,128)} %refs_0_.1), channel_id=1, source_target_pairs={{0,1},{1,0},{2,3},{3,2},{4,5},{5,4},{6,7},{7,6},{8,9},{9,8},{10,11... | collective-permute-start | bytes 98312 | tf_op jit(solution)/shard_map/ppermute | solution.py:325
  1.6 5.1 %collective-permute-start.1 = (f32[2,4,16,128]{3,2,1,0:T(8,128)S(1)}, f32[2,4,16,128]{3,2,1,0:T(8,128)S(1)}, u32[]{:S(2)}, u32[]{:S(2)}) collective-permute-start(f32[2,4,16,128]{3,2,1,0:T(8,128)S(1)} %get-tuple-element.30), channel_id=1, source_target_pairs={{0,2},{2,0},{4,6},{6,4},{8,10},{10,8},{12,14},{14,12},{1,9},{3,11}... | collective-permute-start | bytes 196616 | tf_op jit(solution)/shard_map/ppermute | solution.py:289
  6.7 6.1 %collective-permute-start.3 = (f32[2,2,4,16,128]{4,3,2,1,0:T(8,128)S(1)}, f32[2,2,4,16,128]{4,3,2,1,0:T(8,128)S(1)}, u32[]{:S(2)}, u32[]{:S(2)}) collective-permute-start(f32[2,2,4,16,128]{4,3,2,1,0:T(8,128)S(1)} %pad_maximum_fusion.1.refs_0_), channel_id=1, source_target_pairs={{0,8},{2,10},{4,12},{6,14},{8,0},{10,2},{12,4},{14,6},{1,5},{3,7},... | collective-permute-start | bytes 393224 | tf_op jit(solution)/shard_map/ppermute | solution.py:289
  9.9 3.0 %collective-permute-start.2 = (f32[2,2,4,16,128]{4,3,2,1,0:T(8,128)S(1)}, f32[2,2,4,16,128]{4,3,2,1,0:T(8,128)S(1)}, u32[]{:S(2)}, u32[]{:S(2)}) collective-permute-start(f32[2,2,4,16,128]{4,3,2,1,0:T(8,128)S(1)} %pad_maximum_fusion.1.refs_0_), channel_id=1, source_target_pairs={{1,7},{3,5},{5,3},{7,1},{9,15},{11,13},{13,11},{15,9},{17,23},{19,... | collective-permute-start | bytes 393224 | tf_op jit(solution)/shard_map/ppermute | solution.py:289
  12.9 3.9 %collective-permute-start.4 = (f32[4,2,4,16,128]{4,3,2,1,0:T(8,128)S(1)}, f32[4,2,4,16,128]{4,3,2,1,0:T(8,128)S(1)}, u32[]{:S(2)}, u32[]{:S(2)}) collective-permute-start(f32[4,2,4,16,128]{4,3,2,1,0:T(8,128)S(1)} %pad_maximum_fusion), channel_id=1, source_target_pairs={{0,1},{1,0},{2,3},{3,2},{4,5},{5,4},{6,7},{7,6},{8,9},{9,8},{10,11... | collective-permute-start | bytes 786440 | tf_op jit(solution)/shard_map/ppermute | solution.py:342

commit v8 on v6

--- a/solution.py
+++ b/solution.py
@@ -102,49 +102,51 @@
     out[...] = jnp.broadcast_to(jnp.sum(spread, -1, keepdims=True), (tokens, width))
 
 
-def pick(pair):
-    return jnp.where(lax.axis_index("col") == 0, *pair)
-
-
-def edges(masks, slots, halves, source, chains, mask, bias, proj_w, gate_w, start, gates, left, right):
-    rows, cols, width = source(slots[0], 0).shape
+def edges(masks, items, chains, mask, bias, proj_w, gate_w, start, gates, left, right):
+    rows, cols, width = items[0][2].shape
     tokens = chains.shape[0]
     me = lax.axis_index("row")
+    col = lax.axis_index("col")
     bias_v = bias[...]
     hidden = proj_w.shape[2] // 4
-    for h in halves:
-        col = lax.axis_index("col")
-        first = pl.multiple_of((col if h == 0 else 1 - col) * cols, cols)
+    for half in range(2):
+        batch = [(slot, block) for slot, h, block in items if h == half]
+        if not batch:
+            continue
+        first = pl.multiple_of((col if half == 0 else 1 - col) * cols, cols)
         chain_cols = chains[pl.ds(first, cols), :]
         mask_cols = mask[pl.ds(first, cols), :]
         states, pmasks = [], []
-        for slot in slots:
-            block = source(slot, h)
+        for slot, block in batch:
             for t in range(rows):
-                token = (me ^ pick(masks[slot])) * rows + t
+                token = (me ^ masks[slot]) * rows + t
                 same = chain_cols == chains[pl.ds(token, 1), :]
                 states.append(block[t] + jnp.where(same, bias_v, 0.0))
                 pmasks.append(mask_cols * mask[pl.ds(token, 1), :])
         state = jnp.concatenate(states, 0)
         pmask = jnp.concatenate(pmasks, 0)
-        count = len(slots) * rows
-        span = pl.ds(slots[0] * rows * cols, count * cols)
-        start[h, span, :] = state
         normed = tile_norm(state).astype(jnp.bfloat16)
         proj = dot(normed, proj_w[0])
-        gates[h, span, :] = dot(normed, gate_w[0])
-        left[h, span, :] = rounded(gate_of(proj[:, :hidden]) * proj[:, hidden : 2 * hidden] * pmask)
+        gate = dot(normed, gate_w[0])
+        lft = rounded(gate_of(proj[:, :hidden]) * proj[:, hidden : 2 * hidden] * pmask)
         rgt = rounded(gate_of(proj[:, 2 * hidden : 3 * hidden]) * proj[:, 3 * hidden :] * pmask)
-        for n in range(count):
-            at, t = divmod(n, rows)
-            token = (me ^ pick(masks[slots[at]])) * rows + t
-            right[h, pl.ds(token, cols, tokens), :] = rgt[n * cols : (n + 1) * cols]
-
-
-def prep_kernel(*refs):
-    sources, targets, (chains, mask, chains_v, mask_v, sems) = refs[:6], refs[6:10], refs[10:]
+        size = rows * cols
+        for n, (slot, _) in enumerate(batch):
+            span, part = pl.ds(slot * size, size), slice(n * size, (n + 1) * size)
+            start[half, span, :] = state[part]
+            gates[half, span, :] = gate[part]
+            left[half, span, :] = lft[part]
+            for t in range(rows):
+                token = (me ^ masks[slot]) * rows + t
+                at = n * size + t * cols
+                right[half, pl.ds(token, cols, tokens), :] = rgt[at : at + cols]
+
+
+def own_kernel(masks, *refs):
+    sources, rest = refs[:7], refs[7:]
+    pair, bias, proj_w, gate_w, out_w, chains, mask, start, gates, left, right, chains_v, mask_v, sems = rest
     loads = []
-    for n, (source, target) in enumerate(zip(sources, targets + (chains_v, mask_v))):
+    for n, (source, target) in enumerate(zip(sources, (pair, bias, proj_w, gate_w, out_w, chains_v, mask_v))):
         loads.append(pltpu.make_async_copy(source, target, sems.at[n]))
     for load in loads:
         load.start()
@@ -152,21 +154,18 @@
         load.wait()
     table(chains_v, chains)
     table(mask_v, mask)
-
-
-def mine_kernel(masks, *refs):
-    blocks, rest = refs[: len(masks) // 2], refs[len(masks) // 2 :]
-
-    def source(slot, half):
-        return blocks[slot][half]
-
-    edges(masks, list(range(len(blocks))), (0, 1), source, *rest)
+    edges(masks, [(0, 0, pair[...])], chains, mask, bias, proj_w, gate_w, start, gates, left, right)
+
+
+def mine_kernel(masks, halves, mine, chains, mask, bias, proj_w, gate_w, s_in, g_in, l_in, r_in, *outs):
+    items = [(slot, halves[slot], mine[slot]) for slot in range(1, len(masks))]
+    edges(masks, items, chains, mask, bias, proj_w, gate_w, *outs)
 
 
 def crop_kernel(
     masks,
-    last,
-    swapped,
+    halves,
+    other,
     chains,
     mask,
     bias,
@@ -186,19 +185,13 @@
     left1,
     right1,
 ):
-    ranks = len(masks)
-    rows, cols, width = last.shape[1:]
+    ranks, rows, cols, width = other.shape
     tokens = ranks * rows
     me = lax.axis_index("row")
     col = lax.axis_index("col")
     hidden = proj_w.shape[2] // 4
-
-    def source(slot, half):
-        there = swapped[slot - ranks // 2, 1 - half]
-        return jnp.where(col == 1, last[half], there) if slot == ranks - 1 else there
-
-    slots = list(range(ranks // 2, ranks))
-    edges(masks, slots, (0, 1), source, chains, mask, bias, proj_w, gate_w, start, gates, left, right)
+    items = [(slot, 1 - halves[slot], other[slot]) for slot in range(ranks)]
+    edges(masks, items, chains, mask, bias, proj_w, gate_w, start, gates, left, right)
 
     low = me * rows // 8 * 8
     groups = [col * cols + 8 * n for n in range(cols // 8)] + [low]
@@ -244,7 +237,7 @@
     row_masks = []
     for slot in range(ranks):
         for t in range(rows):
-            row_masks.append(mask[pl.ds((me ^ pick(masks[slot])) * rows + t, 1), :])
+            row_masks.append(mask[pl.ds((me ^ masks[slot]) * rows + t, 1), :])
 
     normed = tile_norm(updated_state(count - 1)).astype(jnp.bfloat16)
     proj = dot(normed, proj_w[1, :, : 2 * hidden])
@@ -280,11 +273,9 @@
             updated[t, pl.ds(8 * n, 8), :] = out[8 * t : 8 * t + 8]
 
 
-def exchange(block, pair):
+def exchange(block, bits):
     ranks = lax.axis_size("row")
-    hops = []
-    for c, bits in enumerate(pair):
-        hops += [(2 * i + c, 2 * (i ^ bits) + c) for i in range(ranks) if bits]
+    hops = [(2 * i + c, 2 * (i ^ bits) + 1 - c) for i in range(ranks) for c in range(2)]
     return lax.ppermute(block, ("row", "col"), hops)
 
 
@@ -319,49 +310,52 @@
     half = [(2, tokens * cols, width), (2, tokens * cols, width), (2, tokens * cols, hidden), (2, tokens * cols, hidden)]
     half = floats(*half)
     flops = 2 * tokens * cols * width * 5 * hidden
-    peers = sorted(range(1, ranks), key=lambda bits: (bits & 1, bits))
-    zero, one = peers[: ranks // 2 - 1], peers[ranks // 2 - 1 :]
-    steps = list(zip(zero + [0], one))
-    masks = [(0, 0)] + steps[:-1] + [(b, a) for a, b in steps[:-1]] + [(one[-1], one[-1])]
-    chip = jnp.stack([pair, lax.ppermute(pair, "col", [(0, 1), (1, 0)])])
-    got = [exchange(chip, step) for step in steps]
-    swapped = lax.ppermute(jnp.stack(got), "col", [(0, 1), (1, 0)])
-    loaded = (bias, proj_weight, gate_weight, out_weight, chains[None, :], token_mask[None, :])
-    bias, proj_weight, gate_weight, out_weight, chains_t, mask_t = call(
-        prep_kernel,
+    top = ranks // 2
+    masks, halves = [0, top], [0, 1]
+    for bits in range(top - 1, 0, -1):
+        masks += [bits, bits ^ top]
+        halves += [1, 0]
+    far = exchange(pair, top)
+    loaded = (pair, bias, proj_weight, gate_weight, out_weight, chains[None, :], token_mask[None, :])
+    own, bias, proj_weight, gate_weight, out_weight, chains_t, mask_t, *partial = call(
+        functools.partial(own_kernel, masks),
         [pltpu.with_memory_space_constraint(each, pltpu.HBM) for each in loaded],
-        like(*loaded[:4]) + floats((tokens, width), (tokens, width)),
-        [pltpu.VMEM((1, tokens), jnp.int32), pltpu.VMEM((1, tokens), jnp.int32), pltpu.SemaphoreType.DMA((6,))],
-        "prep",
+        like(*loaded[:5]) + floats((tokens, width), (tokens, width)) + half,
+        [pltpu.VMEM((1, tokens), jnp.int32), pltpu.VMEM((1, tokens), jnp.int32), pltpu.SemaphoreType.DMA((7,))],
+        "own",
         flops // ranks,
         space=pltpu.HBM,
     )
+    two = jnp.stack([own, far])
+    mine = jnp.concatenate([two] + [exchange(two, bits) for bits in range(top - 1, 0, -1)], 0)
+    other = lax.ppermute(mine, "col", [(0, 1), (1, 0)])
     edge_inputs = (chains_t, mask_t, bias, proj_weight, gate_weight)
     partial = call(
-        functools.partial(mine_kernel, masks),
-        (chip, *got[:-1], *edge_inputs),
+        functools.partial(mine_kernel, masks, halves),
+        (mine, *edge_inputs, *partial),
         half,
         [],
         "mine",
         flops,
+        {n + 6: n for n in range(4)},
     )
     groups = cols // 8 + 1
     extra = [(groups, tokens * 8, hidden), (tokens * 8, hidden), (groups - 1, tokens * 8, hidden)]
     return call(
-        functools.partial(crop_kernel, masks),
-        (got[-1], swapped, *edge_inputs, out_weight, *partial),
+        functools.partial(crop_kernel, masks, halves),
+        (other, *edge_inputs, out_weight, *partial),
         floats(pair.shape) + half,
         [pltpu.VMEM(each.shape, jnp.float32) for each in floats(*extra)],
         "crop",
         4 * flops,
-        {n + 8: n + 1 for n in range(4)},
+        {n + 7: n + 1 for n in range(4)},
     )[0]
 
 
 def shards(pair, token_mask, *rest):
     tokens = token_mask.shape[0]
     ranks = lax.axis_size("row")
-    small = tokens * tokens * pair.shape[2] <= 1 << 18 and ranks & (ranks - 1) == 0 and tokens % 16 == 0
+    small = tokens * tokens * pair.shape[2] <= 1 << 18 and ranks & (ranks - 1) == 0 and pair.shape[1] % 8 == 0
     plan = whole_crop_plan if small and lax.axis_size("col") == 2 else sharded_plan
     return plan(pair, token_mask, *rest)
 

time: 23.3 us -> 19.4 us (0.83)
  starting transfers between devices: 11.5 us -> 6.95 us
  waiting for transfers between devices: 4.98 us -> 6.28 us
  other arithmetic: 0.78 us -> 0.01 us
  Pallas kernels: 5.7 us -> 5.95 us
    ppermute x2 -> x1, starting transfers between devices: 5.32 us -> 0.22 us  [whole_crop_plan(): other = lax.ppermute(mine, 'col', [(0, 1), (1, 0)])]
    ppermute x4, waiting for transfers between devices: 3.9 us -> 5.55 us  [exchange(): return lax.ppermute(block, ('row', 'col'), hops)]
    another operation x2 -> x1, other arithmetic: 0.78 us -> 0.01 us  [whole_crop_plan(): two = jnp.stack([own, far])]
    ppermute x4, starting transfers between devices: 6.22 us -> 6.73 us  [exchange(): return lax.ppermute(block, ('row', 'col'), hops)]
    ppermute x2 -> x1, waiting for transfers between devices: 1.07 us -> 0.73 us  [whole_crop_plan(): other = lax.ppermute(mine, 'col', [(0, 1), (1, 0)])]
    pallas_call x3, Pallas kernels: 5.7 us -> 5.95 us  [call(): pl.pallas_call(body, out_shape=outputs, in_specs=[pl.BlockSpec(memory_spa...]
  transfers between devices with their start and end apart: 6 -> 5, of which waited for: 3 -> 3; matrix products, arithmetic and copies ran while one was open for 0% -> 0% of each run, Pallas kernels for 8% -> 11%
where the time goes in v8:
time: 19.4 us; the launch traced here: 19.3 us
  starting transfers between devices  6.95 us (36%)
  waiting for transfers between devices  6.28 us (32%)
  Pallas kernels  5.95 us (31%)
    ppermute x4, starting transfers between devices, exchange(): return lax.ppermute(block, ('row', 'col'), hops)  6.73 us
    pallas_call x3, Pallas kernels, call(): pl.pallas_call(body, out_shape=outputs, in_specs=[pl.BlockSpec(memory_spa...  5.95 us
    ppermute x4, waiting for transfers between devices, exchange(): return lax.ppermute(block, ('row', 'col'), hops)  5.55 us
    ppermute x1, waiting for transfers between devices, whole_crop_plan(): other = lax.ppermute(mine, 'col', [(0, 1), (1, 0)])  0.73 us
  transfers between devices with their start and end apart: 5, of which 3 were waited for; matrix products, arithmetic and copies ran while one was open for 0% of the time, Pallas kernels for 11%

profile of v8, /device:TPU:0, one launch (start us, length us, event | category | flops | bytes accessed | tf_op | source)
XLA Modules:
  0.0 19.3 jit_solution(17931124927148163928)
XLA Ops:
  0.0 3.5 %collective-permute-start = (f32[4,16,128]{2,1,0:T(8,128)}, f32[4,16,128]{2,1,0:T(8,128)S(1)}, u32[]{:S(2)}, u32[]{:S(2)}) collective-permute-start(f32[4,16,128]{2,1,0:T(8,128)} %refs_0_.1), channel_id=1, source_target_pairs={{0,9},{1,8},{2,11},{3,10},{4,13},{5,12},{6,15},{7,14},{8,1},{9,0},... | collective-permute-start | bytes 98312 | tf_op jit(solution)/shard_map/ppermute | solution.py:279
  3.5 1.5 %own.1 = (f32[4,16,128]{2,1,0:T(8,128)S(1)}, f32[1,128]{1,0:T(1,128)S(1)}, bf16[2,128,512]{2,1,0:T(8,128)(2,1)S(1)}, bf16[2,128,128]{2,1,0:T(8,128)(2,1)S(1)}, b...) custom-call(f32[4,16,128]{2,1,0:T(8,128)} %refs_0_.1, ...), custom_call_target="tpu_custom_call" | custom-call | flops 10485760 | bytes 2097152 | tf_op jit(solution)/shard_map/own/pallas_call | solution.py:283
  5.0 0.6 %collective-permute-done = f32[4,16,128]{2,1,0:T(8,128)S(1)} collective-permute-done((f32[4,16,128]{2,1,0:T(8,128)}, f32[4,16,128]{2,1,0:T(8,128)S(1)}, u32[]{:S(2)}, u32[]{:S(2)}) %collective-permute-start) | collective-permute-done | bytes 32800 | tf_op jit(solution)/shard_map/ppermute | solution.py:279
  5.6 1.7 %collective-permute-start.3 = (f32[2,4,16,128]{3,2,1,0:T(8,128)S(1)}, f32[2,4,16,128]{3,2,1,0:T(8,128)S(1)}, u32[]{:S(2)}, u32[]{:S(2)}) collective-permute-start(f32[2,4,16,128]{3,2,1,0:T(8,128)S(1)} %pad_maximum_fusion), channel_id=1, source_target_pairs={{0,3},{1,2},{2,1},{3,0},{4,7},{5,6},{6,5},{7,4},{8,11},{9,10},{10,... | collective-permute-start | bytes 196616 | tf_op jit(solution)/shard_map/ppermute | solution.py:279
  7.2 1.6 %collective-permute-start.2 = (f32[2,4,16,128]{3,2,1,0:T(8,128)S(1)}, f32[2,4,16,128]{3,2,1,0:T(8,128)S(1)}, u32[]{:S(2)}, u32[]{:S(2)}) collective-permute-start(f32[2,4,16,128]{3,2,1,0:T(8,128)S(1)} %pad_maximum_fusion), channel_id=1, source_target_pairs={{0,5},{1,4},{2,7},{3,6},{4,1},{5,0},{6,3},{7,2},{8,13},{9,12},{10,... | collective-permute-start | bytes 196616 | tf_op jit(solution)/shard_map/ppermute | solution.py:279
  8.8 0.0 collective-permute-start.1
  8.8 5.0 %collective-permute-done.1 = f32[2,4,16,128]{3,2,1,0:T(8,128)S(1)} collective-permute-done((f32[2,4,16,128]{3,2,1,0:T(8,128)S(1)}, f32[2,4,16,128]{3,2,1,0:T(8,128)S(1)}, u32[]{:S(2)}, u32[]{:S(2)}) %collective-permute-start.1) | collective-permute-done | bytes 65568 | tf_op jit(solution)/shard_map/ppermute | solution.py:279
  13.8 0.0 collective-permute-done.2
  13.8 0.0 collective-permute-done.3
  13.8 0.2 %collective-permute-start.4 = (f32[8,4,16,128]{3,2,1,0:T(8,128)S(1)}, f32[8,4,16,128]{3,2,1,0:T(8,128)S(1)}, u32[]{:S(2)}, u32[]{:S(2)}) collective-permute-start(f32[8,4,16,128]{3,2,1,0:T(8,128)S(1)} %constant_dynamic-update-slice_fusion.mine), channel_id=1, source_target_pairs={{0,1},{1,0},{2,3},{3,2},{4,5},{5,4},{6,7},{7,6},{8,9},{9,8},{10,11... | collective-permute-start | bytes 786440 | tf_op jit(solution)/shard_map/ppermute | solution.py:331
  14.1 0.6 %mine.1 = (f32[2,512,128]{2,1,0:T(8,128)S(1)}, f32[2,512,128]{2,1,0:T(8,128)S(1)}, f32[2,512,128]{2,1,0:T(8,128)S(1)}, f32[2,512,128]{2,1,0:T(8,128)S(1)}) custom-call(f32[8,4,16,128]{3,2,1,0:T(8,128)S(1)} %constant_dynamic-update-slice_fusion.mine, ...), custom_call_target="tpu_custom_call", output_to_operand_aliasing={{0}: (6, {}), {1}: (7, {}), {2}: (8, {}), {3}: (9, {})} | custom-call | flops 83886080 | bytes 2097152 | tf_op jit(solution)/shard_map/mine/pallas_call | solution.py:283
  14.7 0.7 %collective-permute-done.4.other = f32[8,4,16,128]{3,2,1,0:T(8,128)S(1)} collective-permute-done((f32[8,4,16,128]{3,2,1,0:T(8,128)S(1)}, f32[8,4,16,128]{3,2,1,0:T(8,128)S(1)}, u32[]{:S(2)}, u32[]{:S(2)}) %collective-permute-start.4) | collective-permute-done | bytes 262176 | tf_op jit(solution)/shard_map/ppermute | solution.py:331
  15.4 3.8 %crop.1 = (f32[4,16,128]{2,1,0:T(8,128)}, f32[2,512,128]{2,1,0:T(8,128)S(1)}, f32[2,512,128]{2,1,0:T(8,128)S(1)}, f32[2,512,128]{2,1,0:T(8,128)S(1)}, f32[2,512,128]{2,1,0:T(8,128)S(1)}) custom-call(f32[8,4,16,128]{3,2,1,0:T(8,128)S(1)} %collective-permute-done.4.other, ...), custom_call_target="tpu_custom_call", output_to_operand_aliasing={{1}: (7, {}), {2}: (8, {}), {3}: (9, {}), {4}: (10, {})} | custom-call | flops 335544320 | bytes 2097152 | tf_op jit(solution)/shard_map/crop/pallas_call | solution.py:283
  (6 shorter events, 0.0 us)
Async XLA Ops:
  0.0 5.6 %collective-permute-start = (f32[4,16,128]{2,1,0:T(8,128)}, f32[4,16,128]{2,1,0:T(8,128)S(1)}, u32[]{:S(2)}, u32[]{:S(2)}) collective-permute-start(f32[4,16,128]{2,1,0:T(8,128)} %refs_0_.1), channel_id=1, source_target_pairs={{0,9},{1,8},{2,11},{3,10},{4,13},{5,12},{6,15},{7,14},{8,1},{9,0},... | collective-permute-start | bytes 98312 | tf_op jit(solution)/shard_map/ppermute | solution.py:279
  5.6 8.3 %collective-permute-start.3 = (f32[2,4,16,128]{3,2,1,0:T(8,128)S(1)}, f32[2,4,16,128]{3,2,1,0:T(8,128)S(1)}, u32[]{:S(2)}, u32[]{:S(2)}) collective-permute-start(f32[2,4,16,128]{3,2,1,0:T(8,128)S(1)} %pad_maximum_fusion), channel_id=1, source_target_pairs={{0,3},{1,2},{2,1},{3,0},{4,7},{5,6},{6,5},{7,4},{8,11},{9,10},{10,... | collective-permute-start | bytes 196616 | tf_op jit(solution)/shard_map/ppermute | solution.py:279
  7.2 6.5 %collective-permute-start.2 = (f32[2,4,16,128]{3,2,1,0:T(8,128)S(1)}, f32[2,4,16,128]{3,2,1,0:T(8,128)S(1)}, u32[]{:S(2)}, u32[]{:S(2)}) collective-permute-start(f32[2,4,16,128]{3,2,1,0:T(8,128)S(1)} %pad_maximum_fusion), channel_id=1, source_target_pairs={{0,5},{1,4},{2,7},{3,6},{4,1},{5,0},{6,3},{7,2},{8,13},{9,12},{10,... | collective-permute-start | bytes 196616 | tf_op jit(solution)/shard_map/ppermute | solution.py:279
  8.8 5.0 %collective-permute-start.1 = (f32[2,4,16,128]{3,2,1,0:T(8,128)S(1)}, f32[2,4,16,128]{3,2,1,0:T(8,128)S(1)}, u32[]{:S(2)}, u32[]{:S(2)}) collective-permute-start(f32[2,4,16,128]{3,2,1,0:T(8,128)S(1)} %pad_maximum_fusion), channel_id=1, source_target_pairs={{0,7},{1,6},{2,5},{3,4},{4,3},{5,2},{6,1},{7,0},{8,15},{9,14},{10,... | collective-permute-start | bytes 196616 | tf_op jit(solution)/shard_map/ppermute | solution.py:279
  13.8 1.6 %collective-permute-start.4 = (f32[8,4,16,128]{3,2,1,0:T(8,128)S(1)}, f32[8,4,16,128]{3,2,1,0:T(8,128)S(1)}, u32[]{:S(2)}, u32[]{:S(2)}) collective-permute-start(f32[8,4,16,128]{3,2,1,0:T(8,128)S(1)} %constant_dynamic-update-slice_fusion.mine), channel_id=1, source_target_pairs={{0,1},{1,0},{2,3},{3,2},{4,5},{5,4},{6,7},{7,6},{8,9},{9,8},{10,11... | collective-permute-start | bytes 786440 | tf_op jit(solution)/shard_map/ppermute | solution.py:331

commit v9 on v8

--- a/solution.py
+++ b/solution.py
@@ -312,7 +312,7 @@
     flops = 2 * tokens * cols * width * 5 * hidden
     top = ranks // 2
     masks, halves = [0, top], [0, 1]
-    for bits in range(top - 1, 0, -1):
+    for bits in range(1, top):
         masks += [bits, bits ^ top]
         halves += [1, 0]
     far = exchange(pair, top)
@@ -327,7 +327,7 @@
         space=pltpu.HBM,
     )
     two = jnp.stack([own, far])
-    mine = jnp.concatenate([two] + [exchange(two, bits) for bits in range(top - 1, 0, -1)], 0)
+    mine = jnp.concatenate([two] + [exchange(two, bits) for bits in range(1, top)], 0)
     other = lax.ppermute(mine, "col", [(0, 1), (1, 0)])
     edge_inputs = (chains_t, mask_t, bias, proj_weight, gate_weight)
     partial = call(

time: 19.4 us -> 18.5 us (0.954)
  waiting for transfers between devices: 6.28 us -> 5.32 us
    ppermute x4, waiting for transfers between devices: 5.55 us -> 4.56 us  [exchange(): return lax.ppermute(block, ('row', 'col'), hops)]
  transfers between devices with their start and end apart: 5 -> 5, of which waited for: 3 -> 3; matrix products, arithmetic and copies ran while one was open for 0% -> 0% of each run, Pallas kernels for 11% -> 12%
where the time goes in v9:
time: 18.5 us; the launch traced here: 18.3 us
  starting transfers between devices  6.99 us (38%)
  Pallas kernels  5.94 us (32%)
  waiting for transfers between devices  5.32 us (29%)
    ppermute x4, starting transfers between devices, exchange(): return lax.ppermute(block, ('row', 'col'), hops)  6.81 us
    pallas_call x3, Pallas kernels, call(): pl.pallas_call(body, out_shape=outputs, in_specs=[pl.BlockSpec(memory_spa...  5.94 us
    ppermute x4, waiting for transfers between devices, exchange(): return lax.ppermute(block, ('row', 'col'), hops)  4.56 us
    ppermute x1, waiting for transfers between devices, whole_crop_plan(): other = lax.ppermute(mine, 'col', [(0, 1), (1, 0)])  0.76 us
  transfers between devices with their start and end apart: 5, of which 3 were waited for; matrix products, arithmetic and copies ran while one was open for 0% of the time, Pallas kernels for 12%

profile of v9, /device:TPU:0, one launch (start us, length us, event | category | flops | bytes accessed | tf_op | source)
XLA Modules:
  0.0 18.3 jit_solution(7834131864930301104)
XLA Ops:
  0.0 3.5 %collective-permute-start = (f32[4,16,128]{2,1,0:T(8,128)}, f32[4,16,128]{2,1,0:T(8,128)S(1)}, u32[]{:S(2)}, u32[]{:S(2)}) collective-permute-start(f32[4,16,128]{2,1,0:T(8,128)} %refs_0_.1), channel_id=1, source_target_pairs={{0,9},{1,8},{2,11},{3,10},{4,13},{5,12},{6,15},{7,14},{8,1},{9,0},... | collective-permute-start | bytes 98312 | tf_op jit(solution)/shard_map/ppermute | solution.py:279
  3.5 1.5 %own.1 = (f32[4,16,128]{2,1,0:T(8,128)S(1)}, f32[1,128]{1,0:T(1,128)S(1)}, bf16[2,128,512]{2,1,0:T(8,128)(2,1)S(1)}, bf16[2,128,128]{2,1,0:T(8,128)(2,1)S(1)}, b...) custom-call(f32[4,16,128]{2,1,0:T(8,128)} %refs_0_.1, ...), custom_call_target="tpu_custom_call" | custom-call | flops 10485760 | bytes 2097152 | tf_op jit(solution)/shard_map/own/pallas_call | solution.py:283
  5.0 0.6 %collective-permute-done = f32[4,16,128]{2,1,0:T(8,128)S(1)} collective-permute-done((f32[4,16,128]{2,1,0:T(8,128)}, f32[4,16,128]{2,1,0:T(8,128)S(1)}, u32[]{:S(2)}, u32[]{:S(2)}) %collective-permute-start) | collective-permute-done | bytes 32800 | tf_op jit(solution)/shard_map/ppermute | solution.py:279
  5.6 2.7 %collective-permute-start.3 = (f32[2,4,16,128]{3,2,1,0:T(8,128)S(1)}, f32[2,4,16,128]{3,2,1,0:T(8,128)S(1)}, u32[]{:S(2)}, u32[]{:S(2)}) collective-permute-start(f32[2,4,16,128]{3,2,1,0:T(8,128)S(1)} %pad_maximum_fusion), channel_id=1, source_target_pairs={{0,7},{1,6},{2,5},{3,4},{4,3},{5,2},{6,1},{7,0},{8,15},{9,14},{10,... | collective-permute-start | bytes 196616 | tf_op jit(solution)/shard_map/ppermute | solution.py:279
  8.3 0.5 %collective-permute-start.2 = (f32[2,4,16,128]{3,2,1,0:T(8,128)S(1)}, f32[2,4,16,128]{3,2,1,0:T(8,128)S(1)}, u32[]{:S(2)}, u32[]{:S(2)}) collective-permute-start(f32[2,4,16,128]{3,2,1,0:T(8,128)S(1)} %pad_maximum_fusion), channel_id=1, source_target_pairs={{0,5},{1,4},{2,7},{3,6},{4,1},{5,0},{6,3},{7,2},{8,13},{9,12},{10,... | collective-permute-start | bytes 196616 | tf_op jit(solution)/shard_map/ppermute | solution.py:279
  8.7 0.2 collective-permute-start.1
  8.9 4.0 %collective-permute-done.1 = f32[2,4,16,128]{3,2,1,0:T(8,128)S(1)} collective-permute-done((f32[2,4,16,128]{3,2,1,0:T(8,128)S(1)}, f32[2,4,16,128]{3,2,1,0:T(8,128)S(1)}, u32[]{:S(2)}, u32[]{:S(2)}) %collective-permute-start.1) | collective-permute-done | bytes 65568 | tf_op jit(solution)/shard_map/ppermute | solution.py:279
  12.9 0.0 collective-permute-done.2
  12.9 0.0 collective-permute-done.3
  12.9 0.2 collective-permute-start.4
  13.1 0.6 %mine.1 = (f32[2,512,128]{2,1,0:T(8,128)S(1)}, f32[2,512,128]{2,1,0:T(8,128)S(1)}, f32[2,512,128]{2,1,0:T(8,128)S(1)}, f32[2,512,128]{2,1,0:T(8,128)S(1)}) custom-call(f32[8,4,16,128]{3,2,1,0:T(8,128)S(1)} %constant_dynamic-update-slice_fusion.mine, ...), custom_call_target="tpu_custom_call", output_to_operand_aliasing={{0}: (6, {}), {1}: (7, {}), {2}: (8, {}), {3}: (9, {})} | custom-call | flops 83886080 | bytes 2097152 | tf_op jit(solution)/shard_map/mine/pallas_call | solution.py:283
  13.8 0.8 %collective-permute-done.4.other = f32[8,4,16,128]{3,2,1,0:T(8,128)S(1)} collective-permute-done((f32[8,4,16,128]{3,2,1,0:T(8,128)S(1)}, f32[8,4,16,128]{3,2,1,0:T(8,128)S(1)}, u32[]{:S(2)}, u32[]{:S(2)}) %collective-permute-start.4) | collective-permute-done | bytes 262176 | tf_op jit(solution)/shard_map/ppermute | solution.py:331
  14.5 3.8 %crop.1 = (f32[4,16,128]{2,1,0:T(8,128)}, f32[2,512,128]{2,1,0:T(8,128)S(1)}, f32[2,512,128]{2,1,0:T(8,128)S(1)}, f32[2,512,128]{2,1,0:T(8,128)S(1)}, f32[2,512,128]{2,1,0:T(8,128)S(1)}) custom-call(f32[8,4,16,128]{3,2,1,0:T(8,128)S(1)} %collective-permute-done.4.other, ...), custom_call_target="tpu_custom_call", output_to_operand_aliasing={{1}: (7, {}), {2}: (8, {}), {3}: (9, {}), {4}: (10, {})} | custom-call | flops 335544320 | bytes 2097152 | tf_op jit(solution)/shard_map/crop/pallas_call | solution.py:283
  (6 shorter events, 0.0 us)
Async XLA Ops:
  0.0 5.6 %collective-permute-start = (f32[4,16,128]{2,1,0:T(8,128)}, f32[4,16,128]{2,1,0:T(8,128)S(1)}, u32[]{:S(2)}, u32[]{:S(2)}) collective-permute-start(f32[4,16,128]{2,1,0:T(8,128)} %refs_0_.1), channel_id=1, source_target_pairs={{0,9},{1,8},{2,11},{3,10},{4,13},{5,12},{6,15},{7,14},{8,1},{9,0},... | collective-permute-start | bytes 98312 | tf_op jit(solution)/shard_map/ppermute | solution.py:279
  5.6 7.3 %collective-permute-start.3 = (f32[2,4,16,128]{3,2,1,0:T(8,128)S(1)}, f32[2,4,16,128]{3,2,1,0:T(8,128)S(1)}, u32[]{:S(2)}, u32[]{:S(2)}) collective-permute-start(f32[2,4,16,128]{3,2,1,0:T(8,128)S(1)} %pad_maximum_fusion), channel_id=1, source_target_pairs={{0,7},{1,6},{2,5},{3,4},{4,3},{5,2},{6,1},{7,0},{8,15},{9,14},{10,... | collective-permute-start | bytes 196616 | tf_op jit(solution)/shard_map/ppermute | solution.py:279
  8.3 4.6 %collective-permute-start.2 = (f32[2,4,16,128]{3,2,1,0:T(8,128)S(1)}, f32[2,4,16,128]{3,2,1,0:T(8,128)S(1)}, u32[]{:S(2)}, u32[]{:S(2)}) collective-permute-start(f32[2,4,16,128]{3,2,1,0:T(8,128)S(1)} %pad_maximum_fusion), channel_id=1, source_target_pairs={{0,5},{1,4},{2,7},{3,6},{4,1},{5,0},{6,3},{7,2},{8,13},{9,12},{10,... | collective-permute-start | bytes 196616 | tf_op jit(solution)/shard_map/ppermute | solution.py:279
  8.7 4.1 %collective-permute-start.1 = (f32[2,4,16,128]{3,2,1,0:T(8,128)S(1)}, f32[2,4,16,128]{3,2,1,0:T(8,128)S(1)}, u32[]{:S(2)}, u32[]{:S(2)}) collective-permute-start(f32[2,4,16,128]{3,2,1,0:T(8,128)S(1)} %pad_maximum_fusion), channel_id=1, source_target_pairs={{0,3},{1,2},{2,1},{3,0},{4,7},{5,6},{6,5},{7,4},{8,11},{9,10},{10,... | collective-permute-start | bytes 196616 | tf_op jit(solution)/shard_map/ppermute | solution.py:279
  12.9 1.6 %collective-permute-start.4 = (f32[8,4,16,128]{3,2,1,0:T(8,128)S(1)}, f32[8,4,16,128]{3,2,1,0:T(8,128)S(1)}, u32[]{:S(2)}, u32[]{:S(2)}) collective-permute-start(f32[8,4,16,128]{3,2,1,0:T(8,128)S(1)} %constant_dynamic-update-slice_fusion.mine), channel_id=1, source_target_pairs={{0,1},{1,0},{2,3},{3,2},{4,5},{5,4},{6,7},{7,6},{8,9},{9,8},{10,11... | collective-permute-start | bytes 786440 | tf_op jit(solution)/shard_map/ppermute | solution.py:331

commit v10 on v9

--- a/solution.py
+++ b/solution.py
@@ -75,11 +75,17 @@
     return finish(state, normed, tri, gate_weight[1], out_weight[1])
 
 
+def lane_mean(values):
+    width = values.shape[-1]
+    high = values.astype(jnp.bfloat16)
+    low = (values - high.astype(jnp.float32)).astype(jnp.bfloat16)
+    share = jnp.full((2 * width, width), 1 / width, jnp.bfloat16)
+    return dot(jnp.concatenate([high, low], -1), share)
+
+
 def tile_norm(values):
-    mean = jnp.mean(values, -1, keepdims=True)
-    centred = values - mean
-    var = jnp.mean(centred * centred, -1, keepdims=True)
-    return centred * lax.rsqrt(var + 1e-05)
+    centred = values - lane_mean(values)
+    return centred * lax.rsqrt(lane_mean(centred * centred) + 1e-05)
 
 
 def gate_of(values):

time: 18.5 us -> 19.7 us (1.065)
  Pallas kernels: 5.94 us -> 7.57 us
  waiting for transfers between devices: 5.32 us -> 4.95 us
    pallas_call x3, Pallas kernels: 5.94 us -> 7.57 us  [call(): pl.pallas_call(body, out_shape=outputs, in_specs=[pl.BlockSpec(memory_spa...]
    ppermute x1, waiting for transfers between devices: 0.76 us -> 0.48 us  [whole_crop_plan(): other = lax.ppermute(mine, 'col', [(0, 1), (1, 0)])]
  transfers between devices with their start and end apart: 5 -> 5, of which waited for: 3 -> 3; matrix products, arithmetic and copies ran while one was open for 0% -> 0% of each run, Pallas kernels for 12% -> 13%
where the time goes in v10:
time: 19.7 us; the launch traced here: 19.6 us
  Pallas kernels  7.57 us (38%)
  starting transfers between devices  6.99 us (35%)
  waiting for transfers between devices  4.95 us (25%)
    pallas_call x3, Pallas kernels, call(): pl.pallas_call(body, out_shape=outputs, in_specs=[pl.BlockSpec(memory_spa...  7.57 us
    ppermute x4, starting transfers between devices, exchange(): return lax.ppermute(block, ('row', 'col'), hops)  6.81 us
    ppermute x4, waiting for transfers between devices, exchange(): return lax.ppermute(block, ('row', 'col'), hops)  4.47 us
    ppermute x1, waiting for transfers between devices, whole_crop_plan(): other = lax.ppermute(mine, 'col', [(0, 1), (1, 0)])  0.48 us
  transfers between devices with their start and end apart: 5, of which 3 were waited for; matrix products, arithmetic and copies ran while one was open for 0% of the time, Pallas kernels for 13%

profile of v10, /device:TPU:0, one launch (start us, length us, event | category | flops | bytes accessed | tf_op | source)
XLA Modules:
  0.0 19.6 jit_solution(3081965980416724194)
XLA Ops:
  0.0 3.5 %collective-permute-start = (f32[4,16,128]{2,1,0:T(8,128)}, f32[4,16,128]{2,1,0:T(8,128)S(1)}, u32[]{:S(2)}, u32[]{:S(2)}) collective-permute-start(f32[4,16,128]{2,1,0:T(8,128)} %refs_0_.1), channel_id=1, source_target_pairs={{0,9},{1,8},{2,11},{3,10},{4,13},{5,12},{6,15},{7,14},{8,1},{9,0},... | collective-permute-start | bytes 98312 | tf_op jit(solution)/shard_map/ppermute | solution.py:285
  3.5 1.6 %own.1 = (f32[4,16,128]{2,1,0:T(8,128)S(1)}, f32[1,128]{1,0:T(1,128)S(1)}, bf16[2,128,512]{2,1,0:T(8,128)(2,1)S(1)}, bf16[2,128,128]{2,1,0:T(8,128)(2,1)S(1)}, b...) custom-call(f32[4,16,128]{2,1,0:T(8,128)} %refs_0_.1, ...), custom_call_target="tpu_custom_call" | custom-call | flops 10485760 | bytes 2097152 | tf_op jit(solution)/shard_map/own/pallas_call | solution.py:289
  5.1 0.5 %collective-permute-done = f32[4,16,128]{2,1,0:T(8,128)S(1)} collective-permute-done((f32[4,16,128]{2,1,0:T(8,128)}, f32[4,16,128]{2,1,0:T(8,128)S(1)}, u32[]{:S(2)}, u32[]{:S(2)}) %collective-permute-start) | collective-permute-done | bytes 32800 | tf_op jit(solution)/shard_map/ppermute | solution.py:285
  5.6 2.7 %collective-permute-start.3 = (f32[2,4,16,128]{3,2,1,0:T(8,128)S(1)}, f32[2,4,16,128]{3,2,1,0:T(8,128)S(1)}, u32[]{:S(2)}, u32[]{:S(2)}) collective-permute-start(f32[2,4,16,128]{3,2,1,0:T(8,128)S(1)} %pad_maximum_fusion), channel_id=1, source_target_pairs={{0,7},{1,6},{2,5},{3,4},{4,3},{5,2},{6,1},{7,0},{8,15},{9,14},{10,... | collective-permute-start | bytes 196616 | tf_op jit(solution)/shard_map/ppermute | solution.py:285
  8.3 0.5 %collective-permute-start.2 = (f32[2,4,16,128]{3,2,1,0:T(8,128)S(1)}, f32[2,4,16,128]{3,2,1,0:T(8,128)S(1)}, u32[]{:S(2)}, u32[]{:S(2)}) collective-permute-start(f32[2,4,16,128]{3,2,1,0:T(8,128)S(1)} %pad_maximum_fusion), channel_id=1, source_target_pairs={{0,5},{1,4},{2,7},{3,6},{4,1},{5,0},{6,3},{7,2},{8,13},{9,12},{10,... | collective-permute-start | bytes 196616 | tf_op jit(solution)/shard_map/ppermute | solution.py:285
  8.7 0.2 collective-permute-start.1
  8.9 4.0 %collective-permute-done.1 = f32[2,4,16,128]{3,2,1,0:T(8,128)S(1)} collective-permute-done((f32[2,4,16,128]{3,2,1,0:T(8,128)S(1)}, f32[2,4,16,128]{3,2,1,0:T(8,128)S(1)}, u32[]{:S(2)}, u32[]{:S(2)}) %collective-permute-start.1) | collective-permute-done | bytes 65568 | tf_op jit(solution)/shard_map/ppermute | solution.py:285
  12.9 0.0 collective-permute-done.2
  12.9 0.0 collective-permute-done.3
  12.9 0.2 collective-permute-start.4
  13.1 0.9 %mine.1 = (f32[2,512,128]{2,1,0:T(8,128)S(1)}, f32[2,512,128]{2,1,0:T(8,128)S(1)}, f32[2,512,128]{2,1,0:T(8,128)S(1)}, f32[2,512,128]{2,1,0:T(8,128)S(1)}) custom-call(f32[8,4,16,128]{3,2,1,0:T(8,128)S(1)} %constant_dynamic-update-slice_fusion.mine, ...), custom_call_target="tpu_custom_call", output_to_operand_aliasing={{0}: (6, {}), {1}: (7, {}), {2}: (8, {}), {3}: (9, {})} | custom-call | flops 83886080 | bytes 2097152 | tf_op jit(solution)/shard_map/mine/pallas_call | solution.py:289
  14.0 0.5 %collective-permute-done.4.other = f32[8,4,16,128]{3,2,1,0:T(8,128)S(1)} collective-permute-done((f32[8,4,16,128]{3,2,1,0:T(8,128)S(1)}, f32[8,4,16,128]{3,2,1,0:T(8,128)S(1)}, u32[]{:S(2)}, u32[]{:S(2)}) %collective-permute-start.4) | collective-permute-done | bytes 262176 | tf_op jit(solution)/shard_map/ppermute | solution.py:337
  14.5 5.1 %crop.1 = (f32[4,16,128]{2,1,0:T(8,128)}, f32[2,512,128]{2,1,0:T(8,128)S(1)}, f32[2,512,128]{2,1,0:T(8,128)S(1)}, f32[2,512,128]{2,1,0:T(8,128)S(1)}, f32[2,512,128]{2,1,0:T(8,128)S(1)}) custom-call(f32[8,4,16,128]{3,2,1,0:T(8,128)S(1)} %collective-permute-done.4.other, ...), custom_call_target="tpu_custom_call", output_to_operand_aliasing={{1}: (7, {}), {2}: (8, {}), {3}: (9, {}), {4}: (10, {})} | custom-call | flops 335544320 | bytes 2097152 | tf_op jit(solution)/shard_map/crop/pallas_call | solution.py:289
  (6 shorter events, 0.0 us)
Async XLA Ops:
  0.0 5.6 %collective-permute-start = (f32[4,16,128]{2,1,0:T(8,128)}, f32[4,16,128]{2,1,0:T(8,128)S(1)}, u32[]{:S(2)}, u32[]{:S(2)}) collective-permute-start(f32[4,16,128]{2,1,0:T(8,128)} %refs_0_.1), channel_id=1, source_target_pairs={{0,9},{1,8},{2,11},{3,10},{4,13},{5,12},{6,15},{7,14},{8,1},{9,0},... | collective-permute-start | bytes 98312 | tf_op jit(solution)/shard_map/ppermute | solution.py:285
  5.6 7.3 %collective-permute-start.3 = (f32[2,4,16,128]{3,2,1,0:T(8,128)S(1)}, f32[2,4,16,128]{3,2,1,0:T(8,128)S(1)}, u32[]{:S(2)}, u32[]{:S(2)}) collective-permute-start(f32[2,4,16,128]{3,2,1,0:T(8,128)S(1)} %pad_maximum_fusion), channel_id=1, source_target_pairs={{0,7},{1,6},{2,5},{3,4},{4,3},{5,2},{6,1},{7,0},{8,15},{9,14},{10,... | collective-permute-start | bytes 196616 | tf_op jit(solution)/shard_map/ppermute | solution.py:285
  8.3 4.6 %collective-permute-start.2 = (f32[2,4,16,128]{3,2,1,0:T(8,128)S(1)}, f32[2,4,16,128]{3,2,1,0:T(8,128)S(1)}, u32[]{:S(2)}, u32[]{:S(2)}) collective-permute-start(f32[2,4,16,128]{3,2,1,0:T(8,128)S(1)} %pad_maximum_fusion), channel_id=1, source_target_pairs={{0,5},{1,4},{2,7},{3,6},{4,1},{5,0},{6,3},{7,2},{8,13},{9,12},{10,... | collective-permute-start | bytes 196616 | tf_op jit(solution)/shard_map/ppermute | solution.py:285
  8.7 4.1 %collective-permute-start.1 = (f32[2,4,16,128]{3,2,1,0:T(8,128)S(1)}, f32[2,4,16,128]{3,2,1,0:T(8,128)S(1)}, u32[]{:S(2)}, u32[]{:S(2)}) collective-permute-start(f32[2,4,16,128]{3,2,1,0:T(8,128)S(1)} %pad_maximum_fusion), channel_id=1, source_target_pairs={{0,3},{1,2},{2,1},{3,0},{4,7},{5,6},{6,5},{7,4},{8,11},{9,10},{10,... | collective-permute-start | bytes 196616 | tf_op jit(solution)/shard_map/ppermute | solution.py:285
  12.9 1.6 %collective-permute-start.4 = (f32[8,4,16,128]{3,2,1,0:T(8,128)S(1)}, f32[8,4,16,128]{3,2,1,0:T(8,128)S(1)}, u32[]{:S(2)}, u32[]{:S(2)}) collective-permute-start(f32[8,4,16,128]{3,2,1,0:T(8,128)S(1)} %constant_dynamic-update-slice_fusion.mine), channel_id=1, source_target_pairs={{0,1},{1,0},{2,3},{3,2},{4,5},{5,4},{6,7},{7,6},{8,9},{9,8},{10,11... | collective-permute-start | bytes 786440 | tf_op jit(solution)/shard_map/ppermute | solution.py:337

commit v11 on v9

--- a/solution.py
+++ b/solution.py
@@ -102,49 +102,45 @@
     out[...] = jnp.broadcast_to(jnp.sum(spread, -1, keepdims=True), (tokens, width))
 
 
-def edges(masks, items, chains, mask, bias, proj_w, gate_w, start, gates, left, right):
+def edges(masks, items, chains, mask, bias, weights, start, gates, left, right):
     rows, cols, width = items[0][2].shape
     tokens = chains.shape[0]
     me = lax.axis_index("row")
     col = lax.axis_index("col")
     bias_v = bias[...]
-    hidden = proj_w.shape[2] // 4
-    for half in range(2):
-        batch = [(slot, block) for slot, h, block in items if h == half]
-        if not batch:
-            continue
-        first = pl.multiple_of((col if half == 0 else 1 - col) * cols, cols)
-        chain_cols = chains[pl.ds(first, cols), :]
-        mask_cols = mask[pl.ds(first, cols), :]
-        states, pmasks = [], []
-        for slot, block in batch:
-            for t in range(rows):
-                token = (me ^ masks[slot]) * rows + t
-                same = chain_cols == chains[pl.ds(token, 1), :]
-                states.append(block[t] + jnp.where(same, bias_v, 0.0))
-                pmasks.append(mask_cols * mask[pl.ds(token, 1), :])
-        state = jnp.concatenate(states, 0)
-        pmask = jnp.concatenate(pmasks, 0)
-        normed = tile_norm(state).astype(jnp.bfloat16)
-        proj = dot(normed, proj_w[0])
-        gate = dot(normed, gate_w[0])
-        lft = rounded(gate_of(proj[:, :hidden]) * proj[:, hidden : 2 * hidden] * pmask)
-        rgt = rounded(gate_of(proj[:, 2 * hidden : 3 * hidden]) * proj[:, 3 * hidden :] * pmask)
-        size = rows * cols
-        for n, (slot, _) in enumerate(batch):
-            span, part = pl.ds(slot * size, size), slice(n * size, (n + 1) * size)
-            start[half, span, :] = state[part]
-            gates[half, span, :] = gate[part]
-            left[half, span, :] = lft[part]
-            for t in range(rows):
-                token = (me ^ masks[slot]) * rows + t
-                at = n * size + t * cols
-                right[half, pl.ds(token, cols, tokens), :] = rgt[at : at + cols]
+    hidden = left.shape[-1]
+    firsts = [pl.multiple_of(each * cols, cols) for each in (col, 1 - col)]
+    chain_cols = [chains[pl.ds(first, cols), :] for first in firsts]
+    mask_cols = [mask[pl.ds(first, cols), :] for first in firsts]
+    states, pmasks = [], []
+    for slot, half, block in items:
+        for t in range(rows):
+            token = (me ^ masks[slot]) * rows + t
+            same = chain_cols[half] == chains[pl.ds(token, 1), :]
+            states.append(block[t] + jnp.where(same, bias_v, 0.0))
+            pmasks.append(mask_cols[half] * mask[pl.ds(token, 1), :])
+    state = jnp.concatenate(states, 0)
+    pmask = jnp.concatenate(pmasks, 0)
+    proj = dot(tile_norm(state).astype(jnp.bfloat16), weights[0])
+    lft = rounded(gate_of(proj[:, :hidden]) * proj[:, hidden : 2 * hidden] * pmask)
+    rgt = rounded(gate_of(proj[:, 2 * hidden : 3 * hidden]) * proj[:, 3 * hidden : 4 * hidden] * pmask)
+    size = rows * cols
+    for n, (slot, half, _) in enumerate(items):
+        span, part = pl.ds(slot * size, size), slice(n * size, (n + 1) * size)
+        start[half, span, :] = state[part]
+        gates[half, span, :] = proj[part, 4 * hidden :]
+        left[half, span, :] = lft[part]
+        for t in range(rows):
+            token = (me ^ masks[slot]) * rows + t
+            at = n * size + t * cols
+            right[half, pl.ds(token, cols, tokens), :] = rgt[at : at + cols]
 
 
 def own_kernel(masks, *refs):
     sources, rest = refs[:7], refs[7:]
-    pair, bias, proj_w, gate_w, out_w, chains, mask, start, gates, left, right, chains_v, mask_v, sems = rest
+    pair, bias, weights, out_w, chains, mask, start, gates, left, right, chains_v, mask_v, sems = rest
+    split = sources[2].shape[-1]
+    proj_w, gate_w = weights.at[:, :, pl.ds(0, split)], weights.at[:, :, pl.ds(split, weights.shape[-1] - split)]
     loads = []
     for n, (source, target) in enumerate(zip(sources, (pair, bias, proj_w, gate_w, out_w, chains_v, mask_v))):
         loads.append(pltpu.make_async_copy(source, target, sems.at[n]))
@@ -154,12 +150,12 @@
         load.wait()
     table(chains_v, chains)
     table(mask_v, mask)
-    edges(masks, [(0, 0, pair[...])], chains, mask, bias, proj_w, gate_w, start, gates, left, right)
-
-
-def mine_kernel(masks, halves, mine, chains, mask, bias, proj_w, gate_w, s_in, g_in, l_in, r_in, *outs):
+    edges(masks, [(0, 0, pair[...])], chains, mask, bias, weights, start, gates, left, right)
+
+
+def mine_kernel(masks, halves, mine, chains, mask, bias, weights, s_in, g_in, l_in, r_in, *outs):
     items = [(slot, halves[slot], mine[slot]) for slot in range(1, len(masks))]
-    edges(masks, items, chains, mask, bias, proj_w, gate_w, *outs)
+    edges(masks, items, chains, mask, bias, weights, *outs)
 
 
 def crop_kernel(
@@ -169,8 +165,7 @@
     chains,
     mask,
     bias,
-    proj_w,
-    gate_w,
+    weights,
     out_w,
     start_in,
     gates_in,
@@ -189,9 +184,9 @@
     tokens = ranks * rows
     me = lax.axis_index("row")
     col = lax.axis_index("col")
-    hidden = proj_w.shape[2] // 4
+    hidden = left.shape[-1]
     items = [(slot, 1 - halves[slot], other[slot]) for slot in range(ranks)]
-    edges(masks, items, chains, mask, bias, proj_w, gate_w, start, gates, left, right)
+    edges(masks, items, chains, mask, bias, weights, start, gates, left, right)
 
     low = me * rows // 8 * 8
     groups = [col * cols + 8 * n for n in range(cols // 8)] + [low]
@@ -212,7 +207,7 @@
                         acc[k][n] = term if half + l == 0 else acc[k][n] + term
         for n in range(count):
             for k in range(block):
-                tris[n, pl.ds(pl.multiple_of((k0 + k) * 8, 8), 8), :] = acc[k][n]
+                tris[pl.ds(pl.multiple_of((n * tokens + k0 + k) * 8, 8), 8), :] = acc[k][n]
         return carry
 
     lax.fori_loop(0, tokens // block, tri_block, 0)
@@ -227,50 +222,43 @@
             return values[0, pl.ds(k * cols + 8 * n, 8), :]
         return values[low_half, pl.ds(pl.multiple_of(k * cols + low_off, 8), 8), :]
 
-    def updated_state(n):
-        tri = tris[n]
-        tnorm = tile_norm(tri).astype(jnp.bfloat16)
-        gate = gate_of(jnp.concatenate([gather(gates, n, k) for k in range(tokens)], 0))
-        state = jnp.concatenate([gather(start, n, k) for k in range(tokens)], 0)
-        return state + gate * dot(tnorm, out_w[0])
-
     row_masks = []
     for slot in range(ranks):
         for t in range(rows):
             row_masks.append(mask[pl.ds((me ^ masks[slot]) * rows + t, 1), :])
 
-    normed = tile_norm(updated_state(count - 1)).astype(jnp.bfloat16)
-    proj = dot(normed, proj_w[1, :, : 2 * hidden])
-    edge = gate_of(proj[:, :hidden]) * proj[:, hidden:]
+    cells = [(n, k) for n in range(count) for k in range(tokens)]
+    tnorm = tile_norm(tris[...]).astype(jnp.bfloat16)
+    gate = gate_of(jnp.concatenate([gather(gates, n, k) for n, k in cells], 0))
+    state = jnp.concatenate([gather(start, n, k) for n, k in cells], 0)
+    state = state + gate * dot(tnorm, out_w[0])
+    normed = tile_norm(state).astype(jnp.bfloat16)
+    edge_rows = (count - 1) * tokens * 8
+    proj_r = dot(normed[:edge_rows], weights[1, :, 2 * hidden : 4 * hidden])
+    proj_l = dot(normed[edge_rows:], weights[1, :, : 2 * hidden])
+    own = [slice(n * tokens * 8, n * tokens * 8 + rows * 8) for n in range(count - 1)]
+    own_state = jnp.concatenate([state[part] for part in own], 0)
+    own_logit = dot(jnp.concatenate([normed[part] for part in own], 0), weights[1, :, 4 * hidden :])
     pm = jnp.concatenate([mask_left * m for m in row_masks], 0)
-    left1[...] = rounded(edge * pm)
-
-    own_state, own_logits = [], []
+    left1[...] = rounded(gate_of(proj_l[:, :hidden]) * proj_l[:, hidden:] * pm)
+    pm = jnp.concatenate([mask_right[8 * n : 8 * n + 8] * m for n in range(count - 1) for m in row_masks], 0)
+    right1[...] = rounded(gate_of(proj_r[:, :hidden]) * proj_r[:, hidden:] * pm)
+
+    shift = lax.rem(me * rows, 8)
+    acc = [[None] * rows for _ in range(count - 1)]
+    for k in range(tokens):
+        for n in range(count - 1):
+            cell = right1[pl.ds((n * tokens + k) * 8, 8), :]
+            for t in range(rows):
+                term = left1[pl.ds(k * 8 + shift + t, 1), :] * cell
+                acc[n][t] = term if k == 0 else acc[n][t] + term
+    tri = jnp.concatenate([acc[n][t] for n in range(count - 1) for t in range(rows)], 0)
+    tnorm = tile_norm(tri).astype(jnp.bfloat16)
+    out = own_state + gate_of(own_logit) * dot(tnorm, out_w[1])
     for n in range(count - 1):
-        state = updated_state(n)
-        normed = tile_norm(state).astype(jnp.bfloat16)
-        own_state.append(state[: rows * 8])
-        own_logits.append(dot(normed[: rows * 8], gate_w[1]))
-        proj = dot(normed, proj_w[1, :, 2 * hidden :])
-        edge = gate_of(proj[:, :hidden]) * proj[:, hidden:]
-        pm = jnp.concatenate([mask_right[8 * n : 8 * n + 8] * m for m in row_masks], 0)
-        right1[n] = rounded(edge * pm)
-
-    shift = lax.rem(me * rows, 8)
-    acc = [[None] * (count - 1) for _ in range(rows)]
-    for k in range(tokens):
-        cells = [right1[n, pl.ds(k * 8, 8), :] for n in range(count - 1)]
         for t in range(rows):
-            row = left1[pl.ds(k * 8 + shift + t, 1), :]
-            for n in range(count - 1):
-                term = row * cells[n]
-                acc[t][n] = term if k == 0 else acc[t][n] + term
-    for n in range(count - 1):
-        tri = jnp.concatenate([acc[t][n] for t in range(rows)], 0)
-        tnorm = tile_norm(tri).astype(jnp.bfloat16)
-        out = own_state[n] + gate_of(own_logits[n]) * dot(tnorm, out_w[1])
-        for t in range(rows):
-            updated[t, pl.ds(8 * n, 8), :] = out[8 * t : 8 * t + 8]
+            at = (n * rows + t) * 8
+            updated[t, pl.ds(8 * n, 8), :] = out[at : at + 8]
 
 
 def exchange(block, bits):
@@ -317,10 +305,11 @@
         halves += [1, 0]
     far = exchange(pair, top)
     loaded = (pair, bias, proj_weight, gate_weight, out_weight, chains[None, :], token_mask[None, :])
-    own, bias, proj_weight, gate_weight, out_weight, chains_t, mask_t, *partial = call(
+    joined = jax.ShapeDtypeStruct((2, width, 4 * hidden + width), proj_weight.dtype)
+    own, bias, weights, out_weight, chains_t, mask_t, *partial = call(
         functools.partial(own_kernel, masks),
         [pltpu.with_memory_space_constraint(each, pltpu.HBM) for each in loaded],
-        like(*loaded[:5]) + floats((tokens, width), (tokens, width)) + half,
+        like(pair, bias) + [joined] + like(out_weight) + floats((tokens, width), (tokens, width)) + half,
         [pltpu.VMEM((1, tokens), jnp.int32), pltpu.VMEM((1, tokens), jnp.int32), pltpu.SemaphoreType.DMA((7,))],
         "own",
         flops // ranks,
@@ -329,7 +318,7 @@
     two = jnp.stack([own, far])
     mine = jnp.concatenate([two] + [exchange(two, bits) for bits in range(1, top)], 0)
     other = lax.ppermute(mine, "col", [(0, 1), (1, 0)])
-    edge_inputs = (chains_t, mask_t, bias, proj_weight, gate_weight)
+    edge_inputs = (chains_t, mask_t, bias, weights)
     partial = call(
         functools.partial(mine_kernel, masks, halves),
         (mine, *edge_inputs, *partial),
@@ -337,10 +326,10 @@
         [],
         "mine",
         flops,
-        {n + 6: n for n in range(4)},
+        {n + 5: n for n in range(4)},
     )
     groups = cols // 8 + 1
-    extra = [(groups, tokens * 8, hidden), (tokens * 8, hidden), (groups - 1, tokens * 8, hidden)]
+    extra = [(groups * tokens * 8, hidden), (tokens * 8, hidden), ((groups - 1) * tokens * 8, hidden)]
     return call(
         functools.partial(crop_kernel, masks, halves),
         (other, *edge_inputs, out_weight, *partial),
@@ -348,7 +337,7 @@
         [pltpu.VMEM(each.shape, jnp.float32) for each in floats(*extra)],
         "crop",
         4 * flops,
-        {n + 7: n + 1 for n in range(4)},
+        {n + 6: n + 1 for n in range(4)},
     )[0]
 
 

time: 18.5 us -> 18.2 us (0.984)
  Pallas kernels: 5.94 us -> 5.66 us
    pallas_call x3, Pallas kernels: 5.94 us -> 5.66 us  [call(): pl.pallas_call(body, out_shape=outputs, in_specs=[pl.BlockSpec(memory_spa...]
  transfers between devices with their start and end apart: 5 -> 5, of which waited for: 3 -> 3; matrix products, arithmetic and copies ran while one was open for 0% -> 0% of each run, Pallas kernels for 12% -> 11%
where the time goes in v11:
time: 18.2 us; the launch traced here: 18.1 us
  starting transfers between devices  6.99 us (38%)
  Pallas kernels  5.66 us (31%)
  waiting for transfers between devices  5.37 us (30%)
    ppermute x4, starting transfers between devices, exchange(): return lax.ppermute(block, ('row', 'col'), hops)  6.81 us
    pallas_call x3, Pallas kernels, call(): pl.pallas_call(body, out_shape=outputs, in_specs=[pl.BlockSpec(memory_spa...  5.66 us
    ppermute x4, waiting for transfers between devices, exchange(): return lax.ppermute(block, ('row', 'col'), hops)  4.56 us
    ppermute x1, waiting for transfers between devices, whole_crop_plan(): other = lax.ppermute(mine, 'col', [(0, 1), (1, 0)])  0.81 us
  transfers between devices with their start and end apart: 5, of which 3 were waited for; matrix products, arithmetic and copies ran while one was open for 0% of the time, Pallas kernels for 11%

profile of v11, /device:TPU:0, one launch (start us, length us, event | category | flops | bytes accessed | tf_op | source)
XLA Modules:
  0.0 18.1 jit_solution(2627262009760239650)
XLA Ops:
  0.0 3.5 %collective-permute-start = (f32[4,16,128]{2,1,0:T(8,128)}, f32[4,16,128]{2,1,0:T(8,128)S(1)}, u32[]{:S(2)}, u32[]{:S(2)}) collective-permute-start(f32[4,16,128]{2,1,0:T(8,128)} %refs_0_.1), channel_id=1, source_target_pairs={{0,9},{1,8},{2,11},{3,10},{4,13},{5,12},{6,15},{7,14},{8,1},{9,0},... | collective-permute-start | bytes 98312 | tf_op jit(solution)/shard_map/ppermute | solution.py:267
  3.5 1.5 %own.1 = (f32[4,16,128]{2,1,0:T(8,128)S(1)}, f32[1,128]{1,0:T(1,128)S(1)}, bf16[2,128,640]{2,1,0:T(8,128)(2,1)S(1)}, bf16[2,128,128]{2,1,0:T(8,128)(2,1)S(1)}, f...) custom-call(f32[4,16,128]{2,1,0:T(8,128)} %refs_0_.1, ...), custom_call_target="tpu_custom_call" | custom-call | flops 10485760 | bytes 2097152 | tf_op jit(solution)/shard_map/own/pallas_call | solution.py:271
  5.0 0.6 %collective-permute-done = f32[4,16,128]{2,1,0:T(8,128)S(1)} collective-permute-done((f32[4,16,128]{2,1,0:T(8,128)}, f32[4,16,128]{2,1,0:T(8,128)S(1)}, u32[]{:S(2)}, u32[]{:S(2)}) %collective-permute-start) | collective-permute-done | bytes 32800 | tf_op jit(solution)/shard_map/ppermute | solution.py:267
  5.6 2.7 %collective-permute-start.3 = (f32[2,4,16,128]{3,2,1,0:T(8,128)S(1)}, f32[2,4,16,128]{3,2,1,0:T(8,128)S(1)}, u32[]{:S(2)}, u32[]{:S(2)}) collective-permute-start(f32[2,4,16,128]{3,2,1,0:T(8,128)S(1)} %pad_maximum_fusion), channel_id=1, source_target_pairs={{0,7},{1,6},{2,5},{3,4},{4,3},{5,2},{6,1},{7,0},{8,15},{9,14},{10,... | collective-permute-start | bytes 196616 | tf_op jit(solution)/shard_map/ppermute | solution.py:267
  8.3 0.5 %collective-permute-start.2 = (f32[2,4,16,128]{3,2,1,0:T(8,128)S(1)}, f32[2,4,16,128]{3,2,1,0:T(8,128)S(1)}, u32[]{:S(2)}, u32[]{:S(2)}) collective-permute-start(f32[2,4,16,128]{3,2,1,0:T(8,128)S(1)} %pad_maximum_fusion), channel_id=1, source_target_pairs={{0,5},{1,4},{2,7},{3,6},{4,1},{5,0},{6,3},{7,2},{8,13},{9,12},{10,... | collective-permute-start | bytes 196616 | tf_op jit(solution)/shard_map/ppermute | solution.py:267
  8.7 0.2 collective-permute-start.1
  8.9 4.0 %collective-permute-done.1 = f32[2,4,16,128]{3,2,1,0:T(8,128)S(1)} collective-permute-done((f32[2,4,16,128]{3,2,1,0:T(8,128)S(1)}, f32[2,4,16,128]{3,2,1,0:T(8,128)S(1)}, u32[]{:S(2)}, u32[]{:S(2)}) %collective-permute-start.1) | collective-permute-done | bytes 65568 | tf_op jit(solution)/shard_map/ppermute | solution.py:267
  12.9 0.0 collective-permute-done.2
  12.9 0.0 collective-permute-done.3
  12.9 0.2 collective-permute-start.4
  13.1 0.6 %mine.1 = (f32[2,512,128]{2,1,0:T(8,128)S(1)}, f32[2,512,128]{2,1,0:T(8,128)S(1)}, f32[2,512,128]{2,1,0:T(8,128)S(1)}, f32[2,512,128]{2,1,0:T(8,128)S(1)}) custom-call(f32[8,4,16,128]{3,2,1,0:T(8,128)S(1)} %constant_dynamic-update-slice_fusion.mine, ...), custom_call_target="tpu_custom_call", output_to_operand_aliasing={{0}: (5, {}), {1}: (6, {}), {2}: (7, {}), {3}: (8, {})} | custom-call | flops 83886080 | bytes 2097152 | tf_op jit(solution)/shard_map/mine/pallas_call | solution.py:271
  13.7 0.8 %collective-permute-done.4.other = f32[8,4,16,128]{3,2,1,0:T(8,128)S(1)} collective-permute-done((f32[8,4,16,128]{3,2,1,0:T(8,128)S(1)}, f32[8,4,16,128]{3,2,1,0:T(8,128)S(1)}, u32[]{:S(2)}, u32[]{:S(2)}) %collective-permute-start.4) | collective-permute-done | bytes 262176 | tf_op jit(solution)/shard_map/ppermute | solution.py:320
  14.5 3.6 %crop.1 = (f32[4,16,128]{2,1,0:T(8,128)}, f32[2,512,128]{2,1,0:T(8,128)S(1)}, f32[2,512,128]{2,1,0:T(8,128)S(1)}, f32[2,512,128]{2,1,0:T(8,128)S(1)}, f32[2,512,128]{2,1,0:T(8,128)S(1)}) custom-call(f32[8,4,16,128]{3,2,1,0:T(8,128)S(1)} %collective-permute-done.4.other, ...), custom_call_target="tpu_custom_call", output_to_operand_aliasing={{1}: (6, {}), {2}: (7, {}), {3}: (8, {}), {4}: (9, {})} | custom-call | flops 335544320 | bytes 2097152 | tf_op jit(solution)/shard_map/crop/pallas_call | solution.py:271
  (6 shorter events, 0.0 us)
Async XLA Ops:
  0.0 5.6 %collective-permute-start = (f32[4,16,128]{2,1,0:T(8,128)}, f32[4,16,128]{2,1,0:T(8,128)S(1)}, u32[]{:S(2)}, u32[]{:S(2)}) collective-permute-start(f32[4,16,128]{2,1,0:T(8,128)} %refs_0_.1), channel_id=1, source_target_pairs={{0,9},{1,8},{2,11},{3,10},{4,13},{5,12},{6,15},{7,14},{8,1},{9,0},... | collective-permute-start | bytes 98312 | tf_op jit(solution)/shard_map/ppermute | solution.py:267
  5.6 7.3 %collective-permute-start.3 = (f32[2,4,16,128]{3,2,1,0:T(8,128)S(1)}, f32[2,4,16,128]{3,2,1,0:T(8,128)S(1)}, u32[]{:S(2)}, u32[]{:S(2)}) collective-permute-start(f32[2,4,16,128]{3,2,1,0:T(8,128)S(1)} %pad_maximum_fusion), channel_id=1, source_target_pairs={{0,7},{1,6},{2,5},{3,4},{4,3},{5,2},{6,1},{7,0},{8,15},{9,14},{10,... | collective-permute-start | bytes 196616 | tf_op jit(solution)/shard_map/ppermute | solution.py:267
  8.3 4.6 %collective-permute-start.2 = (f32[2,4,16,128]{3,2,1,0:T(8,128)S(1)}, f32[2,4,16,128]{3,2,1,0:T(8,128)S(1)}, u32[]{:S(2)}, u32[]{:S(2)}) collective-permute-start(f32[2,4,16,128]{3,2,1,0:T(8,128)S(1)} %pad_maximum_fusion), channel_id=1, source_target_pairs={{0,5},{1,4},{2,7},{3,6},{4,1},{5,0},{6,3},{7,2},{8,13},{9,12},{10,... | collective-permute-start | bytes 196616 | tf_op jit(solution)/shard_map/ppermute | solution.py:267
  8.7 4.1 %collective-permute-start.1 = (f32[2,4,16,128]{3,2,1,0:T(8,128)S(1)}, f32[2,4,16,128]{3,2,1,0:T(8,128)S(1)}, u32[]{:S(2)}, u32[]{:S(2)}) collective-permute-start(f32[2,4,16,128]{3,2,1,0:T(8,128)S(1)} %pad_maximum_fusion), channel_id=1, source_target_pairs={{0,3},{1,2},{2,1},{3,0},{4,7},{5,6},{6,5},{7,4},{8,11},{9,10},{10,... | collective-permute-start | bytes 196616 | tf_op jit(solution)/shard_map/ppermute | solution.py:267
  12.9 1.6 %collective-permute-start.4 = (f32[8,4,16,128]{3,2,1,0:T(8,128)S(1)}, f32[8,4,16,128]{3,2,1,0:T(8,128)S(1)}, u32[]{:S(2)}, u32[]{:S(2)}) collective-permute-start(f32[8,4,16,128]{3,2,1,0:T(8,128)S(1)} %constant_dynamic-update-slice_fusion.mine), channel_id=1, source_target_pairs={{0,1},{1,0},{2,3},{3,2},{4,5},{5,4},{6,7},{7,6},{8,9},{9,8},{10,11... | collective-permute-start | bytes 786440 | tf_op jit(solution)/shard_map/ppermute | solution.py:320

commit v12 on v11

--- a/solution.py
+++ b/solution.py
@@ -129,10 +129,10 @@
         span, part = pl.ds(slot * size, size), slice(n * size, (n + 1) * size)
         start[half, span, :] = state[part]
         gates[half, span, :] = proj[part, 4 * hidden :]
-        left[half, span, :] = lft[part]
         for t in range(rows):
             token = (me ^ masks[slot]) * rows + t
             at = n * size + t * cols
+            left[half, slot * rows + t] = lft[at : at + cols]
             right[half, pl.ds(token, cols, tokens), :] = rgt[at : at + cols]
 
 
@@ -201,7 +201,7 @@
             for l in range(cols):
                 cells = [right[half, pl.ds(pl.multiple_of(l * tokens + g, 8), 8), :] for g in groups]
                 for k in range(block):
-                    row = left[half, pl.ds((k0 + k) * cols + l, 1), :]
+                    row = left[half, k0 + k, pl.ds(l, 1), :]
                     for n in range(count):
                         term = row * cells[n]
                         acc[k][n] = term if half + l == 0 else acc[k][n] + term
@@ -295,7 +295,7 @@
     tokens = token_mask.shape[0]
     hidden = proj_weight.shape[2] // 4
     bias = chain_bias[None, :]
-    half = [(2, tokens * cols, width), (2, tokens * cols, width), (2, tokens * cols, hidden), (2, tokens * cols, hidden)]
+    half = [(2, tokens * cols, width), (2, tokens * cols, width), (2, tokens, cols, hidden), (2, tokens * cols, hidden)]
     half = floats(*half)
     flops = 2 * tokens * cols * width * 5 * hidden
     top = ranks // 2

time: 18.2 us -> 18.2 us (level)
  no operation moved by 1% of the time
where the time goes in v12:
time: 18.2 us; the launch traced here: 18.1 us
  starting transfers between devices  6.99 us (38%)
  Pallas kernels  5.66 us (31%)
  waiting for transfers between devices  5.37 us (30%)
    ppermute x4, starting transfers between devices, exchange(): return lax.ppermute(block, ('row', 'col'), hops)  6.81 us
    pallas_call x3, Pallas kernels, call(): pl.pallas_call(body, out_shape=outputs, in_specs=[pl.BlockSpec(memory_spa...  5.66 us
    ppermute x4, waiting for transfers between devices, exchange(): return lax.ppermute(block, ('row', 'col'), hops)  4.56 us
    ppermute x1, waiting for transfers between devices, whole_crop_plan(): other = lax.ppermute(mine, 'col', [(0, 1), (1, 0)])  0.81 us
  transfers between devices with their start and end apart: 5, of which 3 were waited for; matrix products, arithmetic and copies ran while one was open for 0% of the time, Pallas kernels for 11%

profile of v12, /device:TPU:0, one launch (start us, length us, event | category | flops | bytes accessed | tf_op | source)
XLA Modules:
  0.0 18.1 jit_solution(2627262009760239650)
XLA Ops:
  0.0 3.5 %collective-permute-start = (f32[4,16,128]{2,1,0:T(8,128)}, f32[4,16,128]{2,1,0:T(8,128)S(1)}, u32[]{:S(2)}, u32[]{:S(2)}) collective-permute-start(f32[4,16,128]{2,1,0:T(8,128)} %refs_0_.1), channel_id=1, source_target_pairs={{0,9},{1,8},{2,11},{3,10},{4,13},{5,12},{6,15},{7,14},{8,1},{9,0},... | collective-permute-start | bytes 98312 | tf_op jit(solution)/shard_map/ppermute | solution.py:267
  3.5 1.5 %own.1 = (f32[4,16,128]{2,1,0:T(8,128)S(1)}, f32[1,128]{1,0:T(1,128)S(1)}, bf16[2,128,640]{2,1,0:T(8,128)(2,1)S(1)}, bf16[2,128,128]{2,1,0:T(8,128)(2,1)S(1)}, f...) custom-call(f32[4,16,128]{2,1,0:T(8,128)} %refs_0_.1, ...), custom_call_target="tpu_custom_call" | custom-call | flops 10485760 | bytes 2097152 | tf_op jit(solution)/shard_map/own/pallas_call | solution.py:271
  5.0 0.6 %collective-permute-done = f32[4,16,128]{2,1,0:T(8,128)S(1)} collective-permute-done((f32[4,16,128]{2,1,0:T(8,128)}, f32[4,16,128]{2,1,0:T(8,128)S(1)}, u32[]{:S(2)}, u32[]{:S(2)}) %collective-permute-start) | collective-permute-done | bytes 32800 | tf_op jit(solution)/shard_map/ppermute | solution.py:267
  5.6 2.7 %collective-permute-start.3 = (f32[2,4,16,128]{3,2,1,0:T(8,128)S(1)}, f32[2,4,16,128]{3,2,1,0:T(8,128)S(1)}, u32[]{:S(2)}, u32[]{:S(2)}) collective-permute-start(f32[2,4,16,128]{3,2,1,0:T(8,128)S(1)} %pad_maximum_fusion), channel_id=1, source_target_pairs={{0,7},{1,6},{2,5},{3,4},{4,3},{5,2},{6,1},{7,0},{8,15},{9,14},{10,... | collective-permute-start | bytes 196616 | tf_op jit(solution)/shard_map/ppermute | solution.py:267
  8.3 0.5 %collective-permute-start.2 = (f32[2,4,16,128]{3,2,1,0:T(8,128)S(1)}, f32[2,4,16,128]{3,2,1,0:T(8,128)S(1)}, u32[]{:S(2)}, u32[]{:S(2)}) collective-permute-start(f32[2,4,16,128]{3,2,1,0:T(8,128)S(1)} %pad_maximum_fusion), channel_id=1, source_target_pairs={{0,5},{1,4},{2,7},{3,6},{4,1},{5,0},{6,3},{7,2},{8,13},{9,12},{10,... | collective-permute-start | bytes 196616 | tf_op jit(solution)/shard_map/ppermute | solution.py:267
  8.7 0.2 collective-permute-start.1
  8.9 4.0 %collective-permute-done.1 = f32[2,4,16,128]{3,2,1,0:T(8,128)S(1)} collective-permute-done((f32[2,4,16,128]{3,2,1,0:T(8,128)S(1)}, f32[2,4,16,128]{3,2,1,0:T(8,128)S(1)}, u32[]{:S(2)}, u32[]{:S(2)}) %collective-permute-start.1) | collective-permute-done | bytes 65568 | tf_op jit(solution)/shard_map/ppermute | solution.py:267
  12.9 0.0 collective-permute-done.2
  12.9 0.0 collective-permute-done.3
  12.9 0.2 collective-permute-start.4
  13.1 0.6 %mine.1 = (f32[2,512,128]{2,1,0:T(8,128)S(1)}, f32[2,512,128]{2,1,0:T(8,128)S(1)}, f32[2,32,16,128]{3,2,1,0:T(8,128)S(1)}, f32[2,512,128]{2,1,0:T(8,128)S(1)}) custom-call(f32[8,4,16,128]{3,2,1,0:T(8,128)S(1)} %constant_dynamic-update-slice_fusion.mine, ...), custom_call_target="tpu_custom_call", output_to_operand_aliasing={{0}: (5, {}), {1}: (6, {}), {2}: (7, {}), {3}: (8, {})} | custom-call | flops 83886080 | bytes 2097152 | tf_op jit(solution)/shard_map/mine/pallas_call | solution.py:271
  13.7 0.8 %collective-permute-done.4.other = f32[8,4,16,128]{3,2,1,0:T(8,128)S(1)} collective-permute-done((f32[8,4,16,128]{3,2,1,0:T(8,128)S(1)}, f32[8,4,16,128]{3,2,1,0:T(8,128)S(1)}, u32[]{:S(2)}, u32[]{:S(2)}) %collective-permute-start.4) | collective-permute-done | bytes 262176 | tf_op jit(solution)/shard_map/ppermute | solution.py:320
  14.5 3.6 %crop.1 = (f32[4,16,128]{2,1,0:T(8,128)}, f32[2,512,128]{2,1,0:T(8,128)S(1)}, f32[2,512,128]{2,1,0:T(8,128)S(1)}, f32[2,32,16,128]{3,2,1,0:T(8,128)S(1)}, f32[2,512,128]{2,1,0:T(8,128)S(1)}) custom-call(f32[8,4,16,128]{3,2,1,0:T(8,128)S(1)} %collective-permute-done.4.other, ...), custom_call_target="tpu_custom_call", output_to_operand_aliasing={{1}: (6, {}), {2}: (7, {}), {3}: (8, {}), {4}: (9, {})} | custom-call | flops 335544320 | bytes 2097152 | tf_op jit(solution)/shard_map/crop/pallas_call | solution.py:271
  (6 shorter events, 0.0 us)
Async XLA Ops:
  0.0 5.6 %collective-permute-start = (f32[4,16,128]{2,1,0:T(8,128)}, f32[4,16,128]{2,1,0:T(8,128)S(1)}, u32[]{:S(2)}, u32[]{:S(2)}) collective-permute-start(f32[4,16,128]{2,1,0:T(8,128)} %refs_0_.1), channel_id=1, source_target_pairs={{0,9},{1,8},{2,11},{3,10},{4,13},{5,12},{6,15},{7,14},{8,1},{9,0},... | collective-permute-start | bytes 98312 | tf_op jit(solution)/shard_map/ppermute | solution.py:267
  5.6 7.3 %collective-permute-start.3 = (f32[2,4,16,128]{3,2,1,0:T(8,128)S(1)}, f32[2,4,16,128]{3,2,1,0:T(8,128)S(1)}, u32[]{:S(2)}, u32[]{:S(2)}) collective-permute-start(f32[2,4,16,128]{3,2,1,0:T(8,128)S(1)} %pad_maximum_fusion), channel_id=1, source_target_pairs={{0,7},{1,6},{2,5},{3,4},{4,3},{5,2},{6,1},{7,0},{8,15},{9,14},{10,... | collective-permute-start | bytes 196616 | tf_op jit(solution)/shard_map/ppermute | solution.py:267
  8.3 4.6 %collective-permute-start.2 = (f32[2,4,16,128]{3,2,1,0:T(8,128)S(1)}, f32[2,4,16,128]{3,2,1,0:T(8,128)S(1)}, u32[]{:S(2)}, u32[]{:S(2)}) collective-permute-start(f32[2,4,16,128]{3,2,1,0:T(8,128)S(1)} %pad_maximum_fusion), channel_id=1, source_target_pairs={{0,5},{1,4},{2,7},{3,6},{4,1},{5,0},{6,3},{7,2},{8,13},{9,12},{10,... | collective-permute-start | bytes 196616 | tf_op jit(solution)/shard_map/ppermute | solution.py:267
  8.7 4.1 %collective-permute-start.1 = (f32[2,4,16,128]{3,2,1,0:T(8,128)S(1)}, f32[2,4,16,128]{3,2,1,0:T(8,128)S(1)}, u32[]{:S(2)}, u32[]{:S(2)}) collective-permute-start(f32[2,4,16,128]{3,2,1,0:T(8,128)S(1)} %pad_maximum_fusion), channel_id=1, source_target_pairs={{0,3},{1,2},{2,1},{3,0},{4,7},{5,6},{6,5},{7,4},{8,11},{9,10},{10,... | collective-permute-start | bytes 196616 | tf_op jit(solution)/shard_map/ppermute | solution.py:267
  12.9 1.6 %collective-permute-start.4 = (f32[8,4,16,128]{3,2,1,0:T(8,128)S(1)}, f32[8,4,16,128]{3,2,1,0:T(8,128)S(1)}, u32[]{:S(2)}, u32[]{:S(2)}) collective-permute-start(f32[8,4,16,128]{3,2,1,0:T(8,128)S(1)} %constant_dynamic-update-slice_fusion.mine), channel_id=1, source_target_pairs={{0,1},{1,0},{2,3},{3,2},{4,5},{5,4},{6,7},{7,6},{8,9},{9,8},{10,11... | collective-permute-start | bytes 786440 | tf_op jit(solution)/shard_map/ppermute | solution.py:320

commit v13 on v12

--- a/solution.py
+++ b/solution.py
@@ -136,9 +136,9 @@
             right[half, pl.ds(token, cols, tokens), :] = rgt[at : at + cols]
 
 
-def own_kernel(masks, *refs):
+def prep_kernel(*refs):
     sources, rest = refs[:7], refs[7:]
-    pair, bias, weights, out_w, chains, mask, start, gates, left, right, chains_v, mask_v, sems = rest
+    pair, bias, weights, out_w, chains, mask, chains_v, mask_v, sems = rest
     split = sources[2].shape[-1]
     proj_w, gate_w = weights.at[:, :, pl.ds(0, split)], weights.at[:, :, pl.ds(split, weights.shape[-1] - split)]
     loads = []
@@ -150,11 +150,10 @@
         load.wait()
     table(chains_v, chains)
     table(mask_v, mask)
-    edges(masks, [(0, 0, pair[...])], chains, mask, bias, weights, start, gates, left, right)
-
-
-def mine_kernel(masks, halves, mine, chains, mask, bias, weights, s_in, g_in, l_in, r_in, *outs):
-    items = [(slot, halves[slot], mine[slot]) for slot in range(1, len(masks))]
+
+
+def mine_kernel(masks, halves, mine, chains, mask, bias, weights, *outs):
+    items = [(slot, halves[slot], mine[slot]) for slot in range(len(masks))]
     edges(masks, items, chains, mask, bias, weights, *outs)
 
 
@@ -306,27 +305,34 @@
     far = exchange(pair, top)
     loaded = (pair, bias, proj_weight, gate_weight, out_weight, chains[None, :], token_mask[None, :])
     joined = jax.ShapeDtypeStruct((2, width, 4 * hidden + width), proj_weight.dtype)
-    own, bias, weights, out_weight, chains_t, mask_t, *partial = call(
-        functools.partial(own_kernel, masks),
+    own, bias, weights, out_weight, chains_t, mask_t = call(
+        prep_kernel,
         [pltpu.with_memory_space_constraint(each, pltpu.HBM) for each in loaded],
-        like(pair, bias) + [joined] + like(out_weight) + floats((tokens, width), (tokens, width)) + half,
+        like(pair, bias) + [joined] + like(out_weight) + floats((tokens, width), (tokens, width)),
         [pltpu.VMEM((1, tokens), jnp.int32), pltpu.VMEM((1, tokens), jnp.int32), pltpu.SemaphoreType.DMA((7,))],
-        "own",
+        "prep",
         flops // ranks,
         space=pltpu.HBM,
     )
+    near = [bits for bits in range(1, top) if bits & (bits - 1) == 0]
+    sent = {bits: exchange(own, bits) for bits in near}
     two = jnp.stack([own, far])
-    mine = jnp.concatenate([two] + [exchange(two, bits) for bits in range(1, top)], 0)
+    parts = [own[None], far[None]]
+    for bits in range(1, top):
+        if bits in sent:
+            parts += [sent[bits][None], exchange(far, bits)[None]]
+        else:
+            parts.append(exchange(two, bits))
+    mine = jnp.concatenate(parts, 0)
     other = lax.ppermute(mine, "col", [(0, 1), (1, 0)])
     edge_inputs = (chains_t, mask_t, bias, weights)
     partial = call(
         functools.partial(mine_kernel, masks, halves),
-        (mine, *edge_inputs, *partial),
+        (mine, *edge_inputs),
         half,
         [],
         "mine",
         flops,
-        {n + 5: n for n in range(4)},
     )
     groups = cols // 8 + 1
     extra = [(groups * tokens * 8, hidden), (tokens * 8, hidden), ((groups - 1) * tokens * 8, hidden)]

time: 18.2 us -> 18.8 us (1.033)
  starting transfers between devices: 6.99 us -> 10.1 us
  waiting for transfers between devices: 5.37 us -> 3.04 us
  Pallas kernels: 5.66 us -> 5.38 us
    ppermute x4 -> x6, starting transfers between devices: 6.81 us -> 9.91 us  [exchange(): return lax.ppermute(block, ('row', 'col'), hops)]
    ppermute x4 -> x6, waiting for transfers between devices: 4.56 us -> 2.33 us  [exchange(): return lax.ppermute(block, ('row', 'col'), hops)]
    pallas_call x3, Pallas kernels: 5.66 us -> 5.38 us  [call(): pl.pallas_call(body, out_shape=outputs, in_specs=[pl.BlockSpec(memory_spa...]
  transfers between devices with their start and end apart: 5 -> 7, of which waited for: 3 -> 2; matrix products, arithmetic and copies ran while one was open for 0% -> 0% of each run, Pallas kernels for 11% -> 10%
where the time goes in v13:
time: 18.8 us; the launch traced here: 18.6 us
  starting transfers between devices  10.1 us (54%)
  Pallas kernels  5.38 us (29%)
  waiting for transfers between devices  3.04 us (16%)
    ppermute x6, starting transfers between devices, exchange(): return lax.ppermute(block, ('row', 'col'), hops)  9.91 us
    pallas_call x3, Pallas kernels, call(): pl.pallas_call(body, out_shape=outputs, in_specs=[pl.BlockSpec(memory_spa...  5.38 us
    ppermute x6, waiting for transfers between devices, exchange(): return lax.ppermute(block, ('row', 'col'), hops)  2.33 us
    ppermute x1, waiting for transfers between devices, whole_crop_plan(): other = lax.ppermute(mine, 'col', [(0, 1), (1, 0)])  0.71 us
  transfers between devices with their start and end apart: 7, of which 2 were waited for; matrix products, arithmetic and copies ran while one was open for 0% of the time, Pallas kernels for 10%

profile of v13, /device:TPU:0, one launch (start us, length us, event | category | flops | bytes accessed | tf_op | source)
XLA Modules:
  0.0 18.6 jit_solution(17840600012603102250)
XLA Ops:
  0.0 3.5 %collective-permute-start = (f32[4,16,128]{2,1,0:T(8,128)}, f32[4,16,128]{2,1,0:T(8,128)S(1)}, u32[]{:S(2)}, u32[]{:S(2)}) collective-permute-start(f32[4,16,128]{2,1,0:T(8,128)} %refs_0_.1), channel_id=1, source_target_pairs={{0,9},{1,8},{2,11},{3,10},{4,13},{5,12},{6,15},{7,14},{8,1},{9,0},... | collective-permute-start | bytes 98312 | tf_op jit(solution)/shard_map/ppermute | solution.py:266
  3.5 1.1 %prep.1 = (f32[4,16,128]{2,1,0:T(8,128)S(1)}, f32[1,128]{1,0:T(1,128)S(1)}, bf16[2,128,640]{2,1,0:T(8,128)(2,1)S(1)}, bf16[2,128,128]{2,1,0:T(8,128)(2,1)S(1)}, ...) custom-call(f32[4,16,128]{2,1,0:T(8,128)} %refs_0_.1, f32[1,128]{1,0:T(1,128)} %bitcast.17, bf16[2,128,512]{2,1,0:T(8,128)(2,1)} %refs_2_.1, ...), custom_call_target="tpu_custom_call" | custom-call | flops 10485760 | bytes 2097152 | tf_op jit(solution)/shard_map/prep/pallas_call | solution.py:270
  4.6 1.9 %collective-permute-start.3 = (f32[4,16,128]{2,1,0:T(8,128)S(1)}, f32[4,16,128]{2,1,0:T(8,128)S(1)}, u32[]{:S(2)}, u32[]{:S(2)}) collective-permute-start(f32[4,16,128]{2,1,0:T(8,128)S(1)} %get-tuple-element.16), channel_id=1, source_target_pairs={{0,5},{1,4},{2,7},{3,6},{4,1},{5,0},{6,3},{7,2},{8,13},{9,12},{10,... | collective-permute-start | bytes 98312 | tf_op jit(solution)/shard_map/ppermute | solution.py:266
  6.5 1.0 %collective-permute-start.1 = (f32[4,16,128]{2,1,0:T(8,128)S(1)}, f32[4,16,128]{2,1,0:T(8,128)S(1)}, u32[]{:S(2)}, u32[]{:S(2)}) collective-permute-start(f32[4,16,128]{2,1,0:T(8,128)S(1)} %get-tuple-element.16), channel_id=1, source_target_pairs={{0,3},{1,2},{2,1},{3,0},{4,7},{5,6},{6,5},{7,4},{8,11},{9,10},{10,... | collective-permute-start | bytes 98312 | tf_op jit(solution)/shard_map/ppermute | solution.py:266
  7.5 0.0 collective-permute-done
  7.5 0.8 %collective-permute-start.5 = (f32[2,4,16,128]{3,2,1,0:T(8,128)S(1)}, f32[2,4,16,128]{3,2,1,0:T(8,128)S(1)}, u32[]{:S(2)}, u32[]{:S(2)}) collective-permute-start(f32[2,4,16,128]{3,2,1,0:T(8,128)S(1)} %pad_maximum_fusion), channel_id=1, source_target_pairs={{0,7},{1,6},{2,5},{3,4},{4,3},{5,2},{6,1},{7,0},{8,15},{9,14},{10,... | collective-permute-start | bytes 196616 | tf_op jit(solution)/shard_map/ppermute | solution.py:266
  8.3 1.1 %collective-permute-start.4 = (f32[4,16,128]{2,1,0:T(8,128)S(1)}, f32[4,16,128]{2,1,0:T(8,128)S(1)}, u32[]{:S(2)}, u32[]{:S(2)}) collective-permute-start(f32[4,16,128]{2,1,0:T(8,128)S(1)} %collective-permute-done), channel_id=1, source_target_pairs={{0,5},{1,4},{2,7},{3,6},{4,1},{5,0},{6,3},{7,2},{8,13},{9,12},{10,... | collective-permute-start | bytes 98312 | tf_op jit(solution)/shard_map/ppermute | solution.py:266
  9.3 1.7 %collective-permute-start.2 = (f32[4,16,128]{2,1,0:T(8,128)S(1)}, f32[4,16,128]{2,1,0:T(8,128)S(1)}, u32[]{:S(2)}, u32[]{:S(2)}) collective-permute-start(f32[4,16,128]{2,1,0:T(8,128)S(1)} %collective-permute-done), channel_id=1, source_target_pairs={{0,3},{1,2},{2,1},{3,0},{4,7},{5,6},{6,5},{7,4},{8,11},{9,10},{10,... | collective-permute-start | bytes 98312 | tf_op jit(solution)/shard_map/ppermute | solution.py:266
  11.1 0.0 collective-permute-done.1
  11.1 2.3 %collective-permute-done.2 = f32[4,16,128]{2,1,0:T(8,128)S(1)} collective-permute-done((f32[4,16,128]{2,1,0:T(8,128)S(1)}, f32[4,16,128]{2,1,0:T(8,128)S(1)}, u32[]{:S(2)}, u32[]{:S(2)}) %collective-permute-start.2) | collective-permute-done | bytes 32800 | tf_op jit(solution)/shard_map/ppermute | solution.py:266
  13.4 0.0 collective-permute-done.3
  13.4 0.0 collective-permute-done.4
  13.4 0.0 collective-permute-done.5
  13.5 0.2 %collective-permute-start.6 = (f32[8,4,16,128]{3,2,1,0:T(8,128)S(1)}, f32[8,4,16,128]{3,2,1,0:T(8,128)S(1)}, u32[]{:S(2)}, u32[]{:S(2)}) collective-permute-start(f32[8,4,16,128]{3,2,1,0:T(8,128)S(1)} %constant_dynamic-update-slice_fusion.mine), channel_id=1, source_target_pairs={{0,1},{1,0},{2,3},{3,2},{4,5},{5,4},{6,7},{7,6},{8,9},{9,8},{10,11... | collective-permute-start | bytes 786440 | tf_op jit(solution)/shard_map/ppermute | solution.py:327
  13.7 0.7 %mine.1 = (f32[2,512,128]{2,1,0:T(8,128)S(1)}, f32[2,512,128]{2,1,0:T(8,128)S(1)}, f32[2,32,16,128]{3,2,1,0:T(8,128)S(1)}, f32[2,512,128]{2,1,0:T(8,128)S(1)}) custom-call(f32[8,4,16,128]{3,2,1,0:T(8,128)S(1)} %constant_dynamic-update-slice_fusion.mine, f32[32,128]{1,0:T(8,128)S(1)} %get-tuple-element.17.chains, f32[32,128]{1,0:T(8,128)S(1)} %get-tuple-element.18.mask, ...), custom_call_target="tpu_custom_call" | custom-call | flops 83886080 | bytes 2097152 | tf_op jit(solution)/shard_map/mine/pallas_call | solution.py:270
  14.4 0.7 %collective-permute-done.6.other = f32[8,4,16,128]{3,2,1,0:T(8,128)S(1)} collective-permute-done((f32[8,4,16,128]{3,2,1,0:T(8,128)S(1)}, f32[8,4,16,128]{3,2,1,0:T(8,128)S(1)}, u32[]{:S(2)}, u32[]{:S(2)}) %collective-permute-start.6) | collective-permute-done | bytes 262176 | tf_op jit(solution)/shard_map/ppermute | solution.py:327
  15.1 3.6 %crop.1 = (f32[4,16,128]{2,1,0:T(8,128)}, f32[2,512,128]{2,1,0:T(8,128)S(1)}, f32[2,512,128]{2,1,0:T(8,128)S(1)}, f32[2,32,16,128]{3,2,1,0:T(8,128)S(1)}, f32[2,512,128]{2,1,0:T(8,128)S(1)}) custom-call(f32[8,4,16,128]{3,2,1,0:T(8,128)S(1)} %collective-permute-done.6.other, ...), custom_call_target="tpu_custom_call", output_to_operand_aliasing={{1}: (6, {}), {2}: (7, {}), {3}: (8, {}), {4}: (9, {})} | custom-call | flops 335544320 | bytes 2097152 | tf_op jit(solution)/shard_map/crop/pallas_call | solution.py:270
  (8 shorter events, 0.0 us)
Async XLA Ops:
  0.0 7.5 %collective-permute-start = (f32[4,16,128]{2,1,0:T(8,128)}, f32[4,16,128]{2,1,0:T(8,128)S(1)}, u32[]{:S(2)}, u32[]{:S(2)}) collective-permute-start(f32[4,16,128]{2,1,0:T(8,128)} %refs_0_.1), channel_id=1, source_target_pairs={{0,9},{1,8},{2,11},{3,10},{4,13},{5,12},{6,15},{7,14},{8,1},{9,0},... | collective-permute-start | bytes 98312 | tf_op jit(solution)/shard_map/ppermute | solution.py:266
  4.6 8.8 %collective-permute-start.3 = (f32[4,16,128]{2,1,0:T(8,128)S(1)}, f32[4,16,128]{2,1,0:T(8,128)S(1)}, u32[]{:S(2)}, u32[]{:S(2)}) collective-permute-start(f32[4,16,128]{2,1,0:T(8,128)S(1)} %get-tuple-element.16), channel_id=1, source_target_pairs={{0,5},{1,4},{2,7},{3,6},{4,1},{5,0},{6,3},{7,2},{8,13},{9,12},{10,... | collective-permute-start | bytes 98312 | tf_op jit(solution)/shard_map/ppermute | solution.py:266
  6.5 4.5 %collective-permute-start.1 = (f32[4,16,128]{2,1,0:T(8,128)S(1)}, f32[4,16,128]{2,1,0:T(8,128)S(1)}, u32[]{:S(2)}, u32[]{:S(2)}) collective-permute-start(f32[4,16,128]{2,1,0:T(8,128)S(1)} %get-tuple-element.16), channel_id=1, source_target_pairs={{0,3},{1,2},{2,1},{3,0},{4,7},{5,6},{6,5},{7,4},{8,11},{9,10},{10,... | collective-permute-start | bytes 98312 | tf_op jit(solution)/shard_map/ppermute | solution.py:266
  7.5 5.9 %collective-permute-start.5 = (f32[2,4,16,128]{3,2,1,0:T(8,128)S(1)}, f32[2,4,16,128]{3,2,1,0:T(8,128)S(1)}, u32[]{:S(2)}, u32[]{:S(2)}) collective-permute-start(f32[2,4,16,128]{3,2,1,0:T(8,128)S(1)} %pad_maximum_fusion), channel_id=1, source_target_pairs={{0,7},{1,6},{2,5},{3,4},{4,3},{5,2},{6,1},{7,0},{8,15},{9,14},{10,... | collective-permute-start | bytes 196616 | tf_op jit(solution)/shard_map/ppermute | solution.py:266
  8.3 5.2 %collective-permute-start.4 = (f32[4,16,128]{2,1,0:T(8,128)S(1)}, f32[4,16,128]{2,1,0:T(8,128)S(1)}, u32[]{:S(2)}, u32[]{:S(2)}) collective-permute-start(f32[4,16,128]{2,1,0:T(8,128)S(1)} %collective-permute-done), channel_id=1, source_target_pairs={{0,5},{1,4},{2,7},{3,6},{4,1},{5,0},{6,3},{7,2},{8,13},{9,12},{10,... | collective-permute-start | bytes 98312 | tf_op jit(solution)/shard_map/ppermute | solution.py:266
  9.3 4.1 %collective-permute-start.2 = (f32[4,16,128]{2,1,0:T(8,128)S(1)}, f32[4,16,128]{2,1,0:T(8,128)S(1)}, u32[]{:S(2)}, u32[]{:S(2)}) collective-permute-start(f32[4,16,128]{2,1,0:T(8,128)S(1)} %collective-permute-done), channel_id=1, source_target_pairs={{0,3},{1,2},{2,1},{3,0},{4,7},{5,6},{6,5},{7,4},{8,11},{9,10},{10,... | collective-permute-start | bytes 98312 | tf_op jit(solution)/shard_map/ppermute | solution.py:266
  13.5 1.6 %collective-permute-start.6 = (f32[8,4,16,128]{3,2,1,0:T(8,128)S(1)}, f32[8,4,16,128]{3,2,1,0:T(8,128)S(1)}, u32[]{:S(2)}, u32[]{:S(2)}) collective-permute-start(f32[8,4,16,128]{3,2,1,0:T(8,128)S(1)} %constant_dynamic-update-slice_fusion.mine), channel_id=1, source_target_pairs={{0,1},{1,0},{2,3},{3,2},{4,5},{5,4},{6,7},{7,6},{8,9},{9,8},{10,11... | collective-permute-start | bytes 786440 | tf_op jit(solution)/shard_map/ppermute | solution.py:327

commit v14 on v12

--- a/solution.py
+++ b/solution.py
@@ -136,7 +136,8 @@
             right[half, pl.ds(token, cols, tokens), :] = rgt[at : at + cols]
 
 
-def own_kernel(masks, *refs):
+def prep_kernel(masks, halves, early, *refs):
+    blocks, refs = refs[: len(early)], refs[len(early) :]
     sources, rest = refs[:7], refs[7:]
     pair, bias, weights, out_w, chains, mask, start, gates, left, right, chains_v, mask_v, sems = rest
     split = sources[2].shape[-1]
@@ -150,11 +151,12 @@
         load.wait()
     table(chains_v, chains)
     table(mask_v, mask)
-    edges(masks, [(0, 0, pair[...])], chains, mask, bias, weights, start, gates, left, right)
-
-
-def mine_kernel(masks, halves, mine, chains, mask, bias, weights, s_in, g_in, l_in, r_in, *outs):
-    items = [(slot, halves[slot], mine[slot]) for slot in range(1, len(masks))]
+    items = [(len(masks) - 1, halves[-1], pair[...])] + [(slot, halves[slot], block[...]) for slot, block in zip(early, blocks)]
+    edges(masks, items, chains, mask, bias, weights, start, gates, left, right)
+
+
+def mine_kernel(masks, halves, early, mine, chains, mask, bias, weights, s_in, g_in, l_in, r_in, *outs):
+    items = [(slot, halves[slot], mine[slot]) for slot in range(len(masks) - 1) if slot not in early]
     edges(masks, items, chains, mask, bias, weights, *outs)
 
 
@@ -236,7 +238,8 @@
     edge_rows = (count - 1) * tokens * 8
     proj_r = dot(normed[:edge_rows], weights[1, :, 2 * hidden : 4 * hidden])
     proj_l = dot(normed[edge_rows:], weights[1, :, : 2 * hidden])
-    own = [slice(n * tokens * 8, n * tokens * 8 + rows * 8) for n in range(count - 1)]
+    ends = [(n + 1) * tokens * 8 for n in range(count - 1)]
+    own = [slice(end - rows * 8, end) for end in ends]
     own_state = jnp.concatenate([state[part] for part in own], 0)
     own_logit = dot(jnp.concatenate([normed[part] for part in own], 0), weights[1, :, 4 * hidden :])
     pm = jnp.concatenate([mask_left * m for m in row_masks], 0)
@@ -267,11 +270,11 @@
     return lax.ppermute(block, ("row", "col"), hops)
 
 
-def call(body, inputs, outputs, scratch, name, flops, aliases={}, space=pltpu.VMEM):
+def call(body, inputs, outputs, scratch, name, flops, aliases={}, spaces=None):
     return pl.pallas_call(
         body,
         out_shape=outputs,
-        in_specs=[pl.BlockSpec(memory_space=space)] * len(inputs),
+        in_specs=[pl.BlockSpec(memory_space=each) for each in spaces or [pltpu.VMEM] * len(inputs)],
         out_specs=[pl.BlockSpec(memory_space=pltpu.VMEM)] * len(outputs),
         scratch_shapes=scratch,
         compiler_params=pltpu.CompilerParams(vmem_limit_bytes=32 << 20),
@@ -299,28 +302,38 @@
     half = floats(*half)
     flops = 2 * tokens * cols * width * 5 * hidden
     top = ranks // 2
-    masks, halves = [0, top], [0, 1]
+    masks, halves = [top], [1]
     for bits in range(1, top):
         masks += [bits, bits ^ top]
         halves += [1, 0]
+    masks, halves = masks + [0], halves + [0]
+    near = [bits for bits in range(1, top) if bits & (bits - 1) == 0]
+    early = [masks.index(bits) for bits in [top] + near]
     far = exchange(pair, top)
+    sent = {bits: exchange(pair, bits) for bits in near}
     loaded = (pair, bias, proj_weight, gate_weight, out_weight, chains[None, :], token_mask[None, :])
     joined = jax.ShapeDtypeStruct((2, width, 4 * hidden + width), proj_weight.dtype)
     own, bias, weights, out_weight, chains_t, mask_t, *partial = call(
-        functools.partial(own_kernel, masks),
-        [pltpu.with_memory_space_constraint(each, pltpu.HBM) for each in loaded],
+        functools.partial(prep_kernel, masks, halves, early),
+        [far, *sent.values()] + [pltpu.with_memory_space_constraint(each, pltpu.HBM) for each in loaded],
         like(pair, bias) + [joined] + like(out_weight) + floats((tokens, width), (tokens, width)) + half,
         [pltpu.VMEM((1, tokens), jnp.int32), pltpu.VMEM((1, tokens), jnp.int32), pltpu.SemaphoreType.DMA((7,))],
-        "own",
+        "prep",
         flops // ranks,
-        space=pltpu.HBM,
-    )
-    two = jnp.stack([own, far])
-    mine = jnp.concatenate([two] + [exchange(two, bits) for bits in range(1, top)], 0)
+        spaces=[pltpu.VMEM] * len(early) + [pltpu.HBM] * 7,
+    )
+    two = jnp.stack([pair, far])
+    parts = [far[None]]
+    for bits in range(1, top):
+        if bits in sent:
+            parts += [sent[bits][None], exchange(far, bits)[None]]
+        else:
+            parts.append(exchange(two, bits))
+    mine = jnp.concatenate(parts + [own[None]], 0)
     other = lax.ppermute(mine, "col", [(0, 1), (1, 0)])
     edge_inputs = (chains_t, mask_t, bias, weights)
     partial = call(
-        functools.partial(mine_kernel, masks, halves),
+        functools.partial(mine_kernel, masks, halves, early),
         (mine, *edge_inputs, *partial),
         half,
         [],

time: 18.2 us -> 18.7 us (1.027)
  waiting for transfers between devices: 5.37 us -> 1.99 us
  starting transfers between devices: 6.99 us -> 9.96 us
  other arithmetic: 0.01 us -> 0.79 us
    ppermute x4 -> x6, waiting for transfers between devices: 4.56 us -> 1.05 us  [exchange(): return lax.ppermute(block, ('row', 'col'), hops)]
    ppermute x4 -> x6, starting transfers between devices: 6.81 us -> 9.78 us  [exchange(): return lax.ppermute(block, ('row', 'col'), hops)]
    another operation x1, other arithmetic: 0.01 us -> 0.79 us  [whole_crop_plan(): two = jnp.stack([pair, far])]
  transfers between devices with their start and end apart: 5 -> 7, of which waited for: 3 -> 2; matrix products, arithmetic and copies ran while one was open for 0% -> 4% of each run, Pallas kernels for 11% -> 11%
where the time goes in v14:
time: 18.7 us; the launch traced here: 18.5 us
  starting transfers between devices  9.96 us (53%)
  Pallas kernels  5.68 us (30%)
  waiting for transfers between devices  1.99 us (11%)
  other arithmetic  0.79 us (4%)
    ppermute x6, starting transfers between devices, exchange(): return lax.ppermute(block, ('row', 'col'), hops)  9.78 us
    pallas_call x3, Pallas kernels, call(): pl.pallas_call(body, out_shape=outputs, in_specs=[pl.BlockSpec(memory_spa...  5.68 us
    ppermute x6, waiting for transfers between devices, exchange(): return lax.ppermute(block, ('row', 'col'), hops)  1.05 us
    ppermute x1, waiting for transfers between devices, whole_crop_plan(): other = lax.ppermute(mine, 'col', [(0, 1), (1, 0)])  0.94 us
    another operation x1, other arithmetic, whole_crop_plan(): two = jnp.stack([pair, far])  0.79 us
  transfers between devices with their start and end apart: 7, of which 2 were waited for; matrix products, arithmetic and copies ran while one was open for 4% of the time, Pallas kernels for 11%

profile of v14, /device:TPU:0, one launch (start us, length us, event | category | flops | bytes accessed | tf_op | source)
XLA Modules:
  0.0 18.5 jit_solution(4666624320053507181)
XLA Ops:
  0.0 3.5 %collective-permute-start = (f32[4,16,128]{2,1,0:T(8,128)}, f32[4,16,128]{2,1,0:T(8,128)S(1)}, u32[]{:S(2)}, u32[]{:S(2)}) collective-permute-start(f32[4,16,128]{2,1,0:T(8,128)} %refs_3_.1), channel_id=1, source_target_pairs={{0,9},{1,8},{2,11},{3,10},{4,13},{5,12},{6,15},{7,14},{8,1},{9,0},... | collective-permute-start | bytes 98312 | tf_op jit(solution)/shard_map/ppermute | solution.py:270
  3.5 1.9 %collective-permute-start.3 = (f32[4,16,128]{2,1,0:T(8,128)}, f32[4,16,128]{2,1,0:T(8,128)S(1)}, u32[]{:S(2)}, u32[]{:S(2)}) collective-permute-start(f32[4,16,128]{2,1,0:T(8,128)} %refs_3_.1), channel_id=1, source_target_pairs={{0,5},{1,4},{2,7},{3,6},{4,1},{5,0},{6,3},{7,2},{8,13},{9,12},{10,... | collective-permute-start | bytes 98312 | tf_op jit(solution)/shard_map/ppermute | solution.py:270
  5.3 1.0 %collective-permute-start.1 = (f32[4,16,128]{2,1,0:T(8,128)}, f32[4,16,128]{2,1,0:T(8,128)S(1)}, u32[]{:S(2)}, u32[]{:S(2)}) collective-permute-start(f32[4,16,128]{2,1,0:T(8,128)} %refs_3_.1), channel_id=1, source_target_pairs={{0,3},{1,2},{2,1},{3,0},{4,7},{5,6},{6,5},{7,4},{8,11},{9,10},{10,... | collective-permute-start | bytes 98312 | tf_op jit(solution)/shard_map/ppermute | solution.py:270
  6.3 0.0 collective-permute-done.refs_0_
  6.3 0.8 %pad_maximum_fusion = f32[2,4,16,128]{3,2,1,0:T(8,128)S(1)} fusion(f32[1,4,16,128]{3,2,1,0:T(8,128)S(1)} %bitcast.16, f32[1,4,16,128]{3,2,1,0:T(8,128)} %bitcast.17), kind=kLoop, calls=%fused_computation | loop fusion | flops 16384 | bytes 131072 | tf_op jit(solution)/shard_map/stack | solution.py:325
  7.1 2.1 %collective-permute-start.5 = (f32[2,4,16,128]{3,2,1,0:T(8,128)S(1)}, f32[2,4,16,128]{3,2,1,0:T(8,128)S(1)}, u32[]{:S(2)}, u32[]{:S(2)}) collective-permute-start(f32[2,4,16,128]{3,2,1,0:T(8,128)S(1)} %pad_maximum_fusion), channel_id=1, source_target_pairs={{0,7},{1,6},{2,5},{3,4},{4,3},{5,2},{6,1},{7,0},{8,15},{9,14},{10,... | collective-permute-start | bytes 196616 | tf_op jit(solution)/shard_map/ppermute | solution.py:270
  9.2 0.3 %collective-permute-start.4 = (f32[4,16,128]{2,1,0:T(8,128)S(1)}, f32[4,16,128]{2,1,0:T(8,128)S(1)}, u32[]{:S(2)}, u32[]{:S(2)}) collective-permute-start(f32[4,16,128]{2,1,0:T(8,128)S(1)} %collective-permute-done.refs_0_), channel_id=1, source_target_pairs={{0,5},{1,4},{2,7},{3,6},{4,1},{5,0},{6,3},{7,2},{8,13},{9,12},{10,... | collective-permute-start | bytes 98312 | tf_op jit(solution)/shard_map/ppermute | solution.py:270
  9.5 1.1 %collective-permute-start.2 = (f32[4,16,128]{2,1,0:T(8,128)S(1)}, f32[4,16,128]{2,1,0:T(8,128)S(1)}, u32[]{:S(2)}, u32[]{:S(2)}) collective-permute-start(f32[4,16,128]{2,1,0:T(8,128)S(1)} %collective-permute-done.refs_0_), channel_id=1, source_target_pairs={{0,3},{1,2},{2,1},{3,0},{4,7},{5,6},{6,5},{7,4},{8,11},{9,10},{10,... | collective-permute-start | bytes 98312 | tf_op jit(solution)/shard_map/ppermute | solution.py:270
  10.6 0.0 collective-permute-done.1.refs_1_
  10.6 0.0 collective-permute-done.3.refs_2_
  10.6 1.6 %prep.1 = (f32[4,16,128]{2,1,0:T(8,128)S(1)}, f32[1,128]{1,0:T(1,128)S(1)}, bf16[2,128,640]{2,1,0:T(8,128)(2,1)S(1)}, bf16[2,128,128]{2,1,0:T(8,128)(2,1)S(1)}, ...) custom-call(f32[4,16,128]{2,1,0:T(8,128)S(1)} %collective-permute-do, ...), custom_call_target="tpu_custom_call" | custom-call | flops 10485760 | bytes 2097152 | tf_op jit(solution)/shard_map/prep/pallas_call | solution.py:274
  12.2 1.0 %collective-permute-done.2 = f32[4,16,128]{2,1,0:T(8,128)S(1)} collective-permute-done((f32[4,16,128]{2,1,0:T(8,128)S(1)}, f32[4,16,128]{2,1,0:T(8,128)S(1)}, u32[]{:S(2)}, u32[]{:S(2)}) %collective-permute-start.2) | collective-permute-done | bytes 32800 | tf_op jit(solution)/shard_map/ppermute | solution.py:270
  13.3 0.0 collective-permute-done.4
  13.3 0.0 collective-permute-done.5
  13.4 0.2 collective-permute-start.6
  13.5 0.5 %mine.1 = (f32[2,512,128]{2,1,0:T(8,128)S(1)}, f32[2,512,128]{2,1,0:T(8,128)S(1)}, f32[2,32,16,128]{3,2,1,0:T(8,128)S(1)}, f32[2,512,128]{2,1,0:T(8,128)S(1)}) custom-call(f32[8,4,16,128]{3,2,1,0:T(8,128)S(1)} %bitcast_dynamic-update-slice_fusion.mine, ...), custom_call_target="tpu_custom_call", output_to_operand_aliasing={{0}: (5, {}), {1}: (6, {}), {2}: (7, {}), {3}: (8, {})} | custom-call | flops 83886080 | bytes 2097152 | tf_op jit(solution)/shard_map/mine/pallas_call | solution.py:274
  14.0 0.9 %collective-permute-done.6.other = f32[8,4,16,128]{3,2,1,0:T(8,128)S(1)} collective-permute-done((f32[8,4,16,128]{3,2,1,0:T(8,128)S(1)}, f32[8,4,16,128]{3,2,1,0:T(8,128)S(1)}, u32[]{:S(2)}, u32[]{:S(2)}) %collective-permute-start.6) | collective-permute-done | bytes 262176 | tf_op jit(solution)/shard_map/ppermute | solution.py:333
  15.0 3.6 %crop.1 = (f32[4,16,128]{2,1,0:T(8,128)}, f32[2,512,128]{2,1,0:T(8,128)S(1)}, f32[2,512,128]{2,1,0:T(8,128)S(1)}, f32[2,32,16,128]{3,2,1,0:T(8,128)S(1)}, f32[2,512,128]{2,1,0:T(8,128)S(1)}) custom-call(f32[8,4,16,128]{3,2,1,0:T(8,128)S(1)} %collective-permute-done.6.other, ...), custom_call_target="tpu_custom_call", output_to_operand_aliasing={{1}: (6, {}), {2}: (7, {}), {3}: (8, {}), {4}: (9, {})} | custom-call | flops 335544320 | bytes 2097152 | tf_op jit(solution)/shard_map/crop/pallas_call | solution.py:274
  (7 shorter events, 0.0 us)
Async XLA Ops:
  0.0 6.3 %collective-permute-start = (f32[4,16,128]{2,1,0:T(8,128)}, f32[4,16,128]{2,1,0:T(8,128)S(1)}, u32[]{:S(2)}, u32[]{:S(2)}) collective-permute-start(f32[4,16,128]{2,1,0:T(8,128)} %refs_3_.1), channel_id=1, source_target_pairs={{0,9},{1,8},{2,11},{3,10},{4,13},{5,12},{6,15},{7,14},{8,1},{9,0},... | collective-permute-start | bytes 98312 | tf_op jit(solution)/shard_map/ppermute | solution.py:270
  3.5 7.1 %collective-permute-start.3 = (f32[4,16,128]{2,1,0:T(8,128)}, f32[4,16,128]{2,1,0:T(8,128)S(1)}, u32[]{:S(2)}, u32[]{:S(2)}) collective-permute-start(f32[4,16,128]{2,1,0:T(8,128)} %refs_3_.1), channel_id=1, source_target_pairs={{0,5},{1,4},{2,7},{3,6},{4,1},{5,0},{6,3},{7,2},{8,13},{9,12},{10,... | collective-permute-start | bytes 98312 | tf_op jit(solution)/shard_map/ppermute | solution.py:270
  5.3 5.3 %collective-permute-start.1 = (f32[4,16,128]{2,1,0:T(8,128)}, f32[4,16,128]{2,1,0:T(8,128)S(1)}, u32[]{:S(2)}, u32[]{:S(2)}) collective-permute-start(f32[4,16,128]{2,1,0:T(8,128)} %refs_3_.1), channel_id=1, source_target_pairs={{0,3},{1,2},{2,1},{3,0},{4,7},{5,6},{6,5},{7,4},{8,11},{9,10},{10,... | collective-permute-start | bytes 98312 | tf_op jit(solution)/shard_map/ppermute | solution.py:270
  7.1 6.2 %collective-permute-start.5 = (f32[2,4,16,128]{3,2,1,0:T(8,128)S(1)}, f32[2,4,16,128]{3,2,1,0:T(8,128)S(1)}, u32[]{:S(2)}, u32[]{:S(2)}) collective-permute-start(f32[2,4,16,128]{3,2,1,0:T(8,128)S(1)} %pad_maximum_fusion), channel_id=1, source_target_pairs={{0,7},{1,6},{2,5},{3,4},{4,3},{5,2},{6,1},{7,0},{8,15},{9,14},{10,... | collective-permute-start | bytes 196616 | tf_op jit(solution)/shard_map/ppermute | solution.py:270
  9.2 4.1 %collective-permute-start.4 = (f32[4,16,128]{2,1,0:T(8,128)S(1)}, f32[4,16,128]{2,1,0:T(8,128)S(1)}, u32[]{:S(2)}, u32[]{:S(2)}) collective-permute-start(f32[4,16,128]{2,1,0:T(8,128)S(1)} %collective-permute-done.refs_0_), channel_id=1, source_target_pairs={{0,5},{1,4},{2,7},{3,6},{4,1},{5,0},{6,3},{7,2},{8,13},{9,12},{10,... | collective-permute-start | bytes 98312 | tf_op jit(solution)/shard_map/ppermute | solution.py:270
  9.5 3.8 %collective-permute-start.2 = (f32[4,16,128]{2,1,0:T(8,128)S(1)}, f32[4,16,128]{2,1,0:T(8,128)S(1)}, u32[]{:S(2)}, u32[]{:S(2)}) collective-permute-start(f32[4,16,128]{2,1,0:T(8,128)S(1)} %collective-permute-done.refs_0_), channel_id=1, source_target_pairs={{0,3},{1,2},{2,1},{3,0},{4,7},{5,6},{6,5},{7,4},{8,11},{9,10},{10,... | collective-permute-start | bytes 98312 | tf_op jit(solution)/shard_map/ppermute | solution.py:270
  13.4 1.6 %collective-permute-start.6 = (f32[8,4,16,128]{3,2,1,0:T(8,128)S(1)}, f32[8,4,16,128]{3,2,1,0:T(8,128)S(1)}, u32[]{:S(2)}, u32[]{:S(2)}) collective-permute-start(f32[8,4,16,128]{3,2,1,0:T(8,128)S(1)} %bitcast_dynamic-update-slice_fusion.mine), channel_id=1, source_target_pairs={{0,1},{1,0},{2,3},{3,2},{4,5},{5,4},{6,7},{7,6},{8,9},{9,8},{10,11... | collective-permute-start | bytes 786440 | tf_op jit(solution)/shard_map/ppermute | solution.py:333

commit v15 on v14

--- a/solution.py
+++ b/solution.py
@@ -136,6 +136,12 @@
             right[half, pl.ds(token, cols, tokens), :] = rgt[at : at + cols]
 
 
+def keep_kernel(source, target, sem):
+    load = pltpu.make_async_copy(source, target, sem)
+    load.start()
+    load.wait()
+
+
 def prep_kernel(masks, halves, early, *refs):
     blocks, refs = refs[: len(early)], refs[len(early) :]
     sources, rest = refs[:7], refs[7:]
@@ -311,6 +317,15 @@
     early = [masks.index(bits) for bits in [top] + near]
     far = exchange(pair, top)
     sent = {bits: exchange(pair, bits) for bits in near}
+    kept = call(
+        keep_kernel,
+        [pltpu.with_memory_space_constraint(pair, pltpu.HBM)],
+        like(pair),
+        [pltpu.SemaphoreType.DMA],
+        "keep",
+        flops // ranks,
+        spaces=[pltpu.HBM],
+    )[0]
     loaded = (pair, bias, proj_weight, gate_weight, out_weight, chains[None, :], token_mask[None, :])
     joined = jax.ShapeDtypeStruct((2, width, 4 * hidden + width), proj_weight.dtype)
     own, bias, weights, out_weight, chains_t, mask_t, *partial = call(
@@ -322,7 +337,7 @@
         flops // ranks,
         spaces=[pltpu.VMEM] * len(early) + [pltpu.HBM] * 7,
     )
-    two = jnp.stack([pair, far])
+    two = jnp.stack([kept, far])
     parts = [far[None]]
     for bits in range(1, top):
         if bits in sent:

time: 18.7 us -> 18.5 us (0.989)
  Pallas kernels: 5.68 us -> 6.48 us
  other arithmetic: 0.79 us -> 0.01 us
  waiting for transfers between devices: 1.99 us -> 1.63 us
    pallas_call x3 -> x4, Pallas kernels: 5.68 us -> 6.48 us  [call(): pl.pallas_call(body, out_shape=outputs, in_specs=[pl.BlockSpec(memory_spa...]
    another operation x1, other arithmetic: 0.79 us -> 0.01 us  [whole_crop_plan(): two = jnp.stack([kept, far])]
    ppermute x6, waiting for transfers between devices: 1.05 us -> 0.71 us  [exchange(): return lax.ppermute(block, ('row', 'col'), hops)]
  transfers between devices with their start and end apart: 7 -> 7, of which waited for: 2 -> 2; matrix products, arithmetic and copies ran while one was open for 4% -> 0% of each run, Pallas kernels for 11% -> 16%
where the time goes in v15:
time: 18.5 us; the launch traced here: 18.3 us
  starting transfers between devices  10 us (54%)
  Pallas kernels  6.48 us (35%)
  waiting for transfers between devices  1.63 us (9%)
    ppermute x6, starting transfers between devices, exchange(): return lax.ppermute(block, ('row', 'col'), hops)  9.85 us
    pallas_call x4, Pallas kernels, call(): pl.pallas_call(body, out_shape=outputs, in_specs=[pl.BlockSpec(memory_spa...  6.48 us
    ppermute x1, waiting for transfers between devices, whole_crop_plan(): other = lax.ppermute(mine, 'col', [(0, 1), (1, 0)])  0.92 us
    ppermute x6, waiting for transfers between devices, exchange(): return lax.ppermute(block, ('row', 'col'), hops)  0.71 us
  transfers between devices with their start and end apart: 7, of which 2 were waited for; matrix products, arithmetic and copies ran while one was open for 0% of the time, Pallas kernels for 16%

profile of v15, /device:TPU:0, one launch (start us, length us, event | category | flops | bytes accessed | tf_op | source)
XLA Modules:
  0.0 18.3 jit_solution(12433700905054495758)
XLA Ops:
  0.0 3.5 %collective-permute-start = (f32[4,16,128]{2,1,0:T(8,128)}, f32[4,16,128]{2,1,0:T(8,128)S(1)}, u32[]{:S(2)}, u32[]{:S(2)}) collective-permute-start(f32[4,16,128]{2,1,0:T(8,128)} %refs_3_.1), channel_id=1, source_target_pairs={{0,9},{1,8},{2,11},{3,10},{4,13},{5,12},{6,15},{7,14},{8,1},{9,0},... | collective-permute-start | bytes 98312 | tf_op jit(solution)/shard_map/ppermute | solution.py:276
  3.5 1.9 %collective-permute-start.3 = (f32[4,16,128]{2,1,0:T(8,128)}, f32[4,16,128]{2,1,0:T(8,128)S(1)}, u32[]{:S(2)}, u32[]{:S(2)}) collective-permute-start(f32[4,16,128]{2,1,0:T(8,128)} %refs_3_.1), channel_id=1, source_target_pairs={{0,5},{1,4},{2,7},{3,6},{4,1},{5,0},{6,3},{7,2},{8,13},{9,12},{10,... | collective-permute-start | bytes 98312 | tf_op jit(solution)/shard_map/ppermute | solution.py:276
  5.3 1.0 %collective-permute-start.1 = (f32[4,16,128]{2,1,0:T(8,128)}, f32[4,16,128]{2,1,0:T(8,128)S(1)}, u32[]{:S(2)}, u32[]{:S(2)}) collective-permute-start(f32[4,16,128]{2,1,0:T(8,128)} %refs_3_.1), channel_id=1, source_target_pairs={{0,3},{1,2},{2,1},{3,0},{4,7},{5,6},{6,5},{7,4},{8,11},{9,10},{10,... | collective-permute-start | bytes 98312 | tf_op jit(solution)/shard_map/ppermute | solution.py:276
  6.3 0.8 %keep.1 = f32[4,16,128]{2,1,0:T(8,128)S(1)} custom-call(f32[4,16,128]{2,1,0:T(8,128)} %refs_3_.1), custom_call_target="tpu_custom_call" | custom-call | flops 10485760 | bytes 2097152 | tf_op jit(solution)/shard_map/keep/pallas_call | solution.py:280
  7.1 0.0 collective-permute-done.refs_0_
  7.1 1.3 %collective-permute-start.5 = (f32[2,4,16,128]{3,2,1,0:T(8,128)S(1)}, f32[2,4,16,128]{3,2,1,0:T(8,128)S(1)}, u32[]{:S(2)}, u32[]{:S(2)}) collective-permute-start(f32[2,4,16,128]{3,2,1,0:T(8,128)S(1)} %pad_maximum_fusion), channel_id=1, source_target_pairs={{0,7},{1,6},{2,5},{3,4},{4,3},{5,2},{6,1},{7,0},{8,15},{9,14},{10,... | collective-permute-start | bytes 196616 | tf_op jit(solution)/shard_map/ppermute | solution.py:276
  8.5 0.5 %collective-permute-start.4 = (f32[4,16,128]{2,1,0:T(8,128)S(1)}, f32[4,16,128]{2,1,0:T(8,128)S(1)}, u32[]{:S(2)}, u32[]{:S(2)}) collective-permute-start(f32[4,16,128]{2,1,0:T(8,128)S(1)} %collective-permute-done.refs_0_), channel_id=1, source_target_pairs={{0,5},{1,4},{2,7},{3,6},{4,1},{5,0},{6,3},{7,2},{8,13},{9,12},{10,... | collective-permute-start | bytes 98312 | tf_op jit(solution)/shard_map/ppermute | solution.py:276
  9.0 1.7 %collective-permute-start.2 = (f32[4,16,128]{2,1,0:T(8,128)S(1)}, f32[4,16,128]{2,1,0:T(8,128)S(1)}, u32[]{:S(2)}, u32[]{:S(2)}) collective-permute-start(f32[4,16,128]{2,1,0:T(8,128)S(1)} %collective-permute-done.refs_0_), channel_id=1, source_target_pairs={{0,3},{1,2},{2,1},{3,0},{4,7},{5,6},{6,5},{7,4},{8,11},{9,10},{10,... | collective-permute-start | bytes 98312 | tf_op jit(solution)/shard_map/ppermute | solution.py:276
  10.7 0.0 collective-permute-done.1.refs_1_
  10.7 0.0 collective-permute-done.3.refs_2_
  10.7 1.6 %prep.1 = (f32[4,16,128]{2,1,0:T(8,128)S(1)}, f32[1,128]{1,0:T(1,128)S(1)}, bf16[2,128,640]{2,1,0:T(8,128)(2,1)S(1)}, bf16[2,128,128]{2,1,0:T(8,128)(2,1)S(1)}, ...) custom-call(f32[4,16,128]{2,1,0:T(8,128)S(1)} %collective-permute-do, ...), custom_call_target="tpu_custom_call" | custom-call | flops 10485760 | bytes 2097152 | tf_op jit(solution)/shard_map/prep/pallas_call | solution.py:280
  12.3 0.7 %collective-permute-done.2 = f32[4,16,128]{2,1,0:T(8,128)S(1)} collective-permute-done((f32[4,16,128]{2,1,0:T(8,128)S(1)}, f32[4,16,128]{2,1,0:T(8,128)S(1)}, u32[]{:S(2)}, u32[]{:S(2)}) %collective-permute-start.2) | collective-permute-done | bytes 32800 | tf_op jit(solution)/shard_map/ppermute | solution.py:276
  13.1 0.0 collective-permute-done.4
  13.1 0.0 collective-permute-done.5
  13.1 0.2 %collective-permute-start.6 = (f32[8,4,16,128]{3,2,1,0:T(8,128)S(1)}, f32[8,4,16,128]{3,2,1,0:T(8,128)S(1)}, u32[]{:S(2)}, u32[]{:S(2)}) collective-permute-start(f32[8,4,16,128]{3,2,1,0:T(8,128)S(1)} %bitcast_dynamic-update-slice_fusion.mine), channel_id=1, source_target_pairs={{0,1},{1,0},{2,3},{3,2},{4,5},{5,4},{6,7},{7,6},{8,9},{9,8},{10,11... | collective-permute-start | bytes 786440 | tf_op jit(solution)/shard_map/ppermute | solution.py:348
  13.3 0.5 %mine.1 = (f32[2,512,128]{2,1,0:T(8,128)S(1)}, f32[2,512,128]{2,1,0:T(8,128)S(1)}, f32[2,32,16,128]{3,2,1,0:T(8,128)S(1)}, f32[2,512,128]{2,1,0:T(8,128)S(1)}) custom-call(f32[8,4,16,128]{3,2,1,0:T(8,128)S(1)} %bitcast_dynamic-update-slice_fusion.mine, ...), custom_call_target="tpu_custom_call", output_to_operand_aliasing={{0}: (5, {}), {1}: (6, {}), {2}: (7, {}), {3}: (8, {})} | custom-call | flops 83886080 | bytes 2097152 | tf_op jit(solution)/shard_map/mine/pallas_call | solution.py:280
  13.8 0.9 %collective-permute-done.6.other = f32[8,4,16,128]{3,2,1,0:T(8,128)S(1)} collective-permute-done((f32[8,4,16,128]{3,2,1,0:T(8,128)S(1)}, f32[8,4,16,128]{3,2,1,0:T(8,128)S(1)}, u32[]{:S(2)}, u32[]{:S(2)}) %collective-permute-start.6) | collective-permute-done | bytes 262176 | tf_op jit(solution)/shard_map/ppermute | solution.py:348
  14.7 3.6 %crop.1 = (f32[4,16,128]{2,1,0:T(8,128)}, f32[2,512,128]{2,1,0:T(8,128)S(1)}, f32[2,512,128]{2,1,0:T(8,128)S(1)}, f32[2,32,16,128]{3,2,1,0:T(8,128)S(1)}, f32[2,512,128]{2,1,0:T(8,128)S(1)}) custom-call(f32[8,4,16,128]{3,2,1,0:T(8,128)S(1)} %collective-permute-done.6.other, ...), custom_call_target="tpu_custom_call", output_to_operand_aliasing={{1}: (6, {}), {2}: (7, {}), {3}: (8, {}), {4}: (9, {})} | custom-call | flops 335544320 | bytes 2097152 | tf_op jit(solution)/shard_map/crop/pallas_call | solution.py:280
  (8 shorter events, 0.0 us)
Async XLA Ops:
  0.0 7.1 %collective-permute-start = (f32[4,16,128]{2,1,0:T(8,128)}, f32[4,16,128]{2,1,0:T(8,128)S(1)}, u32[]{:S(2)}, u32[]{:S(2)}) collective-permute-start(f32[4,16,128]{2,1,0:T(8,128)} %refs_3_.1), channel_id=1, source_target_pairs={{0,9},{1,8},{2,11},{3,10},{4,13},{5,12},{6,15},{7,14},{8,1},{9,0},... | collective-permute-start | bytes 98312 | tf_op jit(solution)/shard_map/ppermute | solution.py:276
  3.5 7.2 %collective-permute-start.3 = (f32[4,16,128]{2,1,0:T(8,128)}, f32[4,16,128]{2,1,0:T(8,128)S(1)}, u32[]{:S(2)}, u32[]{:S(2)}) collective-permute-start(f32[4,16,128]{2,1,0:T(8,128)} %refs_3_.1), channel_id=1, source_target_pairs={{0,5},{1,4},{2,7},{3,6},{4,1},{5,0},{6,3},{7,2},{8,13},{9,12},{10,... | collective-permute-start | bytes 98312 | tf_op jit(solution)/shard_map/ppermute | solution.py:276
  5.3 5.4 %collective-permute-start.1 = (f32[4,16,128]{2,1,0:T(8,128)}, f32[4,16,128]{2,1,0:T(8,128)S(1)}, u32[]{:S(2)}, u32[]{:S(2)}) collective-permute-start(f32[4,16,128]{2,1,0:T(8,128)} %refs_3_.1), channel_id=1, source_target_pairs={{0,3},{1,2},{2,1},{3,0},{4,7},{5,6},{6,5},{7,4},{8,11},{9,10},{10,... | collective-permute-start | bytes 98312 | tf_op jit(solution)/shard_map/ppermute | solution.py:276
  7.1 6.0 %collective-permute-start.5 = (f32[2,4,16,128]{3,2,1,0:T(8,128)S(1)}, f32[2,4,16,128]{3,2,1,0:T(8,128)S(1)}, u32[]{:S(2)}, u32[]{:S(2)}) collective-permute-start(f32[2,4,16,128]{3,2,1,0:T(8,128)S(1)} %pad_maximum_fusion), channel_id=1, source_target_pairs={{0,7},{1,6},{2,5},{3,4},{4,3},{5,2},{6,1},{7,0},{8,15},{9,14},{10,... | collective-permute-start | bytes 196616 | tf_op jit(solution)/shard_map/ppermute | solution.py:276
  8.5 4.6 %collective-permute-start.4 = (f32[4,16,128]{2,1,0:T(8,128)S(1)}, f32[4,16,128]{2,1,0:T(8,128)S(1)}, u32[]{:S(2)}, u32[]{:S(2)}) collective-permute-start(f32[4,16,128]{2,1,0:T(8,128)S(1)} %collective-permute-done.refs_0_), channel_id=1, source_target_pairs={{0,5},{1,4},{2,7},{3,6},{4,1},{5,0},{6,3},{7,2},{8,13},{9,12},{10,... | collective-permute-start | bytes 98312 | tf_op jit(solution)/shard_map/ppermute | solution.py:276
  9.0 4.1 %collective-permute-start.2 = (f32[4,16,128]{2,1,0:T(8,128)S(1)}, f32[4,16,128]{2,1,0:T(8,128)S(1)}, u32[]{:S(2)}, u32[]{:S(2)}) collective-permute-start(f32[4,16,128]{2,1,0:T(8,128)S(1)} %collective-permute-done.refs_0_), channel_id=1, source_target_pairs={{0,3},{1,2},{2,1},{3,0},{4,7},{5,6},{6,5},{7,4},{8,11},{9,10},{10,... | collective-permute-start | bytes 98312 | tf_op jit(solution)/shard_map/ppermute | solution.py:276
  13.1 1.6 %collective-permute-start.6 = (f32[8,4,16,128]{3,2,1,0:T(8,128)S(1)}, f32[8,4,16,128]{3,2,1,0:T(8,128)S(1)}, u32[]{:S(2)}, u32[]{:S(2)}) collective-permute-start(f32[8,4,16,128]{3,2,1,0:T(8,128)S(1)} %bitcast_dynamic-update-slice_fusion.mine), channel_id=1, source_target_pairs={{0,1},{1,0},{2,3},{3,2},{4,5},{5,4},{6,7},{7,6},{8,9},{9,8},{10,11... | collective-permute-start | bytes 786440 | tf_op jit(solution)/shard_map/ppermute | solution.py:348

commit v16 on v15

--- a/solution.py
+++ b/solution.py
@@ -323,7 +323,7 @@
         like(pair),
         [pltpu.SemaphoreType.DMA],
         "keep",
-        flops // ranks,
+        10 * flops,
         spaces=[pltpu.HBM],
     )[0]
     loaded = (pair, bias, proj_weight, gate_weight, out_weight, chains[None, :], token_mask[None, :])

time: 18.5 us -> 21.1 us (1.14)
  waiting for transfers between devices: 1.63 us -> 4.86 us
  starting transfers between devices: 10 us -> 9.39 us
    ppermute x6, waiting for transfers between devices: 0.71 us -> 3.92 us  [exchange(): return lax.ppermute(block, ('row', 'col'), hops)]
    ppermute x6, starting transfers between devices: 9.85 us -> 9.21 us  [exchange(): return lax.ppermute(block, ('row', 'col'), hops)]
  transfers between devices with their start and end apart: 7 -> 7, of which waited for: 2 -> 3; matrix products, arithmetic and copies ran while one was open for 0% -> 0% of each run, Pallas kernels for 16% -> 14%
where the time goes in v16:
time: 21.1 us; the launch traced here: 20.9 us
  starting transfers between devices  9.39 us (45%)
  Pallas kernels  6.48 us (31%)
  waiting for transfers between devices  4.86 us (23%)
    ppermute x6, starting transfers between devices, exchange(): return lax.ppermute(block, ('row', 'col'), hops)  9.21 us
    pallas_call x4, Pallas kernels, call(): pl.pallas_call(body, out_shape=outputs, in_specs=[pl.BlockSpec(memory_spa...  6.48 us
    ppermute x6, waiting for transfers between devices, exchange(): return lax.ppermute(block, ('row', 'col'), hops)  3.92 us
    ppermute x1, waiting for transfers between devices, whole_crop_plan(): other = lax.ppermute(mine, 'col', [(0, 1), (1, 0)])  0.94 us
  transfers between devices with their start and end apart: 7, of which 3 were waited for; matrix products, arithmetic and copies ran while one was open for 0% of the time, Pallas kernels for 14%

profile of v16, /device:TPU:0, one launch (start us, length us, event | category | flops | bytes accessed | tf_op | source)
XLA Modules:
  0.0 20.9 jit_solution(16171368733618142051)
XLA Ops:
  0.0 2.5 %collective-permute-start.3 = (f32[4,16,128]{2,1,0:T(8,128)}, f32[4,16,128]{2,1,0:T(8,128)S(1)}, u32[]{:S(2)}, u32[]{:S(2)}) collective-permute-start(f32[4,16,128]{2,1,0:T(8,128)} %refs_3_.1), channel_id=1, source_target_pairs={{0,5},{1,4},{2,7},{3,6},{4,1},{5,0},{6,3},{7,2},{8,13},{9,12},{10,... | collective-permute-start | bytes 98312 | tf_op jit(solution)/shard_map/ppermute | solution.py:276
  2.5 1.8 %collective-permute-start.1 = (f32[4,16,128]{2,1,0:T(8,128)}, f32[4,16,128]{2,1,0:T(8,128)S(1)}, u32[]{:S(2)}, u32[]{:S(2)}) collective-permute-start(f32[4,16,128]{2,1,0:T(8,128)} %refs_3_.1), channel_id=1, source_target_pairs={{0,3},{1,2},{2,1},{3,0},{4,7},{5,6},{6,5},{7,4},{8,11},{9,10},{10,... | collective-permute-start | bytes 98312 | tf_op jit(solution)/shard_map/ppermute | solution.py:276
  4.3 2.0 %collective-permute-start = (f32[4,16,128]{2,1,0:T(8,128)}, f32[4,16,128]{2,1,0:T(8,128)S(1)}, u32[]{:S(2)}, u32[]{:S(2)}) collective-permute-start(f32[4,16,128]{2,1,0:T(8,128)} %refs_3_.1), channel_id=1, source_target_pairs={{0,9},{1,8},{2,11},{3,10},{4,13},{5,12},{6,15},{7,14},{8,1},{9,0},... | collective-permute-start | bytes 98312 | tf_op jit(solution)/shard_map/ppermute | solution.py:276
  6.3 0.8 %keep.1 = f32[4,16,128]{2,1,0:T(8,128)S(1)} custom-call(f32[4,16,128]{2,1,0:T(8,128)} %refs_3_.1), custom_call_target="tpu_custom_call" | custom-call | flops 838860800 | bytes 2097152 | tf_op jit(solution)/shard_map/keep/pallas_call | solution.py:280
  7.1 2.5 %collective-permute-done.refs_0_ = f32[4,16,128]{2,1,0:T(8,128)S(1)} collective-permute-done((f32[4,16,128]{2,1,0:T(8,128)}, f32[4,16,128]{2,1,0:T(8,128)S(1)}, u32[]{:S(2)}, u32[]{:S(2)}) %collective-permute-start) | collective-permute-done | bytes 32800 | tf_op jit(solution)/shard_map/ppermute | solution.py:276
  9.6 0.0 collective-permute-start.5
  9.6 1.6 %collective-permute-start.4 = (f32[4,16,128]{2,1,0:T(8,128)S(1)}, f32[4,16,128]{2,1,0:T(8,128)S(1)}, u32[]{:S(2)}, u32[]{:S(2)}) collective-permute-start(f32[4,16,128]{2,1,0:T(8,128)S(1)} %collective-permute-done.refs_0_), channel_id=1, source_target_pairs={{0,5},{1,4},{2,7},{3,6},{4,1},{5,0},{6,3},{7,2},{8,13},{9,12},{10,... | collective-permute-start | bytes 98312 | tf_op jit(solution)/shard_map/ppermute | solution.py:276
  11.3 1.3 %collective-permute-start.2 = (f32[4,16,128]{2,1,0:T(8,128)S(1)}, f32[4,16,128]{2,1,0:T(8,128)S(1)}, u32[]{:S(2)}, u32[]{:S(2)}) collective-permute-start(f32[4,16,128]{2,1,0:T(8,128)S(1)} %collective-permute-done.refs_0_), channel_id=1, source_target_pairs={{0,3},{1,2},{2,1},{3,0},{4,7},{5,6},{6,5},{7,4},{8,11},{9,10},{10,... | collective-permute-start | bytes 98312 | tf_op jit(solution)/shard_map/ppermute | solution.py:276
  12.6 0.0 collective-permute-done.1.refs_1_
  12.6 0.0 collective-permute-done.3.refs_2_
  12.6 1.6 %prep.1 = (f32[4,16,128]{2,1,0:T(8,128)S(1)}, f32[1,128]{1,0:T(1,128)S(1)}, bf16[2,128,640]{2,1,0:T(8,128)(2,1)S(1)}, bf16[2,128,128]{2,1,0:T(8,128)(2,1)S(1)}, ...) custom-call(f32[4,16,128]{2,1,0:T(8,128)S(1)} %collective-permute-do, ...), custom_call_target="tpu_custom_call" | custom-call | flops 10485760 | bytes 2097152 | tf_op jit(solution)/shard_map/prep/pallas_call | solution.py:280
  14.2 1.4 %collective-permute-done.2 = f32[4,16,128]{2,1,0:T(8,128)S(1)} collective-permute-done((f32[4,16,128]{2,1,0:T(8,128)S(1)}, f32[4,16,128]{2,1,0:T(8,128)S(1)}, u32[]{:S(2)}, u32[]{:S(2)}) %collective-permute-start.2) | collective-permute-done | bytes 32800 | tf_op jit(solution)/shard_map/ppermute | solution.py:276
  15.6 0.0 collective-permute-done.4
  15.6 0.0 collective-permute-done.5
  15.7 0.2 collective-permute-start.6
  15.9 0.5 %mine.1 = (f32[2,512,128]{2,1,0:T(8,128)S(1)}, f32[2,512,128]{2,1,0:T(8,128)S(1)}, f32[2,32,16,128]{3,2,1,0:T(8,128)S(1)}, f32[2,512,128]{2,1,0:T(8,128)S(1)}) custom-call(f32[8,4,16,128]{3,2,1,0:T(8,128)S(1)} %bitcast_dynamic-update-slice_fusion.mine, ...), custom_call_target="tpu_custom_call", output_to_operand_aliasing={{0}: (5, {}), {1}: (6, {}), {2}: (7, {}), {3}: (8, {})} | custom-call | flops 83886080 | bytes 2097152 | tf_op jit(solution)/shard_map/mine/pallas_call | solution.py:280
  16.3 0.9 %collective-permute-done.6.other = f32[8,4,16,128]{3,2,1,0:T(8,128)S(1)} collective-permute-done((f32[8,4,16,128]{3,2,1,0:T(8,128)S(1)}, f32[8,4,16,128]{3,2,1,0:T(8,128)S(1)}, u32[]{:S(2)}, u32[]{:S(2)}) %collective-permute-start.6) | collective-permute-done | bytes 262176 | tf_op jit(solution)/shard_map/ppermute | solution.py:348
  17.3 3.6 %crop.1 = (f32[4,16,128]{2,1,0:T(8,128)}, f32[2,512,128]{2,1,0:T(8,128)S(1)}, f32[2,512,128]{2,1,0:T(8,128)S(1)}, f32[2,32,16,128]{3,2,1,0:T(8,128)S(1)}, f32[2,512,128]{2,1,0:T(8,128)S(1)}) custom-call(f32[8,4,16,128]{3,2,1,0:T(8,128)S(1)} %collective-permute-done.6.other, ...), custom_call_target="tpu_custom_call", output_to_operand_aliasing={{1}: (6, {}), {2}: (7, {}), {3}: (8, {}), {4}: (9, {})} | custom-call | flops 335544320 | bytes 2097152 | tf_op jit(solution)/shard_map/crop/pallas_call | solution.py:280
  (8 shorter events, 0.0 us)
Async XLA Ops:
  0.0 12.6 %collective-permute-start.3 = (f32[4,16,128]{2,1,0:T(8,128)}, f32[4,16,128]{2,1,0:T(8,128)S(1)}, u32[]{:S(2)}, u32[]{:S(2)}) collective-permute-start(f32[4,16,128]{2,1,0:T(8,128)} %refs_3_.1), channel_id=1, source_target_pairs={{0,5},{1,4},{2,7},{3,6},{4,1},{5,0},{6,3},{7,2},{8,13},{9,12},{10,... | collective-permute-start | bytes 98312 | tf_op jit(solution)/shard_map/ppermute | solution.py:276
  2.5 10.1 %collective-permute-start.1 = (f32[4,16,128]{2,1,0:T(8,128)}, f32[4,16,128]{2,1,0:T(8,128)S(1)}, u32[]{:S(2)}, u32[]{:S(2)}) collective-permute-start(f32[4,16,128]{2,1,0:T(8,128)} %refs_3_.1), channel_id=1, source_target_pairs={{0,3},{1,2},{2,1},{3,0},{4,7},{5,6},{6,5},{7,4},{8,11},{9,10},{10,... | collective-permute-start | bytes 98312 | tf_op jit(solution)/shard_map/ppermute | solution.py:276
  4.3 5.4 %collective-permute-start = (f32[4,16,128]{2,1,0:T(8,128)}, f32[4,16,128]{2,1,0:T(8,128)S(1)}, u32[]{:S(2)}, u32[]{:S(2)}) collective-permute-start(f32[4,16,128]{2,1,0:T(8,128)} %refs_3_.1), channel_id=1, source_target_pairs={{0,9},{1,8},{2,11},{3,10},{4,13},{5,12},{6,15},{7,14},{8,1},{9,0},... | collective-permute-start | bytes 98312 | tf_op jit(solution)/shard_map/ppermute | solution.py:276
  9.6 6.0 %collective-permute-start.5 = (f32[2,4,16,128]{3,2,1,0:T(8,128)S(1)}, f32[2,4,16,128]{3,2,1,0:T(8,128)S(1)}, u32[]{:S(2)}, u32[]{:S(2)}) collective-permute-start(f32[2,4,16,128]{3,2,1,0:T(8,128)S(1)} %pad_maximum_fusion), channel_id=1, source_target_pairs={{0,7},{1,6},{2,5},{3,4},{4,3},{5,2},{6,1},{7,0},{8,15},{9,14},{10,... | collective-permute-start | bytes 196616 | tf_op jit(solution)/shard_map/ppermute | solution.py:276
  9.6 6.0 %collective-permute-start.4 = (f32[4,16,128]{2,1,0:T(8,128)S(1)}, f32[4,16,128]{2,1,0:T(8,128)S(1)}, u32[]{:S(2)}, u32[]{:S(2)}) collective-permute-start(f32[4,16,128]{2,1,0:T(8,128)S(1)} %collective-permute-done.refs_0_), channel_id=1, source_target_pairs={{0,5},{1,4},{2,7},{3,6},{4,1},{5,0},{6,3},{7,2},{8,13},{9,12},{10,... | collective-permute-start | bytes 98312 | tf_op jit(solution)/shard_map/ppermute | solution.py:276
  11.3 4.3 %collective-permute-start.2 = (f32[4,16,128]{2,1,0:T(8,128)S(1)}, f32[4,16,128]{2,1,0:T(8,128)S(1)}, u32[]{:S(2)}, u32[]{:S(2)}) collective-permute-start(f32[4,16,128]{2,1,0:T(8,128)S(1)} %collective-permute-done.refs_0_), channel_id=1, source_target_pairs={{0,3},{1,2},{2,1},{3,0},{4,7},{5,6},{6,5},{7,4},{8,11},{9,10},{10,... | collective-permute-start | bytes 98312 | tf_op jit(solution)/shard_map/ppermute | solution.py:276
  15.7 1.6 %collective-permute-start.6 = (f32[8,4,16,128]{3,2,1,0:T(8,128)S(1)}, f32[8,4,16,128]{3,2,1,0:T(8,128)S(1)}, u32[]{:S(2)}, u32[]{:S(2)}) collective-permute-start(f32[8,4,16,128]{3,2,1,0:T(8,128)S(1)} %bitcast_dynamic-update-slice_fusion.mine), channel_id=1, source_target_pairs={{0,1},{1,0},{2,3},{3,2},{4,5},{5,4},{6,7},{7,6},{8,9},{9,8},{10,11... | collective-permute-start | bytes 786440 | tf_op jit(solution)/shard_map/ppermute | solution.py:348

commit v17 on v15

--- a/solution.py
+++ b/solution.py
@@ -313,7 +313,7 @@
         masks += [bits, bits ^ top]
         halves += [1, 0]
     masks, halves = masks + [0], halves + [0]
-    near = [bits for bits in range(1, top) if bits & (bits - 1) == 0]
+    near = [top - 1]
     early = [masks.index(bits) for bits in [top] + near]
     far = exchange(pair, top)
     sent = {bits: exchange(pair, bits) for bits in near}

time: 18.5 us -> 18.5 us (level)
  waiting for transfers between devices: 1.63 us -> 2.3 us
  starting transfers between devices: 10 us -> 9.37 us
    ppermute x6 -> x5, waiting for transfers between devices: 0.71 us -> 1.61 us  [exchange(): return lax.ppermute(block, ('row', 'col'), hops)]
    ppermute x6 -> x5, starting transfers between devices: 9.85 us -> 9 us  [exchange(): return lax.ppermute(block, ('row', 'col'), hops)]
    ppermute x1, waiting for transfers between devices: 0.92 us -> 0.69 us  [whole_crop_plan(): other = lax.ppermute(mine, 'col', [(0, 1), (1, 0)])]
  transfers between devices with their start and end apart: 7 -> 6, of which waited for: 2 -> 3; matrix products, arithmetic and copies ran while one was open for 0% -> 0% of each run, Pallas kernels for 16% -> 16%
where the time goes in v17:
time: 18.5 us; the launch traced here: 18.3 us
  starting transfers between devices  9.37 us (51%)
  Pallas kernels  6.48 us (35%)
  waiting for transfers between devices  2.3 us (12%)
    ppermute x5, starting transfers between devices, exchange(): return lax.ppermute(block, ('row', 'col'), hops)  9 us
    pallas_call x4, Pallas kernels, call(): pl.pallas_call(body, out_shape=outputs, in_specs=[pl.BlockSpec(memory_spa...  6.48 us
    ppermute x5, waiting for transfers between devices, exchange(): return lax.ppermute(block, ('row', 'col'), hops)  1.61 us
    ppermute x1, waiting for transfers between devices, whole_crop_plan(): other = lax.ppermute(mine, 'col', [(0, 1), (1, 0)])  0.69 us
    ppermute x1, starting transfers between devices, whole_crop_plan(): other = lax.ppermute(mine, 'col', [(0, 1), (1, 0)])  0.37 us
  transfers between devices with their start and end apart: 6, of which 3 were waited for; matrix products, arithmetic and copies ran while one was open for 0% of the time, Pallas kernels for 16%

profile of v17, /device:TPU:0, one launch (start us, length us, event | category | flops | bytes accessed | tf_op | source)
XLA Modules:
  0.0 18.3 jit_solution(14186163937374332426)
XLA Ops:
  0.0 3.5 %collective-permute-start = (f32[4,16,128]{2,1,0:T(8,128)}, f32[4,16,128]{2,1,0:T(8,128)S(1)}, u32[]{:S(2)}, u32[]{:S(2)}) collective-permute-start(f32[4,16,128]{2,1,0:T(8,128)} %refs_2_.1), channel_id=1, source_target_pairs={{0,9},{1,8},{2,11},{3,10},{4,13},{5,12},{6,15},{7,14},{8,1},{9,0},... | collective-permute-start | bytes 98312 | tf_op jit(solution)/shard_map/ppermute | solution.py:276
  3.5 2.8 %collective-permute-start.3 = (f32[4,16,128]{2,1,0:T(8,128)}, f32[4,16,128]{2,1,0:T(8,128)S(1)}, u32[]{:S(2)}, u32[]{:S(2)}) collective-permute-start(f32[4,16,128]{2,1,0:T(8,128)} %refs_2_.1), channel_id=1, source_target_pairs={{0,7},{1,6},{2,5},{3,4},{4,3},{5,2},{6,1},{7,0},{8,15},{9,14},{10,... | collective-permute-start | bytes 98312 | tf_op jit(solution)/shard_map/ppermute | solution.py:276
  6.3 0.8 %keep.1 = f32[4,16,128]{2,1,0:T(8,128)S(1)} custom-call(f32[4,16,128]{2,1,0:T(8,128)} %refs_2_.1), custom_call_target="tpu_custom_call" | custom-call | flops 10485760 | bytes 2097152 | tf_op jit(solution)/shard_map/keep/pallas_call | solution.py:280
  7.1 0.0 collective-permute-done.refs_0_
  7.1 0.2 %collective-permute-start.2 = (f32[2,4,16,128]{3,2,1,0:T(8,128)S(1)}, f32[2,4,16,128]{3,2,1,0:T(8,128)S(1)}, u32[]{:S(2)}, u32[]{:S(2)}) collective-permute-start(f32[2,4,16,128]{3,2,1,0:T(8,128)S(1)} %pad_maximum_fusion), channel_id=1, source_target_pairs={{0,5},{1,4},{2,7},{3,6},{4,1},{5,0},{6,3},{7,2},{8,13},{9,12},{10,... | collective-permute-start | bytes 196616 | tf_op jit(solution)/shard_map/ppermute | solution.py:276
  7.3 1.5 %collective-permute-start.1 = (f32[2,4,16,128]{3,2,1,0:T(8,128)S(1)}, f32[2,4,16,128]{3,2,1,0:T(8,128)S(1)}, u32[]{:S(2)}, u32[]{:S(2)}) collective-permute-start(f32[2,4,16,128]{3,2,1,0:T(8,128)S(1)} %pad_maximum_fusion), channel_id=1, source_target_pairs={{0,3},{1,2},{2,1},{3,0},{4,7},{5,6},{6,5},{7,4},{8,11},{9,10},{10,... | collective-permute-start | bytes 196616 | tf_op jit(solution)/shard_map/ppermute | solution.py:276
  8.8 1.0 %collective-permute-start.4 = (f32[4,16,128]{2,1,0:T(8,128)S(1)}, f32[4,16,128]{2,1,0:T(8,128)S(1)}, u32[]{:S(2)}, u32[]{:S(2)}) collective-permute-start(f32[4,16,128]{2,1,0:T(8,128)S(1)} %collective-permute-done.refs_0_), channel_id=1, source_target_pairs={{0,7},{1,6},{2,5},{3,4},{4,3},{5,2},{6,1},{7,0},{8,15},{9,14},{10,... | collective-permute-start | bytes 98312 | tf_op jit(solution)/shard_map/ppermute | solution.py:276
  9.8 0.0 collective-permute-done.3.refs_1_
  9.8 1.6 %prep.1 = (f32[4,16,128]{2,1,0:T(8,128)S(1)}, f32[1,128]{1,0:T(1,128)S(1)}, bf16[2,128,640]{2,1,0:T(8,128)(2,1)S(1)}, bf16[2,128,128]{2,1,0:T(8,128)(2,1)S(1)}, ...) custom-call(f32[4,16,128]{2,1,0:T(8,128)S(1)} %collective-permute-do, ...), custom_call_target="tpu_custom_call" | custom-call | flops 10485760 | bytes 2097152 | tf_op jit(solution)/shard_map/prep/pallas_call | solution.py:280
  11.4 0.0 collective-permute-done.1
  11.4 0.1 collective-permute-done.2
  11.6 1.5 %collective-permute-done.4 = f32[4,16,128]{2,1,0:T(8,128)S(1)} collective-permute-done((f32[4,16,128]{2,1,0:T(8,128)S(1)}, f32[4,16,128]{2,1,0:T(8,128)S(1)}, u32[]{:S(2)}, u32[]{:S(2)}) %collective-permute-start.4) | collective-permute-done | bytes 32800 | tf_op jit(solution)/shard_map/ppermute | solution.py:276
  13.1 0.4 %collective-permute-start.5 = (f32[8,4,16,128]{3,2,1,0:T(8,128)S(1)}, f32[8,4,16,128]{3,2,1,0:T(8,128)S(1)}, u32[]{:S(2)}, u32[]{:S(2)}) collective-permute-start(f32[8,4,16,128]{3,2,1,0:T(8,128)S(1)} %bitcast_dynamic-update-slice_fusion.mine), channel_id=1, source_target_pairs={{0,1},{1,0},{2,3},{3,2},{4,5},{5,4},{6,7},{7,6},{8,9},{9,8},{10,11... | collective-permute-start | bytes 786440 | tf_op jit(solution)/shard_map/ppermute | solution.py:348
  13.4 0.5 %mine.1 = (f32[2,512,128]{2,1,0:T(8,128)S(1)}, f32[2,512,128]{2,1,0:T(8,128)S(1)}, f32[2,32,16,128]{3,2,1,0:T(8,128)S(1)}, f32[2,512,128]{2,1,0:T(8,128)S(1)}) custom-call(f32[8,4,16,128]{3,2,1,0:T(8,128)S(1)} %bitcast_dynamic-update-slice_fusion.mine, ...), custom_call_target="tpu_custom_call", output_to_operand_aliasing={{0}: (5, {}), {1}: (6, {}), {2}: (7, {}), {3}: (8, {})} | custom-call | flops 83886080 | bytes 2097152 | tf_op jit(solution)/shard_map/mine/pallas_call | solution.py:280
  14.0 0.7 %collective-permute-done.5.other = f32[8,4,16,128]{3,2,1,0:T(8,128)S(1)} collective-permute-done((f32[8,4,16,128]{3,2,1,0:T(8,128)S(1)}, f32[8,4,16,128]{3,2,1,0:T(8,128)S(1)}, u32[]{:S(2)}, u32[]{:S(2)}) %collective-permute-start.5) | collective-permute-done | bytes 262176 | tf_op jit(solution)/shard_map/ppermute | solution.py:348
  14.7 3.6 %crop.1 = (f32[4,16,128]{2,1,0:T(8,128)}, f32[2,512,128]{2,1,0:T(8,128)S(1)}, f32[2,512,128]{2,1,0:T(8,128)S(1)}, f32[2,32,16,128]{3,2,1,0:T(8,128)S(1)}, f32[2,512,128]{2,1,0:T(8,128)S(1)}) custom-call(f32[8,4,16,128]{3,2,1,0:T(8,128)S(1)} %collective-permute-done.5.other, ...), custom_call_target="tpu_custom_call", output_to_operand_aliasing={{1}: (6, {}), {2}: (7, {}), {3}: (8, {}), {4}: (9, {})} | custom-call | flops 335544320 | bytes 2097152 | tf_op jit(solution)/shard_map/crop/pallas_call | solution.py:280
  (7 shorter events, 0.0 us)
Async XLA Ops:
  0.0 7.1 %collective-permute-start = (f32[4,16,128]{2,1,0:T(8,128)}, f32[4,16,128]{2,1,0:T(8,128)S(1)}, u32[]{:S(2)}, u32[]{:S(2)}) collective-permute-start(f32[4,16,128]{2,1,0:T(8,128)} %refs_2_.1), channel_id=1, source_target_pairs={{0,9},{1,8},{2,11},{3,10},{4,13},{5,12},{6,15},{7,14},{8,1},{9,0},... | collective-permute-start | bytes 98312 | tf_op jit(solution)/shard_map/ppermute | solution.py:276
  3.5 6.4 %collective-permute-start.3 = (f32[4,16,128]{2,1,0:T(8,128)}, f32[4,16,128]{2,1,0:T(8,128)S(1)}, u32[]{:S(2)}, u32[]{:S(2)}) collective-permute-start(f32[4,16,128]{2,1,0:T(8,128)} %refs_2_.1), channel_id=1, source_target_pairs={{0,7},{1,6},{2,5},{3,4},{4,3},{5,2},{6,1},{7,0},{8,15},{9,14},{10,... | collective-permute-start | bytes 98312 | tf_op jit(solution)/shard_map/ppermute | solution.py:276
  7.1 4.4 %collective-permute-start.2 = (f32[2,4,16,128]{3,2,1,0:T(8,128)S(1)}, f32[2,4,16,128]{3,2,1,0:T(8,128)S(1)}, u32[]{:S(2)}, u32[]{:S(2)}) collective-permute-start(f32[2,4,16,128]{3,2,1,0:T(8,128)S(1)} %pad_maximum_fusion), channel_id=1, source_target_pairs={{0,5},{1,4},{2,7},{3,6},{4,1},{5,0},{6,3},{7,2},{8,13},{9,12},{10,... | collective-permute-start | bytes 196616 | tf_op jit(solution)/shard_map/ppermute | solution.py:276
  7.3 4.1 %collective-permute-start.1 = (f32[2,4,16,128]{3,2,1,0:T(8,128)S(1)}, f32[2,4,16,128]{3,2,1,0:T(8,128)S(1)}, u32[]{:S(2)}, u32[]{:S(2)}) collective-permute-start(f32[2,4,16,128]{3,2,1,0:T(8,128)S(1)} %pad_maximum_fusion), channel_id=1, source_target_pairs={{0,3},{1,2},{2,1},{3,0},{4,7},{5,6},{6,5},{7,4},{8,11},{9,10},{10,... | collective-permute-start | bytes 196616 | tf_op jit(solution)/shard_map/ppermute | solution.py:276
  8.8 4.2 %collective-permute-start.4 = (f32[4,16,128]{2,1,0:T(8,128)S(1)}, f32[4,16,128]{2,1,0:T(8,128)S(1)}, u32[]{:S(2)}, u32[]{:S(2)}) collective-permute-start(f32[4,16,128]{2,1,0:T(8,128)S(1)} %collective-permute-done.refs_0_), channel_id=1, source_target_pairs={{0,7},{1,6},{2,5},{3,4},{4,3},{5,2},{6,1},{7,0},{8,15},{9,14},{10,... | collective-permute-start | bytes 98312 | tf_op jit(solution)/shard_map/ppermute | solution.py:276
  13.1 1.6 %collective-permute-start.5 = (f32[8,4,16,128]{3,2,1,0:T(8,128)S(1)}, f32[8,4,16,128]{3,2,1,0:T(8,128)S(1)}, u32[]{:S(2)}, u32[]{:S(2)}) collective-permute-start(f32[8,4,16,128]{3,2,1,0:T(8,128)S(1)} %bitcast_dynamic-update-slice_fusion.mine), channel_id=1, source_target_pairs={{0,1},{1,0},{2,3},{3,2},{4,5},{5,4},{6,7},{7,6},{8,9},{9,8},{10,11... | collective-permute-start | bytes 786440 | tf_op jit(solution)/shard_map/ppermute | solution.py:348

commit v18 on v12

--- a/solution.py
+++ b/solution.py
@@ -194,23 +194,50 @@
     count = len(groups)
     block = 8
 
+    real = jnp.sum(mask[...][:, :1]).astype(jnp.int32)
+    lower = jnp.where(col == 0, 0, 1)
+
+    def add_terms(acc, half, l, slots):
+        cells = [right[half, pl.ds(pl.multiple_of(l * tokens + g, 8), 8), :] for g in groups]
+        sums = []
+        for k in range(block):
+            row = left[half, slots[k // rows] * rows + k % rows, pl.ds(l, 1), :]
+            for n in range(count):
+                term = row * cells[n]
+                sums.append(term if acc is None else acc[k * count + n] + term)
+        return tuple(sums)
+
+    def slots_of(step):
+        ids = [(step * (block // rows) + n) ^ me for n in range(block // rows)]
+        return [2 * lax.rem(each, ranks // 2) + each // (ranks // 2) for each in ids]
+
+    def store(slots, values):
+        for k in range(block):
+            at = slots[k // rows] * rows + k % rows
+            for n in range(count):
+                tris[pl.ds(pl.multiple_of((n * tokens + at) * 8, 8), 8), :] = values[k * count + n]
+
     def tri_block(step, carry):
-        k0 = step * block
-        acc = [[None] * count for _ in range(block)]
-        for half in range(2):
-            for l in range(cols):
-                cells = [right[half, pl.ds(pl.multiple_of(l * tokens + g, 8), 8), :] for g in groups]
-                for k in range(block):
-                    row = left[half, k0 + k, pl.ds(l, 1), :]
-                    for n in range(count):
-                        term = row * cells[n]
-                        acc[k][n] = term if half + l == 0 else acc[k][n] + term
-        for n in range(count):
-            for k in range(block):
-                tris[pl.ds(pl.multiple_of((n * tokens + k0 + k) * 8, 8), 8), :] = acc[k][n]
+        slots = slots_of(step)
+        acc = None
+        for l in range(cols):
+            acc = add_terms(acc, lower, l, slots)
+
+        def upper(chunk, acc):
+            for n in range(4):
+                acc = add_terms(acc, 1 - lower, chunk * 4 + n, slots)
+            return acc
+
+        store(slots, lax.fori_loop(0, (real - cols + 3) // 4, upper, acc))
         return carry
 
-    lax.fori_loop(0, tokens // block, tri_block, 0)
+    def zero_block(step, carry):
+        store(slots_of(step), [jnp.zeros((8, hidden), jnp.float32)] * (block * count))
+        return carry
+
+    filled = (real + block - 1) // block
+    lax.fori_loop(0, filled, tri_block, 0)
+    lax.fori_loop(filled, tokens // block, zero_block, 0)
 
     low_half = jnp.where(low // cols == col, 0, 1)
     low_off = lax.rem(low, cols)

time: 18.2 us -> 17.9 us (0.984)
  Pallas kernels: 5.66 us -> 5.29 us
    pallas_call x3, Pallas kernels: 5.66 us -> 5.29 us  [call(): pl.pallas_call(body, out_shape=outputs, in_specs=[pl.BlockSpec(memory_spa...]
  transfers between devices with their start and end apart: 5 -> 5, of which waited for: 3 -> 3; matrix products, arithmetic and copies ran while one was open for 0% -> 0% of each run, Pallas kernels for 11% -> 12%
where the time goes in v18:
time: 17.9 us; the launch traced here: 17.7 us
  starting transfers between devices  6.99 us (39%)
  waiting for transfers between devices  5.37 us (30%)
  Pallas kernels  5.29 us (30%)
    ppermute x4, starting transfers between devices, exchange(): return lax.ppermute(block, ('row', 'col'), hops)  6.81 us
    pallas_call x3, Pallas kernels, call(): pl.pallas_call(body, out_shape=outputs, in_specs=[pl.BlockSpec(memory_spa...  5.29 us
    ppermute x4, waiting for transfers between devices, exchange(): return lax.ppermute(block, ('row', 'col'), hops)  4.56 us
    ppermute x1, waiting for transfers between devices, whole_crop_plan(): other = lax.ppermute(mine, 'col', [(0, 1), (1, 0)])  0.81 us
  transfers between devices with their start and end apart: 5, of which 3 were waited for; matrix products, arithmetic and copies ran while one was open for 0% of the time, Pallas kernels for 12%

profile of v18, /device:TPU:0, one launch (start us, length us, event | category | flops | bytes accessed | tf_op | source)
XLA Modules:
  0.0 17.7 jit_solution(6117493890865150190)
XLA Ops:
  0.0 3.5 %collective-permute-start = (f32[4,16,128]{2,1,0:T(8,128)}, f32[4,16,128]{2,1,0:T(8,128)S(1)}, u32[]{:S(2)}, u32[]{:S(2)}) collective-permute-start(f32[4,16,128]{2,1,0:T(8,128)} %refs_0_.1), channel_id=1, source_target_pairs={{0,9},{1,8},{2,11},{3,10},{4,13},{5,12},{6,15},{7,14},{8,1},{9,0},... | collective-permute-start | bytes 98312 | tf_op jit(solution)/shard_map/ppermute | solution.py:294
  3.5 1.5 %own.1 = (f32[4,16,128]{2,1,0:T(8,128)S(1)}, f32[1,128]{1,0:T(1,128)S(1)}, bf16[2,128,640]{2,1,0:T(8,128)(2,1)S(1)}, bf16[2,128,128]{2,1,0:T(8,128)(2,1)S(1)}, f...) custom-call(f32[4,16,128]{2,1,0:T(8,128)} %refs_0_.1, ...), custom_call_target="tpu_custom_call" | custom-call | flops 10485760 | bytes 2097152 | tf_op jit(solution)/shard_map/own/pallas_call | solution.py:298
  5.0 0.6 %collective-permute-done = f32[4,16,128]{2,1,0:T(8,128)S(1)} collective-permute-done((f32[4,16,128]{2,1,0:T(8,128)}, f32[4,16,128]{2,1,0:T(8,128)S(1)}, u32[]{:S(2)}, u32[]{:S(2)}) %collective-permute-start) | collective-permute-done | bytes 32800 | tf_op jit(solution)/shard_map/ppermute | solution.py:294
  5.6 2.7 %collective-permute-start.3 = (f32[2,4,16,128]{3,2,1,0:T(8,128)S(1)}, f32[2,4,16,128]{3,2,1,0:T(8,128)S(1)}, u32[]{:S(2)}, u32[]{:S(2)}) collective-permute-start(f32[2,4,16,128]{3,2,1,0:T(8,128)S(1)} %pad_maximum_fusion), channel_id=1, source_target_pairs={{0,7},{1,6},{2,5},{3,4},{4,3},{5,2},{6,1},{7,0},{8,15},{9,14},{10,... | collective-permute-start | bytes 196616 | tf_op jit(solution)/shard_map/ppermute | solution.py:294
  8.3 0.5 %collective-permute-start.2 = (f32[2,4,16,128]{3,2,1,0:T(8,128)S(1)}, f32[2,4,16,128]{3,2,1,0:T(8,128)S(1)}, u32[]{:S(2)}, u32[]{:S(2)}) collective-permute-start(f32[2,4,16,128]{3,2,1,0:T(8,128)S(1)} %pad_maximum_fusion), channel_id=1, source_target_pairs={{0,5},{1,4},{2,7},{3,6},{4,1},{5,0},{6,3},{7,2},{8,13},{9,12},{10,... | collective-permute-start | bytes 196616 | tf_op jit(solution)/shard_map/ppermute | solution.py:294
  8.7 0.2 collective-permute-start.1
  8.9 4.0 %collective-permute-done.1 = f32[2,4,16,128]{3,2,1,0:T(8,128)S(1)} collective-permute-done((f32[2,4,16,128]{3,2,1,0:T(8,128)S(1)}, f32[2,4,16,128]{3,2,1,0:T(8,128)S(1)}, u32[]{:S(2)}, u32[]{:S(2)}) %collective-permute-start.1) | collective-permute-done | bytes 65568 | tf_op jit(solution)/shard_map/ppermute | solution.py:294
  12.9 0.0 collective-permute-done.2
  12.9 0.0 collective-permute-done.3
  12.9 0.2 %collective-permute-start.4 = (f32[8,4,16,128]{3,2,1,0:T(8,128)S(1)}, f32[8,4,16,128]{3,2,1,0:T(8,128)S(1)}, u32[]{:S(2)}, u32[]{:S(2)}) collective-permute-start(f32[8,4,16,128]{3,2,1,0:T(8,128)S(1)} %constant_dynamic-update-slice_fusion.mine), channel_id=1, source_target_pairs={{0,1},{1,0},{2,3},{3,2},{4,5},{5,4},{6,7},{7,6},{8,9},{9,8},{10,11... | collective-permute-start | bytes 786440 | tf_op jit(solution)/shard_map/ppermute | solution.py:347
  13.1 0.6 %mine.1 = (f32[2,512,128]{2,1,0:T(8,128)S(1)}, f32[2,512,128]{2,1,0:T(8,128)S(1)}, f32[2,32,16,128]{3,2,1,0:T(8,128)S(1)}, f32[2,512,128]{2,1,0:T(8,128)S(1)}) custom-call(f32[8,4,16,128]{3,2,1,0:T(8,128)S(1)} %constant_dynamic-update-slice_fusion.mine, ...), custom_call_target="tpu_custom_call", output_to_operand_aliasing={{0}: (5, {}), {1}: (6, {}), {2}: (7, {}), {3}: (8, {})} | custom-call | flops 83886080 | bytes 2097152 | tf_op jit(solution)/shard_map/mine/pallas_call | solution.py:298
  13.7 0.8 %collective-permute-done.4.other = f32[8,4,16,128]{3,2,1,0:T(8,128)S(1)} collective-permute-done((f32[8,4,16,128]{3,2,1,0:T(8,128)S(1)}, f32[8,4,16,128]{3,2,1,0:T(8,128)S(1)}, u32[]{:S(2)}, u32[]{:S(2)}) %collective-permute-start.4) | collective-permute-done | bytes 262176 | tf_op jit(solution)/shard_map/ppermute | solution.py:347
  14.5 3.2 %crop.1 = (f32[4,16,128]{2,1,0:T(8,128)}, f32[2,512,128]{2,1,0:T(8,128)S(1)}, f32[2,512,128]{2,1,0:T(8,128)S(1)}, f32[2,32,16,128]{3,2,1,0:T(8,128)S(1)}, f32[2,512,128]{2,1,0:T(8,128)S(1)}) custom-call(f32[8,4,16,128]{3,2,1,0:T(8,128)S(1)} %collective-permute-done.4.other, ...), custom_call_target="tpu_custom_call", output_to_operand_aliasing={{1}: (6, {}), {2}: (7, {}), {3}: (8, {}), {4}: (9, {})} | custom-call | flops 335544320 | bytes 2097152 | tf_op jit(solution)/shard_map/crop/pallas_call | solution.py:298
  (6 shorter events, 0.0 us)
Async XLA Ops:
  0.0 5.6 %collective-permute-start = (f32[4,16,128]{2,1,0:T(8,128)}, f32[4,16,128]{2,1,0:T(8,128)S(1)}, u32[]{:S(2)}, u32[]{:S(2)}) collective-permute-start(f32[4,16,128]{2,1,0:T(8,128)} %refs_0_.1), channel_id=1, source_target_pairs={{0,9},{1,8},{2,11},{3,10},{4,13},{5,12},{6,15},{7,14},{8,1},{9,0},... | collective-permute-start | bytes 98312 | tf_op jit(solution)/shard_map/ppermute | solution.py:294
  5.6 7.3 %collective-permute-start.3 = (f32[2,4,16,128]{3,2,1,0:T(8,128)S(1)}, f32[2,4,16,128]{3,2,1,0:T(8,128)S(1)}, u32[]{:S(2)}, u32[]{:S(2)}) collective-permute-start(f32[2,4,16,128]{3,2,1,0:T(8,128)S(1)} %pad_maximum_fusion), channel_id=1, source_target_pairs={{0,7},{1,6},{2,5},{3,4},{4,3},{5,2},{6,1},{7,0},{8,15},{9,14},{10,... | collective-permute-start | bytes 196616 | tf_op jit(solution)/shard_map/ppermute | solution.py:294
  8.3 4.6 %collective-permute-start.2 = (f32[2,4,16,128]{3,2,1,0:T(8,128)S(1)}, f32[2,4,16,128]{3,2,1,0:T(8,128)S(1)}, u32[]{:S(2)}, u32[]{:S(2)}) collective-permute-start(f32[2,4,16,128]{3,2,1,0:T(8,128)S(1)} %pad_maximum_fusion), channel_id=1, source_target_pairs={{0,5},{1,4},{2,7},{3,6},{4,1},{5,0},{6,3},{7,2},{8,13},{9,12},{10,... | collective-permute-start | bytes 196616 | tf_op jit(solution)/shard_map/ppermute | solution.py:294
  8.7 4.1 %collective-permute-start.1 = (f32[2,4,16,128]{3,2,1,0:T(8,128)S(1)}, f32[2,4,16,128]{3,2,1,0:T(8,128)S(1)}, u32[]{:S(2)}, u32[]{:S(2)}) collective-permute-start(f32[2,4,16,128]{3,2,1,0:T(8,128)S(1)} %pad_maximum_fusion), channel_id=1, source_target_pairs={{0,3},{1,2},{2,1},{3,0},{4,7},{5,6},{6,5},{7,4},{8,11},{9,10},{10,... | collective-permute-start | bytes 196616 | tf_op jit(solution)/shard_map/ppermute | solution.py:294
  12.9 1.6 %collective-permute-start.4 = (f32[8,4,16,128]{3,2,1,0:T(8,128)S(1)}, f32[8,4,16,128]{3,2,1,0:T(8,128)S(1)}, u32[]{:S(2)}, u32[]{:S(2)}) collective-permute-start(f32[8,4,16,128]{3,2,1,0:T(8,128)S(1)} %constant_dynamic-update-slice_fusion.mine), channel_id=1, source_target_pairs={{0,1},{1,0},{2,3},{3,2},{4,5},{5,4},{6,7},{7,6},{8,9},{9,8},{10,11... | collective-permute-start | bytes 786440 | tf_op jit(solution)/shard_map/ppermute | solution.py:347
